TPU v7x, 128 devices: a whole 4x4x4 slice. The times are simulated.
128 devices in a mesh: lat: 8 (over x, z_hi), lon: 16 (over y, z_lo, core).
Axes of the slice: x: 4, y: 4, z: 4 (z_hi: 2, z_lo: 2; z = z_hi * 2 + z_lo), core: 2. Of those that a mesh axis runs over, the one named last changes fastest.
Arguments:
- tokens: bfloat16 [32, 4, 352, 512], P('lat', None, 'lon'), may hold values from -6 to 6
- cotangent: bfloat16 [32, 4, 352, 512], P('lat', None, 'lon'), may hold values from -6 to 6
- inproj_lon: bfloat16 [512, 1536], replicated, may hold values from -3 to 3
- outproj_lon: bfloat16 [512, 512], replicated, may hold values from -0.25 to 0.25
- inproj_lat: bfloat16 [512, 1536], replicated, may hold values from -3 to 3
- outproj_lat: bfloat16 [512, 512], replicated, may hold values from -0.25 to 0.25
- mlp_in: bfloat16 [512, 2048], replicated, may hold values from -0.25 to 0.25
- mlp_out: bfloat16 [2048, 512], replicated, may hold values from -0.125 to 0.125
Outputs:
- output: float32 [32, 4, 352, 512], P('lat', None, 'lon')
- grad_tokens: float32 [32, 4, 352, 512], P('lat', None, 'lon')
- grad_inproj_lon: float32 [512, 1536], P(None, ('lat', 'lon'))
- grad_outproj_lon: float32 [512, 512], P(None, ('lat', 'lon'))
- grad_inproj_lat: float32 [512, 1536], P(None, ('lat', 'lon'))
- grad_outproj_lat: float32 [512, 512], P(None, ('lat', 'lon'))
- grad_mlp_in: float32 [512, 2048], P(None, ('lat', 'lon'))
- grad_mlp_out: float32 [2048, 512], P(None, ('lat', 'lon'))
All inputs are finite; a program needn't handle non-finite values.
Results may differ from a plain program's by a relative error of at most 0.035.
Values may be sent and summed in bfloat16 or wider, within the bound.
No kernel may reach another device: no remote copies, remote signals or barrier semaphores. Data moves between devices by JAX's collectives and lax.ppermute only.
A program may use at most 128 MiB of HBM per device.

v0:
```python
import jax
import jax.numpy as jnp
from jax import lax
from jax.experimental import pallas as pl
from jax.experimental.pallas import tpu as pltpu
from jax.sharding import Mesh, PartitionSpec as P

HEADS = 8
WIDTH = 512
FF = 2048
HEAD = WIDTH // HEADS
SCALE = HEAD**-0.5
EPSILON = 1e-05
ROWS = 352
LATS = 32
NEAR = 22
PART = 11
LON = ("y", "l", "c")
TURN = ("y", "x", "h")
CHIPS = ("x", "h", "y", "l")
WHOLE = ((0, ROWS),)
BLOCKS = ((0, 128), (128, 128), (256, 96))
f32 = jnp.float32
bf16 = jnp.bfloat16


def normalize(values):
    center = values - jnp.mean(values, axis=-1, keepdims=True)
    inverse = lax.rsqrt(jnp.mean(center * center, axis=-1, keepdims=True) + EPSILON)
    return center * inverse, inverse


def norm_back(scaled, inverse, upstream):
    return inverse * (
        upstream
        - jnp.mean(upstream, axis=-1, keepdims=True)
        - scaled * jnp.mean(upstream * scaled, axis=-1, keepdims=True)
    )


def dot(left, right, left_dim=1, right_dim=0):
    dims = (((left_dim,), (right_dim,)), ((), ()))
    return lax.dot_general(left, right, dims, preferred_element_type=f32)


def same_column(rows):
    shape = (rows, rows)
    keys = lax.broadcasted_iota(jnp.int32, shape, 0) // LATS
    return keys == lax.broadcasted_iota(jnp.int32, shape, 1) // LATS


def probabilities(keys, queries, masked):
    scores = dot(keys, queries, 1, 1)
    if masked:
        scores = jnp.where(same_column(scores.shape[0]), scores, -1e30)
    powers = jnp.exp(scores - jnp.max(scores, axis=0, keepdims=True))
    return powers * (1.0 / jnp.sum(powers, axis=0, keepdims=True))


def half_of(values, half):
    lanes = lax.broadcasted_iota(jnp.int32, values.shape, 1) // HEAD
    return jnp.where(lanes == half, values, jnp.zeros_like(values))


def pair_columns(part, pair):
    return pl.ds(pl.multiple_of(part * WIDTH + pair * 2 * HEAD, 2 * HEAD), 2 * HEAD)


def attend(packed, turned, blocks):
    masked = len(blocks) > 1

    def one_pair(pair, _):
        for first, count in blocks:
            rows = pl.ds(first, count)
            queries, keys, values = (packed[rows, pair_columns(p, pair)] for p in range(3))
            for half in range(2):
                probs = probabilities(half_of(keys * SCALE, half), queries, masked).astype(bf16)
                mixed = dot(values, probs, 0, 0)
                place = pl.ds(pl.multiple_of(pair * 2 * HEAD + half * HEAD, HEAD), HEAD)
                turned[place, rows] = mixed[half * HEAD : (half + 1) * HEAD]
        return 0

    lax.fori_loop(0, HEADS // 2, one_pair, 0)


def attend_back(packed, upstream, grads, blocks):
    masked = len(blocks) > 1

    def one_pair(pair, _):
        for first, count in blocks:
            rows = pl.ds(first, count)
            queries, keys, values = (packed[rows, pair_columns(p, pair)] for p in range(3))
            grad_mix = upstream[rows, pair_columns(0, pair)]
            found = []
            for half in range(2):
                probs = probabilities(half_of(keys * SCALE, half), queries, masked)
                grad_probs = dot(half_of(values, half), grad_mix, 1, 1)
                inner = jnp.sum(grad_probs * probs, axis=0, keepdims=True)
                grad_scores = (probs * (grad_probs - inner) * SCALE).astype(bf16)
                found.append(
                    (
                        dot(grad_scores, keys, 0, 0),
                        dot(grad_scores, queries),
                        dot(probs.astype(bf16), grad_mix),
                    )
                )
            for part in range(3):
                joined = half_of(found[0][part], 0) + half_of(found[1][part], 1)
                grads[rows, pair_columns(part, pair)] = joined.astype(bf16)
        return 0

    lax.fori_loop(0, HEADS // 2, one_pair, 0)


def project(normed, inproj, packed):
    for part in range(3):
        columns = pl.ds(part * WIDTH, WIDTH)
        packed[:, columns] = dot(normed, inproj[:, columns]).astype(bf16)


def row_forward(pack, inproj, outproj, out, tokens, normed, packed, mixed, hidden, cotangent, turned):
    for block in range(16):
        piece = pack[block].astype(f32)
        rows = pl.ds(block * NEAR, NEAR)
        hidden[rows, :] = piece[:NEAR]
        cotangent[rows, :] = piece[NEAR:]
    values = hidden[...]
    tokens[...] = values.astype(bf16)
    normed[...] = normalize(values)[0].astype(bf16)
    project(normed[...], inproj, packed)
    attend(packed, turned, WHOLE)
    mixed[...] = turned[...].T.astype(bf16)
    hidden[...] += dot(mixed[...], outproj[...])
    for block in range(LATS):
        rows = pl.ds(block * PART, PART)
        out[block] = jnp.concatenate([hidden[rows, :], cotangent[rows, :]], axis=0).astype(bf16)


def row_backward(pack, tokens, packed, inproj, outproj, out, grads, low, hidden, output, upstream):
    for block in range(LATS):
        piece = pack[block].astype(f32)
        rows = pl.ds(block * PART, PART)
        hidden[rows, :] = piece[:PART]
        output[rows, :] = piece[PART:]
    low[...] = hidden[...].astype(bf16)
    upstream[...] = dot(low[...], outproj[...], 1, 1).astype(bf16)
    attend_back(packed, upstream, grads, WHOLE)
    grad_normed = dot(grads[...], inproj[...], 1, 1)
    hidden[...] += norm_back(*normalize(tokens[...].astype(f32)), grad_normed)
    for block in range(16):
        rows = pl.ds(block * NEAR, NEAR)
        out[block] = jnp.concatenate([hidden[rows, :], output[rows, :]], axis=0).astype(bf16)


def to_columns(pack, first, second):
    for lat in range(LATS):
        piece = pack[lat].astype(f32)
        for tile in range(4):
            lanes = slice(tile * 128, (tile + 1) * 128)
            first[tile, pl.ds(lat, PART, stride=LATS), :] = piece[:PART, lanes]
            second[tile, pl.ds(lat, PART, stride=LATS), :] = piece[PART:, lanes]


def joined(tiles):
    return jnp.concatenate([tiles[tile] for tile in range(4)], axis=1)


def put_tiles(tiles, values):
    for tile in range(4):
        tiles[tile] = values[:, tile * 128 : (tile + 1) * 128]


def from_columns(out, first, second):
    for lat in range(LATS):
        rows = pl.ds(lat, PART, stride=LATS)
        parts = [
            jnp.concatenate([tiles[tile, rows, :] for tile in range(4)], axis=1)
            for tiles in (first, second)
        ]
        out[lat] = jnp.concatenate(parts, axis=0).astype(bf16)


def column_both(
    pack, inproj, outproj, mlp_in, mlp_out,
    out, normed, mixed, grads, low, normed_mlp, activated, grad_inner, cotangent,
    first, second, turned, packed, hidden_one, hidden_two, grad_normed, output, grad_mix,
):
    to_columns(pack, first, second)
    hidden_one[...] = joined(first)
    cotangent[...] = joined(second).astype(bf16)
    normed[...] = normalize(hidden_one[...])[0].astype(bf16)
    project(normed[...], inproj, packed)
    attend(packed, turned, BLOCKS)
    mixed[...] = turned[...].T.astype(bf16)
    hidden_two[...] = hidden_one[...] + dot(mixed[...], outproj[...])
    normed_mlp[...] = normalize(hidden_two[...])[0].astype(bf16)
    output[...] = hidden_two[...]
    grad_normed[...] = jnp.zeros_like(grad_normed)

    def one_chunk(chunk, _):
        columns = pl.ds(pl.multiple_of(chunk * 256, 256), 256)
        inner = dot(normed_mlp[...], mlp_in[:, columns])
        spread = 0.5 * (1.0 + lax.erf(inner * 2.0**-0.5))
        slope = spread + inner * (0.5 / jnp.pi) ** 0.5 * jnp.exp(-0.5 * inner * inner)
        active = (inner * spread).astype(bf16)
        activated[:, columns] = active
        output[...] += dot(active, mlp_out[columns, :])
        grad = (dot(cotangent[...], mlp_out[columns, :], 1, 1) * slope).astype(bf16)
        grad_inner[:, columns] = grad
        grad_normed[...] += dot(grad, mlp_in[:, columns], 1, 1)
        return 0

    lax.fori_loop(0, FF // 256, one_chunk, 0)
    put_tiles(second, output[...])
    grad_two = cotangent[...].astype(f32) + norm_back(*normalize(hidden_two[...]), grad_normed[...])
    hidden_two[...] = grad_two
    low[...] = grad_two.astype(bf16)
    grad_mix[...] = dot(low[...], outproj[...], 1, 1).astype(bf16)
    attend_back(packed, grad_mix, grads, BLOCKS)
    back = norm_back(*normalize(hidden_one[...]), dot(grads[...], inproj[...], 1, 1))
    put_tiles(first, hidden_two[...] + back)
    from_columns(out, first, second)


def part_cores(core, terms, mine, other, block, row):
    pairs = terms.reshape(16, 2, 16, WIDTH)
    blocks, rows = pl.ds(block * 16, 16), pl.ds(row, 16)
    mine[blocks, rows, :] = jnp.where(core == 0, pairs[:, 0], pairs[:, 1]).astype(bf16)
    other[blocks, rows, :] = jnp.where(core == 0, pairs[:, 1], pairs[:, 0]).astype(bf16)


def attention_terms(core, grads, normed, low, mixed, mine, other, row):
    for block in range(4):
        wide = dot(grads[:, block * 384 : (block + 1) * 384], normed[...], 0, 0)
        slim = dot(low[:, block * 128 : (block + 1) * 128], mixed[...], 0, 0)
        terms = [wide.reshape(32, 12, WIDTH), slim.reshape(32, 4, WIDTH)]
        part_cores(core, jnp.concatenate(terms, axis=1), mine, other, block, row)


def row_terms(core, grads, normed, low, mixed, mine, other):
    attention_terms(core[0], grads, normed, low, mixed, mine, other, 0)


def column_terms(
    core, grads, normed, low, mixed, normed_mlp, activated, grad_inner, cotangent, mine, other
):
    attention_terms(core[0], grads, normed, low, mixed, mine, other, 0)
    for block in range(4):
        terms = dot(grad_inner[:, block * 512 : (block + 1) * 512], normed_mlp[...], 0, 0)
        part_cores(core[0], terms.reshape(32, 16, WIDTH), mine, other, block, 16)
        terms = dot(cotangent[:, block * 128 : (block + 1) * 128], activated[...], 0, 0)
        quarters = [
            terms[:, part * WIDTH : (part + 1) * WIDTH].reshape(32, 4, WIDTH) for part in range(4)
        ]
        part_cores(core[0], jnp.concatenate(quarters, axis=1), mine, other, block, 32)


def call(kernel, outs, scratch, args, megabytes, gigaflops, scalars=0):
    return pl.pallas_call(
        kernel,
        out_shape=[jax.ShapeDtypeStruct(shape, kind) for shape, kind in outs],
        in_specs=[pl.BlockSpec(memory_space=pltpu.SMEM)] * scalars
        + [pl.BlockSpec(memory_space=pltpu.VMEM)] * (len(args) - scalars),
        out_specs=[pl.BlockSpec(memory_space=pltpu.VMEM)] * len(outs),
        scratch_shapes=[pltpu.VMEM(shape, kind) for shape, kind in scratch],
        compiler_params=pltpu.CompilerParams(vmem_limit_bytes=megabytes << 20),
        cost_estimate=pl.CostEstimate(
            flops=int(gigaflops * 1e9), bytes_accessed=4 << 20, transcendentals=1 << 20
        ),
    )(*args)


def swap(array, axes):
    return lax.all_to_all(array, axes, split_axis=0, concat_axis=0, tiled=True)


def scatter_sum(mine, other):
    other = lax.ppermute(other, "c", [(0, 1), (1, 0)])
    both = (mine.astype(f32) + other.astype(f32)).astype(bf16)
    return jnp.sum(swap(both, CHIPS).astype(f32), axis=0)


NARROW = (ROWS, WIDTH)
QKV = (ROWS, 3 * WIDTH)
WIDE = (ROWS, FF)
TILES = (4, ROWS, 128)


def per_device(tokens, cotangent, inproj_lon, outproj_lon, inproj_lat, outproj_lat, mlp_in, mlp_out):
    core = lax.axis_index("c").astype(jnp.int32).reshape(1)
    pack = jnp.concatenate([tokens, cotangent], axis=2).reshape(16, 2 * NEAR, WIDTH)
    pack, row_tokens, row_normed, row_packed, row_mixed = call(
        row_forward,
        [((LATS, 2 * PART, WIDTH), bf16), (NARROW, bf16), (NARROW, bf16), (QKV, bf16), (NARROW, bf16)],
        [(NARROW, f32), (NARROW, f32), ((WIDTH, ROWS), f32)],
        (swap(pack, LON), inproj_lon, outproj_lon),
        40,
        1.3,
    )
    pack, *saved = call(
        column_both,
        [((LATS, 2 * PART, WIDTH), bf16), (NARROW, bf16), (NARROW, bf16), (QKV, bf16), (NARROW, bf16)]
        + [(NARROW, bf16), (WIDE, bf16), (WIDE, bf16), (NARROW, bf16)],
        [(TILES, f32), (TILES, f32), ((WIDTH, ROWS), f32), (QKV, bf16)]
        + [(NARROW, f32)] * 4
        + [(NARROW, bf16)],
        (swap(pack, TURN), inproj_lat, outproj_lat, mlp_in, mlp_out),
        48,
        5.0,
    )
    normed, mixed, grads, low, normed_mlp, activated, grad_inner, column_cotangent = saved
    column_mine, column_other = call(
        column_terms,
        [((64, 48, WIDTH), bf16)] * 2,
        [],
        (core, grads, normed, low, mixed, normed_mlp, activated, grad_inner, column_cotangent),
        48,
        2.2,
        scalars=1,
    )
    pack, grads, low = call(
        row_backward,
        [((16, 2 * NEAR, WIDTH), bf16), (QKV, bf16), (NARROW, bf16)],
        [(NARROW, f32), (NARROW, f32), (NARROW, bf16)],
        (swap(pack, TURN), row_tokens, row_packed, inproj_lon, outproj_lon),
        40,
        2.0,
    )
    row_mine, row_other = call(
        row_terms,
        [((64, 16, WIDTH), bf16)] * 2,
        [],
        (core, grads, row_normed, low, row_mixed),
        40,
        0.75,
        scalars=1,
    )
    pack = swap(pack, LON).reshape(4, 4, 2 * NEAR, WIDTH).astype(f32)
    columns = scatter_sum(column_mine, column_other)
    rows = scatter_sum(row_mine, row_other)
    return (
        pack[:, :, NEAR:],
        pack[:, :, :NEAR],
        rows[0:12].T,
        rows[12:16].T,
        columns[0:12].T,
        columns[12:16].T,
        columns[16:32].T,
        columns[32:48].reshape(4, 4, WIDTH).transpose(0, 2, 1).reshape(FF, 4),
    )


def solution(mesh):
    fine = Mesh(mesh.devices.reshape(4, 2, 4, 2, 2), ("x", "h", "y", "l", "c"))
    grid = P(("x", "h"), None, ("y", "l", "c"), None)
    columns = P(None, ("x", "h", "y", "l", "c"))
    return jax.shard_map(
        per_device,
        mesh=fine,
        in_specs=(grid, grid) + (P(),) * 6,
        out_specs=(grid, grid) + (columns,) * 6,
        check_vma=False,
    )
```

profile of v0, /device:TPU:0, one launch (start us, length us, event | category | flops | bytes accessed | tf_op | source)
XLA Modules:
  0.0 212.5 jit_solution(8476848810786157366)
XLA Ops:
  0.6 0.0 copy-start
  0.6 0.0 copy-start.2
  0.7 1.7 pad_maximum_fusion
  2.4 0.2 copy.16
  2.5 19.1 %all_to_all.30.pack = bf16[16,44,512]{2,1,0:T(8,128)(2,1)S(1)} all-to-all(bf16[16,44,512]{2,1,0:T(8,128)(2,1)S(1)} %bitcast.22), channel_id=1, replica_groups=mesh['x'=4,'h'=2,'y'=4,'l'=2,'c'=2] {'y','l','c'}, dimensions={0} | all-to-all | bytes 1441792 | tf_op jit(solution)/shard_map/all_to_all | solution.py:274
  21.7 0.0 copy-done
  21.7 6.0 %shard_map.143 = (bf16[32,22,512]{2,1,0:T(8,128)(2,1)}, bf16[352,512]{1,0:T(8,128)(2,1)S(1)}, bf16[352,512]{1,0:T(8,128)(2,1)S(1)}, bf16[352,1536]{1,0:T(8,128)(2,1)S(1)}, bf16[352,512]{1,0:T(8,128)(2,1)S(1)}) custom-call(bf16[16,44,512]{2,1,0:T(8,128)(2,1)S(1)} %all_to_all.30.pack, bf16[512,1536]{1,0:T(8,128)(2,1)S(1)} %copy-done, ...), custom_call_target="tpu_custom_call" | custom-call | flops 1300000000 | bytes 4194304 | tf_op jit(solution)/shard_map/pallas_call | solution.py:259
  27.7 0.7 copy-done.3
  28.4 0.7 copy-done.5
  29.2 1.0 copy-done.7
  30.2 0.7 copy-done.11
  30.9 8.6 %all-to-all-start.1 = ((bf16[32,22,512]{2,1,0:T(8,128)(2,1)}), bf16[32,22,512]{2,1,0:T(8,128)(2,1)S(1)}, u32[]{:S(2)}, u32[]{:S(2)}) async-start(bf16[32,22,512]{2,1,0:T(8,128)(2,1)} %get-tuple-element.29), calls=%async_computation.1 | async-start | bytes 1572864 | tf_op jit(solution)/shard_map/all_to_all | solution.py:274
  39.6 16.7 %all-to-all-done.1.pack = bf16[32,22,512]{2,1,0:T(8,128)(2,1)S(1)} async-done(((bf16[32,22,512]{2,1,0:T(8,128)(2,1)}), bf16[32,22,512]{2,1,0:T(8,128)(2,1)S(1)}, u32[]{:S(2)}, u32[]{:S(2)}) %all-to-all-start.1) | async-done | bytes 720928 | tf_op jit(solution)/shard_map/all_to_all | solution.py:274
  56.3 0.0 copy-done.1
  56.3 27.1 %shard_map.144 = (bf16[32,22,512]{2,1,0:T(8,128)(2,1)S(1)}, bf16[352,512]{1,0:T(8,128)(2,1)S(1)}, bf16[352,512]{1,0:T(8,128)(2,1)S(1)}, bf16[352,1536]{1,0:T(8,1...) custom-call(bf16[32,22,512]{2,1,0:T(8,128)(2,1)S(1)} %all-to-all-don, ...), custom_call_target="tpu_custom_call" | custom-call | flops 5000000000 | bytes 4194304 | tf_op jit(solution)/shard_map/pallas_call | solution.py:259
  83.4 1.4 copy-done.9
  84.7 1.4 copy-done.10
  86.1 6.5 %shard_map.147 = (bf16[64,48,512]{2,1,0:T(8,128)(2,1)}, bf16[64,48,512]{2,1,0:T(8,128)(2,1)}) custom-call(s32[1]{0:T(128)} %bitcast.2.core, bf16[352,1536]{1,0:T(8,128)(2,1)S(1)} %get-tuple-element.40.grads, bf16[352,512]{1,0:T(8,128)(2,1)S(1)} %get-tuple-element.41.normed, bf16[352,512]{1,0:T(8,128)(2,1)S(1)} %get-tuple-element.42.low, ...), custom_call_target="tpu_custom_call" | custom-call | flops 2200000000 | bytes 4194304 | tf_op jit(solution)/shard_map/pallas_call | solution.py:259
  92.5 0.0 collective-permute-start.1
  92.5 20.6 %all_to_all.31.pack = bf16[32,22,512]{2,1,0:T(8,128)(2,1)S(1)} all-to-all(bf16[32,22,512]{2,1,0:T(8,128)(2,1)S(1)} %get-tuple-element.30), channel_id=1, replica_groups=mesh['x'=4,'h'=2,'y'=4,'l'=2,'c'=2] {'y','x','h'}, dimensions={0} | all-to-all | bytes 1441792 | tf_op jit(solution)/shard_map/all_to_all | solution.py:274
  113.2 0.0 copy-done.8
  113.2 8.6 %shard_map.145 = (bf16[16,44,512]{2,1,0:T(8,128)(2,1)}, bf16[352,1536]{1,0:T(8,128)(2,1)S(1)}, bf16[352,512]{1,0:T(8,128)(2,1)S(1)}) custom-call(bf16[32,22,512]{2,1,0:T(8,128)(2,1)S(1)} %all_to_all.31.pack, bf16[352,512]{1,0:T(8,128)(2,1)S(1)} %copy-done.12, bf16[352,1536]{1,0:T(8,128)(2,1)S(1)} %copy-done.8, bf16[512,1536]{1,0:T(8,128)(2,1)S(1)} %copy-done, ...), custom_call_target="tpu_custom_call" | custom-call | flops 2000000000 | bytes 4194304 | tf_op jit(solution)/shard_map/pallas_call | solution.py:259
  121.8 1.4 shard_map.146
  123.2 0.1 collective-permute-start
  123.3 3.6 %all-to-all-start.3 = ((bf16[16,44,512]{2,1,0:T(8,128)(2,1)}), bf16[16,44,512]{2,1,0:T(8,128)(2,1)S(1)}, u32[]{:S(2)}, u32[]{:S(2)}) async-start(bf16[16,44,512]{2,1,0:T(8,128)(2,1)} %get-tuple-element.33), calls=%async_computation.3 | async-start | bytes 1572864 | tf_op jit(solution)/shard_map/all_to_all | solution.py:274
  126.9 0.0 collective-permute-done
  126.9 2.6 %add_convert_fusion.1 = bf16[64,16,512]{2,1,0:T(8,128)(2,1)} fusion(bf16[64,16,512]{2,1,0:T(8,128)(2,1)} %collective-permute-done, bf16[64,16,512]{2,1,0:T(8,128)(2,1)S(1)} %get-tuple-element.38), kind=kLoop, calls=%fused_computation.3 | loop fusion | flops 2097152 | bytes 3145728 | tf_op jit(solution)/shard_map/convert_element_type | solution.py:279
  129.5 11.0 %all-to-all-done.3 = bf16[16,44,512]{2,1,0:T(8,128)(2,1)S(1)} async-done(((bf16[16,44,512]{2,1,0:T(8,128)(2,1)}), bf16[16,44,512]{2,1,0:T(8,128)(2,1)S(1)}, u32[]{:S(2)}, u32[]{:S(2)}) %all-to-all-start.3) | async-done | bytes 720928 | tf_op jit(solution)/shard_map/all_to_all | solution.py:274
  140.5 4.7 %all-to-all-start.4 = ((bf16[64,16,512]{2,1,0:T(8,128)(2,1)}), bf16[64,16,512]{2,1,0:T(8,128)(2,1)S(1)}, u32[]{:S(2)}, u32[]{:S(2)}) async-start(bf16[64,16,512]{2,1,0:T(8,128)(2,1)} %add_convert_fusion.1), calls=%async_computation.4 | async-start | bytes 2097152 | tf_op jit(solution)/shard_map/all_to_all | solution.py:274
  145.2 0.0 collective-permute-done.1
  145.2 5.7 %add_convert_fusion = bf16[64,48,512]{2,1,0:T(8,128)(2,1)} fusion(bf16[64,48,512]{2,1,0:T(8,128)(2,1)} %collective-permute-done.1, bf16[64,48,512]{2,1,0:T(8,128)(2,1)} %get-tuple-element.48), kind=kLoop, calls=%fused_computation.1 | loop fusion | flops 6291456 | bytes 9437184 | tf_op jit(solution)/shard_map/convert_element_type | solution.py:279
  150.9 0.0 copy-done.13
  150.9 12.9 %all-to-all-done.4 = bf16[64,16,512]{2,1,0:T(8,128)(2,1)S(1)} async-done(((bf16[64,16,512]{2,1,0:T(8,128)(2,1)}), bf16[64,16,512]{2,1,0:T(8,128)(2,1)S(1)}, u32[]{:S(2)}, u32[]{:S(2)}) %all-to-all-start.4) | async-done | bytes 1048608 | tf_op jit(solution)/shard_map/all_to_all | solution.py:274
  163.9 1.0 copy-done.14
  164.9 4.7 %all-to-all-start.5 = ((bf16[64,48,512]{2,1,0:T(8,128)(2,1)}), bf16[64,48,512]{2,1,0:T(8,128)(2,1)S(1)}, u32[]{:S(2)}, u32[]{:S(2)}) async-start(bf16[64,48,512]{2,1,0:T(8,128)(2,1)} %add_convert_fusion), calls=%async_computation.5 | async-start | bytes 6291456 | tf_op jit(solution)/shard_map/all_to_all | solution.py:274
  169.6 0.0 copy-start.15
  169.6 1.5 fusion
  171.1 1.3 copy.20
  172.4 1.3 copy.21
  173.8 0.2 convert_reduce_fusion.1
  173.9 0.6 slice_bitcast_fusion.4
  174.5 0.6 slice_bitcast_fusion.2
  175.1 34.4 %all-to-all-done.5 = bf16[64,48,512]{2,1,0:T(8,128)(2,1)S(1)} async-done(((bf16[64,48,512]{2,1,0:T(8,128)(2,1)}), bf16[64,48,512]{2,1,0:T(8,128)(2,1)S(1)}, u32[]{:S(2)}, u32[]{:S(2)}) %all-to-all-start.5) | async-done | bytes 3145760 | tf_op jit(solution)/shard_map/all_to_all | solution.py:274
  209.5 0.5 convert_reduce_fusion
  210.0 0.6 slice_bitcast_fusion.1
  210.6 0.6 slice_bitcast_fusion.3
  211.2 0.6 fusion.1
  211.9 0.6 copy.22
  (20 shorter events, 0.1 us)
Async XLA Ops:
  0.6 21.0 %copy-start = (bf16[512,1536]{1,0:T(8,128)(2,1)S(1)}, bf16[512,1536]{1,0:T(8,128)(2,1)}, u32[]{:S(2)}) copy-start(bf16[512,1536]{1,0:T(8,128)(2,1)} %inproj.5) | copy-start | bytes 4718596
  0.6 21.0 %copy-start.2 = (bf16[512,512]{1,0:T(8,128)(2,1)S(1)}, bf16[512,512]{1,0:T(8,128)(2,1)}, u32[]{:S(2)}) copy-start(bf16[512,512]{1,0:T(8,128)(2,1)} %outproj.5) | copy-start | bytes 1572868
  21.7 34.6 %copy-start.1 = (bf16[512,512]{1,0:T(8,128)(2,1)S(1)}, bf16[512,512]{1,0:T(8,128)(2,1)}, u32[]{:S(2)}) copy-start(bf16[512,512]{1,0:T(8,128)(2,1)} %outproj.4) | copy-start | bytes 1572868
  27.7 0.7 copy-start.3
  28.4 0.7 copy-start.5
  29.2 1.0 copy-start.7
  30.2 0.7 copy-start.11
  30.9 25.3 %all-to-all-start.1 = ((bf16[32,22,512]{2,1,0:T(8,128)(2,1)}), bf16[32,22,512]{2,1,0:T(8,128)(2,1)S(1)}, u32[]{:S(2)}, u32[]{:S(2)}) async-start(bf16[32,22,512]{2,1,0:T(8,128)(2,1)} %get-tuple-element.29), calls=%async_computation.1 | async-start | bytes 1572864 | tf_op jit(solution)/shard_map/all_to_all | solution.py:274
  83.3 1.4 copy-start.9
  84.7 1.4 copy-start.10
  86.1 27.1 %copy-start.8 = (bf16[352,1536]{1,0:T(8,128)(2,1)S(1)}, bf16[352,1536]{1,0:T(8,128)(2,1)}, u32[]{:S(2)}) copy-start(bf16[352,1536]{1,0:T(8,128)(2,1)} %copy-done.7) | copy-start | bytes 3244036
  86.1 27.1 %copy-start.12 = (bf16[352,512]{1,0:T(8,128)(2,1)S(1)}, bf16[352,512]{1,0:T(8,128)(2,1)}, u32[]{:S(2)}) copy-start(bf16[352,512]{1,0:T(8,128)(2,1)} %copy-done.11) | copy-start | bytes 1081348
  92.5 52.7 %collective-permute-start.1 = (bf16[64,48,512]{2,1,0:T(8,128)(2,1)}, bf16[64,48,512]{2,1,0:T(8,128)(2,1)}, u32[]{:S(2)}, u32[]{:S(2)}) collective-permute-start(bf16[64,48,512]{2,1,0:T(8,128)(2,1)} %get-tuple-element.49), channel_id=1, source_target_pairs={{0,1},{1,0},{2,3},{3,2},{4,5},{5,4},{6,7},{7,6},{8,9},{9,8},{10,11... | collective-permute-start | bytes 9437192 | tf_op jit(solution)/shard_map/ppermute | solution.py:278
  113.2 8.6 %copy-start.4 = (bf16[352,512]{1,0:T(8,128)(2,1)S(1)}, bf16[352,512]{1,0:T(8,128)(2,1)}, u32[]{:S(2)}) copy-start(bf16[352,512]{1,0:T(8,128)(2,1)} %copy-done.3) | copy-start | bytes 1081348
  113.2 8.6 %copy-start.6 = (bf16[352,512]{1,0:T(8,128)(2,1)S(1)}, bf16[352,512]{1,0:T(8,128)(2,1)}, u32[]{:S(2)}) copy-start(bf16[352,512]{1,0:T(8,128)(2,1)} %copy-done.5) | copy-start | bytes 1081348
  123.2 3.7 %collective-permute-start = (bf16[64,16,512]{2,1,0:T(8,128)(2,1)S(1)}, bf16[64,16,512]{2,1,0:T(8,128)(2,1)}, u32[]{:S(2)}, u32[]{:S(2)}) collective-permute-start(bf16[64,16,512]{2,1,0:T(8,128)(2,1)S(1)} %get-tuple-element.39), channel_id=1, source_target_pairs={{0,1},{1,0},{2,3},{3,2},{4,5},{5,4},{6,7},{7,6},{8,9},{9,8},{10,11... | collective-permute-start | bytes 3145736 | tf_op jit(solution)/shard_map/ppermute | solution.py:278
  123.3 17.3 %all-to-all-start.3 = ((bf16[16,44,512]{2,1,0:T(8,128)(2,1)}), bf16[16,44,512]{2,1,0:T(8,128)(2,1)S(1)}, u32[]{:S(2)}, u32[]{:S(2)}) async-start(bf16[16,44,512]{2,1,0:T(8,128)(2,1)} %get-tuple-element.33), calls=%async_computation.3 | async-start | bytes 1572864 | tf_op jit(solution)/shard_map/all_to_all | solution.py:274
  140.5 10.4 %copy-start.13 = (bf16[16,44,512]{2,1,0:T(8,128)(2,1)}, bf16[16,44,512]{2,1,0:T(8,128)(2,1)S(1)}, u32[]{:S(2)}) copy-start(bf16[16,44,512]{2,1,0:T(8,128)(2,1)S(1)} %all-to-all-done.3) | copy-start | bytes 2162692
  140.5 23.3 %all-to-all-start.4 = ((bf16[64,16,512]{2,1,0:T(8,128)(2,1)}), bf16[64,16,512]{2,1,0:T(8,128)(2,1)S(1)}, u32[]{:S(2)}, u32[]{:S(2)}) async-start(bf16[64,16,512]{2,1,0:T(8,128)(2,1)} %add_convert_fusion.1), calls=%async_computation.4 | async-start | bytes 2097152 | tf_op jit(solution)/shard_map/all_to_all | solution.py:274
  163.9 1.0 copy-start.14
  164.9 44.7 %all-to-all-start.5 = ((bf16[64,48,512]{2,1,0:T(8,128)(2,1)}), bf16[64,48,512]{2,1,0:T(8,128)(2,1)S(1)}, u32[]{:S(2)}, u32[]{:S(2)}) async-start(bf16[64,48,512]{2,1,0:T(8,128)(2,1)} %add_convert_fusion), calls=%async_computation.5 | async-start | bytes 6291456 | tf_op jit(solution)/shard_map/all_to_all | solution.py:274
  169.6 4.1 %copy-start.15 = (bf16[64,16,512]{2,1,0:T(8,128)(2,1)S(1)}, bf16[64,16,512]{2,1,0:T(8,128)(2,1)}, u32[]{:S(2)}) copy-start(bf16[64,16,512]{2,1,0:T(8,128)(2,1)} %copy-done.14) | copy-start | bytes 3145732
where the time goes:
time: 213 us
  waiting for transfers between devices  75 us (35%)
  Pallas kernels  49.5 us (23%)
  blocking collectives  39.8 us (19%)
  starting transfers between devices  21.7 us (10%)
  local copies, waits for them, and re-layouts  15 us (7%)
  other arithmetic  10.7 us (5%)
    all_to_all x4, waiting for transfers between devices, swap(): return lax.all_to_all(array, axes, split_axis=0, concat_axis=0, tiled=True)  75 us
    pallas_call x5, Pallas kernels, call(): pl.pallas_call(kernel, out_shape=[jax.ShapeDtypeStruct(shape, kind) for s...  49.5 us
    all_to_all x2, blocking collectives, swap(): return lax.all_to_all(array, axes, split_axis=0, concat_axis=0, tiled=True)  39.8 us
    all_to_all x4, starting transfers between devices, swap(): return lax.all_to_all(array, axes, split_axis=0, concat_axis=0, tiled=True)  21.6 us
    unnamed x35, local copies, waits for them, and re-layouts  10.3 us
    convert_element_type x2, other arithmetic, scatter_sum(): both = (mine.astype(f32) + other.astype(f32)).astype(bf16)  8.36 us
  transfers between devices with their start and end apart: 6, of which 4 were waited for; matrix products, arithmetic and copies ran while one was open for 7% of the time, Pallas kernels for 5%

commit v1 on v0

v1 whole, which is shorter than its diff:
```python
import jax
import jax.numpy as jnp
from jax import lax
from jax.experimental import pallas as pl
from jax.experimental.pallas import tpu as pltpu
from jax.sharding import Mesh, PartitionSpec as P

HEADS = 8
WIDTH = 512
FF = 2048
HEAD = WIDTH // HEADS
SCALE = HEAD**-0.5
EPSILON = 1e-05
ROWS = 352
LATS = 32
NEAR = 22
PART = 11
LON = ("y", "l", "c")
TURN = ("y", "x", "h")
CHIPS = ("x", "h", "y", "l")
UNROLL = 1
GRANT = 56
BLOCKS = ((0, 128), (128, 128), (256, 96))
f32 = jnp.float32
bf16 = jnp.bfloat16


def normalize(values):
    center = values - jnp.mean(values, axis=-1, keepdims=True)
    inverse = lax.rsqrt(jnp.mean(center * center, axis=-1, keepdims=True) + EPSILON)
    return center * inverse, inverse


def norm_back(scaled, inverse, upstream):
    return inverse * (
        upstream
        - jnp.mean(upstream, axis=-1, keepdims=True)
        - scaled * jnp.mean(upstream * scaled, axis=-1, keepdims=True)
    )


def dot(left, right, left_dim=1, right_dim=0):
    dims = (((left_dim,), (right_dim,)), ((), ()))
    return lax.dot_general(left, right, dims, preferred_element_type=f32)


def half_of(values, half):
    lanes = lax.broadcasted_iota(jnp.int32, values.shape, 1) // HEAD
    return jnp.where(lanes == half, values, jnp.zeros_like(values))


def pair_columns(part, pair):
    return pl.ds(pl.multiple_of(part * WIDTH + pair * 2 * HEAD, 2 * HEAD), 2 * HEAD)


def over_pairs(body):
    lax.fori_loop(0, HEADS // 2, lambda pair, _: body(pair) or 0, 0, unroll=UNROLL)


def row_probabilities(packed, pair, half):
    keys = half_of(packed[:, pair_columns(1, pair)] * SCALE, half)
    scores = dot(keys, packed[:, pair_columns(0, pair)], 1, 1)
    powers = jnp.exp(scores - jnp.max(scores, axis=0, keepdims=True))
    return (powers * (1.0 / jnp.sum(powers, axis=0, keepdims=True))).astype(bf16)


def put_mixed(turned, pair, half, rows, mixed):
    place = pl.ds(pl.multiple_of(pair * 2 * HEAD + half * HEAD, HEAD), HEAD)
    turned[place, rows] = mixed[half * HEAD : (half + 1) * HEAD]


def put_grads(grads, pair, rows, found):
    for part in range(3):
        both = half_of(found[0][part], 0) + half_of(found[1][part], 1)
        grads[rows, pair_columns(part, pair)] = both.astype(bf16)


def attend_rows(packed, turned):
    def one_pair(pair):
        values = packed[:, pair_columns(2, pair)]
        probs = [row_probabilities(packed, pair, half) for half in range(2)]
        for half in range(2):
            put_mixed(turned, pair, half, pl.ds(0, ROWS), dot(values, probs[half], 0, 0))

    over_pairs(one_pair)


def row_weights(packed_far, weights_far, packed, weights, semaphores):
    mover = Mover(semaphores)
    mover.start(packed_far, packed).wait()

    def one_pair(pair):
        for half in range(2):
            weights[pair * 2 + half] = row_probabilities(packed, pair, half)

    over_pairs(one_pair)
    mover.start(weights, weights_far).wait()


def attend_rows_back(packed, upstream, weights, grads):
    def one_pair(pair):
        queries, keys, values = (packed[:, pair_columns(p, pair)] for p in range(3))
        grad_mix = upstream[:, pair_columns(0, pair)]
        found = []
        for half in range(2):
            low = weights[pair * 2 + half]
            probs = low.astype(f32)
            grad_probs = dot(half_of(values, half), grad_mix, 1, 1)
            inner = jnp.sum(grad_probs * probs, axis=0, keepdims=True)
            grad_scores = (probs * (grad_probs - inner) * SCALE).astype(bf16)
            found.append(
                (dot(grad_scores, keys, 0, 0), dot(grad_scores, queries), dot(low, grad_mix))
            )
        put_grads(grads, pair, pl.ds(0, ROWS), found)

    over_pairs(one_pair)


def column_lanes(count):
    return lax.broadcasted_iota(jnp.int32, (LATS, count), 1) // LATS


def own_columns(square):
    count = square.shape[0]
    lanes = column_lanes(count)
    kept = square[:LATS]
    for column in range(1, count // LATS):
        kept = jnp.where(lanes == column, square[column * LATS : (column + 1) * LATS], kept)
    return kept


def to_square(kept):
    count = kept.shape[1]
    lanes = column_lanes(count)
    parts = [jnp.where(lanes == column, kept, 0.0) for column in range(count // LATS)]
    return jnp.concatenate(parts, axis=0).astype(bf16)


def attend_columns(packed, turned, probs):
    def scores(pair):
        for first, count in BLOCKS:
            rows = pl.ds(first, count)
            queries, keys = (packed[rows, pair_columns(p, pair)] for p in range(2))
            for half in range(2):
                square = dot(half_of(keys * SCALE, half), queries, 1, 1)
                probs[pair * 2 + half, :, rows] = own_columns(square)

    over_pairs(scores)
    powers = probs[...]
    powers = jnp.exp(powers - jnp.max(powers, axis=1, keepdims=True))
    probs[...] = powers * (1.0 / jnp.sum(powers, axis=1, keepdims=True))

    def mix(pair):
        for first, count in BLOCKS:
            rows = pl.ds(first, count)
            values = packed[rows, pair_columns(2, pair)]
            for half in range(2):
                square = to_square(probs[pair * 2 + half, :, rows])
                put_mixed(turned, pair, half, rows, dot(values, square, 0, 0))

    over_pairs(mix)


def attend_columns_back(packed, upstream, probs, grad_scores, grads):
    def products(pair):
        for first, count in BLOCKS:
            rows = pl.ds(first, count)
            values, grad_mix = packed[rows, pair_columns(2, pair)], upstream[rows, pair_columns(0, pair)]
            for half in range(2):
                square = dot(half_of(values, half), grad_mix, 1, 1)
                grad_scores[pair * 2 + half, :, rows] = own_columns(square)

    over_pairs(products)
    grad_probs = grad_scores[...]
    inner = jnp.sum(grad_probs * probs[...], axis=1, keepdims=True)
    grad_scores[...] = probs[...] * (grad_probs - inner) * SCALE

    def combine(pair):
        for first, count in BLOCKS:
            rows = pl.ds(first, count)
            queries, keys = (packed[rows, pair_columns(p, pair)] for p in range(2))
            grad_mix = upstream[rows, pair_columns(0, pair)]
            found = []
            for half in range(2):
                square = to_square(grad_scores[pair * 2 + half, :, rows])
                weights = to_square(probs[pair * 2 + half, :, rows])
                found.append(
                    (dot(square, keys, 0, 0), dot(square, queries), dot(weights, grad_mix))
                )
            put_grads(grads, pair, rows, found)

    over_pairs(combine)


def project(normed, inproj, packed):
    for part in range(3):
        columns = pl.ds(part * WIDTH, WIDTH)
        packed[:, columns] = dot(normed, inproj[:, columns]).astype(bf16)


class Mover:
    def __init__(self, semaphores):
        self.semaphores, self.count = semaphores, 0

    def start(self, source, target):
        copy = pltpu.make_async_copy(source, target, self.semaphores.at[self.count])
        self.count += 1
        copy.start()
        return copy


def row_forward(
    pack, inproj_far, outproj_far,
    out, tokens_far, normed_far, packed_far, mixed_far,
    inproj, outproj, tokens, normed, packed, mixed, hidden, cotangent, turned, semaphores,
):
    mover = Mover(semaphores)
    inproj_in = mover.start(inproj_far, inproj)
    outproj_in = mover.start(outproj_far, outproj)
    for block in range(16):
        piece = pack[block].astype(f32)
        rows = pl.ds(block * NEAR, NEAR)
        hidden[rows, :] = piece[:NEAR]
        cotangent[rows, :] = piece[NEAR:]
    values = hidden[...]
    tokens[...] = values.astype(bf16)
    normed[...] = normalize(values)[0].astype(bf16)
    leaving = [mover.start(tokens, tokens_far), mover.start(normed, normed_far)]
    inproj_in.wait()
    project(normed[...], inproj, packed)
    leaving.append(mover.start(packed, packed_far))
    attend_rows(packed, turned)
    mixed[...] = turned[...].T.astype(bf16)
    leaving.append(mover.start(mixed, mixed_far))
    outproj_in.wait()
    hidden[...] += dot(mixed[...], outproj[...])
    for block in range(LATS):
        rows = pl.ds(block * PART, PART)
        out[block] = jnp.concatenate([hidden[rows, :], cotangent[rows, :]], axis=0).astype(bf16)
    for copy in leaving:
        copy.wait()


def row_backward(
    pack, tokens_far, packed_far, weights_far, inproj_far, outproj_far,
    out, grads_far, low_far,
    tokens, packed, weights, inproj, outproj, grads, low, hidden, output, upstream, semaphores,
):
    mover = Mover(semaphores)
    outproj_in = mover.start(outproj_far, outproj)
    coming = [mover.start(packed_far, packed), mover.start(weights_far, weights)]
    inproj_in = mover.start(inproj_far, inproj)
    tokens_in = mover.start(tokens_far, tokens)
    for block in range(LATS):
        piece = pack[block].astype(f32)
        rows = pl.ds(block * PART, PART)
        hidden[rows, :] = piece[:PART]
        output[rows, :] = piece[PART:]
    low[...] = hidden[...].astype(bf16)
    leaving = [mover.start(low, low_far)]
    outproj_in.wait()
    upstream[...] = dot(low[...], outproj[...], 1, 1).astype(bf16)
    for copy in coming:
        copy.wait()
    attend_rows_back(packed, upstream, weights, grads)
    leaving.append(mover.start(grads, grads_far))
    inproj_in.wait()
    grad_normed = dot(grads[...], inproj[...], 1, 1)
    tokens_in.wait()
    hidden[...] += norm_back(*normalize(tokens[...].astype(f32)), grad_normed)
    for block in range(16):
        rows = pl.ds(block * NEAR, NEAR)
        out[block] = jnp.concatenate([hidden[rows, :], output[rows, :]], axis=0).astype(bf16)
    for copy in leaving:
        copy.wait()


def to_columns(pack, first, second):
    for lat in range(LATS):
        piece = pack[lat].astype(f32)
        for tile in range(4):
            lanes = slice(tile * 128, (tile + 1) * 128)
            first[tile, pl.ds(lat, PART, stride=LATS), :] = piece[:PART, lanes]
            second[tile, pl.ds(lat, PART, stride=LATS), :] = piece[PART:, lanes]


def joined(tiles):
    return jnp.concatenate([tiles[tile] for tile in range(4)], axis=1)


def put_tiles(tiles, values):
    for tile in range(4):
        tiles[tile] = values[:, tile * 128 : (tile + 1) * 128]


def from_columns(out, first, second):
    for lat in range(LATS):
        rows = pl.ds(lat, PART, stride=LATS)
        parts = [
            jnp.concatenate([tiles[tile, rows, :] for tile in range(4)], axis=1)
            for tiles in (first, second)
        ]
        out[lat] = jnp.concatenate(parts, axis=0).astype(bf16)


def column_both(
    pack, inproj_far, outproj_far, mlp_in_far, mlp_out_far,
    out, normed_far, mixed_far, grads_far, low_far, normed_mlp_far, activated_far, grad_inner_far, cotangent_far,
    inproj, outproj, mlp_in, mlp_out, normed, mixed, grads, low, normed_mlp, activated, grad_inner, cotangent,
    packed, upstream, first, second, turned, hidden_one, hidden, grad_normed, output, probs, grad_scores,
    semaphores,
):
    mover = Mover(semaphores)
    inproj_in = mover.start(inproj_far, inproj)
    outproj_in = mover.start(outproj_far, outproj)
    coming = [mover.start(mlp_in_far, mlp_in), mover.start(mlp_out_far, mlp_out)]
    to_columns(pack, first, second)
    hidden_one[...] = joined(first)
    cotangent[...] = joined(second).astype(bf16)
    normed[...] = normalize(hidden_one[...])[0].astype(bf16)
    leaving = [mover.start(cotangent, cotangent_far), mover.start(normed, normed_far)]
    inproj_in.wait()
    project(normed[...], inproj, packed)
    attend_columns(packed, turned, probs)
    mixed[...] = turned[...].T.astype(bf16)
    leaving.append(mover.start(mixed, mixed_far))
    outproj_in.wait()
    hidden[...] = hidden_one[...] + dot(mixed[...], outproj[...])
    normed_mlp[...] = normalize(hidden[...])[0].astype(bf16)
    leaving.append(mover.start(normed_mlp, normed_mlp_far))
    output[...] = hidden[...]
    grad_normed[...] = jnp.zeros_like(grad_normed)
    for copy in coming:
        copy.wait()

    def one_chunk(chunk, _):
        columns = pl.ds(pl.multiple_of(chunk * 512, 512), 512)
        inner = dot(normed_mlp[...], mlp_in[:, columns])
        spread = 0.5 * (1.0 + lax.erf(inner * 2.0**-0.5))
        slope = spread + inner * (0.5 / jnp.pi) ** 0.5 * jnp.exp(-0.5 * inner * inner)
        active = (inner * spread).astype(bf16)
        activated[:, columns] = active
        output[...] += dot(active, mlp_out[columns, :])
        grad = (dot(cotangent[...], mlp_out[columns, :], 1, 1) * slope).astype(bf16)
        grad_inner[:, columns] = grad
        grad_normed[...] += dot(grad, mlp_in[:, columns], 1, 1)
        return 0

    lax.fori_loop(0, FF // 512, one_chunk, 0)
    leaving.append(mover.start(activated, activated_far))
    leaving.append(mover.start(grad_inner, grad_inner_far))
    put_tiles(second, output[...])
    back = norm_back(*normalize(hidden[...]), grad_normed[...])
    hidden[...] = cotangent[...].astype(f32) + back
    low[...] = hidden[...].astype(bf16)
    leaving.append(mover.start(low, low_far))
    upstream[...] = dot(low[...], outproj[...], 1, 1).astype(bf16)
    attend_columns_back(packed, upstream, probs, grad_scores, grads)
    leaving.append(mover.start(grads, grads_far))
    back = norm_back(*normalize(hidden_one[...]), dot(grads[...], inproj[...], 1, 1))
    put_tiles(first, hidden[...] + back)
    from_columns(out, first, second)
    for copy in leaving:
        copy.wait()


def mlp_terms(
    core, normed_far, activated_far, grad_inner_far, cotangent_far, mine_far, other_far,
    normed, activated, grad_inner, cotangent, mine, other, semaphores,
):
    mover = Mover(semaphores)
    soon = [mover.start(grad_inner_far, grad_inner), mover.start(normed_far, normed)]
    coming = [mover.start(cotangent_far, cotangent), mover.start(activated_far, activated)]
    for copy in soon:
        copy.wait()
    leaving = []
    for block in range(4):
        inner = dot(grad_inner[:, block * 512 : (block + 1) * 512], normed[...], 0, 0)
        if block == 0:
            for copy in coming:
                copy.wait()
        outer = dot(cotangent[:, block * 128 : (block + 1) * 128], activated[...], 0, 0)
        quarters = [
            outer[:, part * WIDTH : (part + 1) * WIDTH].reshape(32, 4, WIDTH) for part in range(4)
        ]
        both = jnp.concatenate([inner.reshape(32, 16, WIDTH)] + quarters, axis=1)
        both = both.astype(bf16).reshape(2, 4, 2, 2, 32, WIDTH)
        for high in range(2):
            even, odd = both[high, :, :, 0], both[high, :, :, 1]
            mine[block, high] = jnp.where(core[0] == 0, even, odd)
            other[block, high] = jnp.where(core[0] == 0, odd, even)
            leaving.append(mover.start(mine.at[block, high], mine_far.at[:, block, high]))
            leaving.append(mover.start(other.at[block, high], other_far.at[:, block, high]))
    for copy in leaving:
        copy.wait()


def attention_terms(
    core, grads_far, normed_far, low_far, mixed_far, mine, other, grads, normed, low, mixed, semaphores
):
    mover = Mover(semaphores)
    pairs = ((grads_far, grads), (normed_far, normed), (low_far, low), (mixed_far, mixed))
    for copy in [mover.start(far, near) for far, near in pairs]:
        copy.wait()
    for block in range(4):
        wide = dot(grads[:, block * 384 : (block + 1) * 384], normed[...], 0, 0)
        slim = dot(low[:, block * 128 : (block + 1) * 128], mixed[...], 0, 0)
        terms = [wide.reshape(32, 12, WIDTH), slim.reshape(32, 4, WIDTH)]
        terms = jnp.concatenate(terms, axis=1).astype(bf16).reshape(16, 2, 16, WIDTH)
        chips = pl.ds(block * 16, 16)
        mine[chips] = jnp.where(core[0] == 0, terms[:, 0], terms[:, 1])
        other[chips] = jnp.where(core[0] == 0, terms[:, 1], terms[:, 0])


def join_cores(lon_mine, lon_other, lat_mine, lat_other, out):
    for block in range(4):
        chips = pl.ds(block * 16, 16)
        lon = lon_mine[chips].astype(f32) + lon_other[chips].astype(f32)
        lat = lat_mine[chips].astype(f32) + lat_other[chips].astype(f32)
        out[chips] = jnp.concatenate([lon, lat], axis=1).astype(bf16)


def add_cores(mine_far, other_far, out_far, mine, other, semaphores):
    mover = Mover(semaphores)
    coming = [
        (mover.start(mine_far.at[block], mine.at[block]), mover.start(other_far.at[block], other.at[block]))
        for block in range(4)
    ]
    leaving = []
    for block in range(4):
        for copy in coming[block]:
            copy.wait()
        mine[block] = (mine[block].astype(f32) + other[block].astype(f32)).astype(bf16)
        leaving.append(mover.start(mine.at[block], out_far.at[block]))
    for copy in leaving:
        copy.wait()


def after_both(first, second, out):
    del first, second, out


SMEM, VMEM, HBM = pltpu.SMEM, pltpu.VMEM, pltpu.HBM


def call(kernel, args, outs, scratch, semaphores, gigaflops, aliases=None):
    arrays, places = zip(*args)
    scratch = [pltpu.VMEM(shape, kind) for shape, kind in scratch]
    if semaphores:
        scratch.append(pltpu.SemaphoreType.DMA((semaphores,)))
    return pl.pallas_call(
        kernel,
        out_shape=[jax.ShapeDtypeStruct(shape, kind) for shape, kind, _ in outs],
        in_specs=[pl.BlockSpec(memory_space=place) for place in places],
        out_specs=[pl.BlockSpec(memory_space=place) for _, _, place in outs],
        scratch_shapes=scratch,
        compiler_params=pltpu.CompilerParams(vmem_limit_bytes=GRANT << 20),
        cost_estimate=pl.CostEstimate(
            flops=int(gigaflops * 1e9), bytes_accessed=1 << 16, transcendentals=0
        ),
        input_output_aliases=aliases or {},
    )(*arrays)


def swap(array, axes):
    return lax.all_to_all(array, axes, split_axis=0, concat_axis=0, tiled=True)


def from_other_core(array):
    return lax.ppermute(array, "c", [(0, 1), (1, 0)])


NARROW = (ROWS, WIDTH)
QKV = (ROWS, 3 * WIDTH)
WIDE = (ROWS, FF)
TILES = (4, ROWS, 128)
TURNED = (WIDTH, ROWS)
TO_TURN = (LATS, 2 * PART, WIDTH)
TO_LON = (16, 2 * NEAR, WIDTH)
LON_WEIGHTS = (HEADS, ROWS, ROWS)
LAT_PROBS = (HEADS, LATS, ROWS)
IN, OUT, MLP_IN, MLP_OUT = (WIDTH, 3 * WIDTH), (WIDTH, WIDTH), (WIDTH, FF), (FF, WIDTH)
SUMS = (64, 16, WIDTH)
BY_CHIP, HELD = (4, 4, 2, 2, 32, WIDTH), (4, 2, 4, 2, 32, WIDTH)


def low(*shapes):
    return [(shape, bf16) for shape in shapes]


def far(*shapes):
    return [(shape, bf16, HBM) for shape in shapes]


def all_far(*arrays):
    return [(array, HBM) for array in arrays]


def weight_terms(core, grads, normed, low_upstream, mixed):
    return call(
        attention_terms,
        [(core, SMEM)] + all_far(grads, normed, low_upstream, mixed),
        [(SUMS, bf16, VMEM)] * 2,
        low(QKV, NARROW, NARROW, NARROW),
        4,
        0.1,
    )


def per_device(tokens, cotangent, inproj_lon, outproj_lon, inproj_lat, outproj_lat, mlp_in, mlp_out):
    core = lax.axis_index("c").astype(jnp.int32).reshape(1)
    pack = jnp.concatenate([tokens, cotangent], axis=2).reshape(TO_LON)
    pack, row_tokens, row_normed, row_packed, row_mixed = call(
        row_forward,
        [(swap(pack, LON), VMEM)] + all_far(inproj_lon, outproj_lon),
        [(TO_TURN, bf16, VMEM)] + far(NARROW, NARROW, QKV, NARROW),
        low(IN, OUT, NARROW, NARROW, QKV, NARROW) + [(NARROW, f32), (NARROW, f32), (TURNED, f32)],
        6,
        5.0,
    )
    pack, normed, mixed, grads, upstream, *saved = call(
        column_both,
        [(swap(pack, TURN), VMEM)] + all_far(inproj_lat, outproj_lat, mlp_in, mlp_out),
        [(TO_TURN, bf16, VMEM)] + far(NARROW, NARROW, QKV, NARROW, NARROW, WIDE, WIDE, NARROW),
        low(IN, OUT, MLP_IN, MLP_OUT, NARROW, NARROW, QKV, NARROW, NARROW, WIDE, WIDE, NARROW, QKV, NARROW)
        + [(TILES, f32), (TILES, f32), (TURNED, f32)] + [(NARROW, f32)] * 4 + [(LAT_PROBS, f32)] * 2,
        12,
        20.0,
    )
    mlp_mine, mlp_other = call(
        mlp_terms,
        [(core, SMEM)] + all_far(*saved),
        far(BY_CHIP, BY_CHIP),
        low(NARROW, WIDE, WIDE, NARROW, HELD, HELD),
        20,
        0.1,
    )
    (mlp,) = call(
        add_cores,
        all_far(mlp_mine, from_other_core(mlp_other)),
        far(BY_CHIP),
        low(BY_CHIP, BY_CHIP),
        12,
        0.1,
    )
    first_sum = lax.psum_scatter(mlp.reshape(FF, WIDTH), "y", scatter_dimension=0, tiled=True)
    lat_mine, lat_other = weight_terms(core, grads, normed, upstream, mixed)
    lat_other = from_other_core(lat_other)
    (weights,) = call(row_weights, all_far(row_packed), far(LON_WEIGHTS), low(QKV, LON_WEIGHTS), 2, 0.1)
    pack, grads, upstream = call(
        row_backward,
        [(swap(pack, TURN), VMEM)] + all_far(row_tokens, row_packed, weights, inproj_lon, outproj_lon),
        [(TO_LON, bf16, VMEM)] + far(QKV, NARROW),
        low(NARROW, QKV, LON_WEIGHTS, IN, OUT, QKV, NARROW) + [(NARROW, f32), (NARROW, f32), (NARROW, bf16)],
        7,
        8.0,
    )
    (first_sum,) = call(
        after_both, all_far(first_sum, upstream), far(first_sum.shape), [], 0, 0.01, {0: 0}
    )
    second_sum = lax.psum_scatter(first_sum, "x", scatter_dimension=0, tiled=True)
    lon_mine, lon_other = weight_terms(core, grads, row_normed, upstream, row_mixed)
    lon_other = from_other_core(lon_other)
    pack = swap(pack, LON).reshape(4, 4, 2 * NEAR, WIDTH).astype(f32)
    (both,) = call(
        join_cores,
        [(lon_mine, VMEM), (lon_other, VMEM), (lat_mine, VMEM), (lat_other, VMEM)],
        [((64, 32, WIDTH), bf16, VMEM)],
        [],
        0,
        0.1,
    )
    rows = jnp.sum(swap(both, CHIPS).astype(f32), axis=0)
    (second_sum,) = call(
        after_both, all_far(second_sum, both), far(second_sum.shape), [], 0, 0.01, {0: 0}
    )
    mlp = jnp.sum(swap(second_sum.reshape(4, 32, WIDTH), ("h", "l")).astype(f32), axis=0)
    return (
        pack[:, :, NEAR:],
        pack[:, :, :NEAR],
        rows[0:12].T,
        rows[12:16].T,
        rows[16:28].T,
        rows[28:32].T,
        mlp[0:16].T,
        mlp[16:32].reshape(4, 4, WIDTH).transpose(0, 2, 1).reshape(FF, 4),
    )


def solution(mesh):
    fine = Mesh(mesh.devices.reshape(4, 2, 4, 2, 2), ("x", "h", "y", "l", "c"))
    grid = P(("x", "h"), None, ("y", "l", "c"), None)
    columns = P(None, ("x", "h", "y", "l", "c"))
    return jax.shard_map(
        per_device,
        mesh=fine,
        in_specs=(grid, grid) + (P(),) * 6,
        out_specs=(grid, grid) + (columns,) * 6,
        check_vma=False,
    )
```

time: 213 us -> 208 us (0.977)
  blocking collectives: 39.8 us -> 19.2 us
  between operations: 0.79 us -> 14.2 us
  Pallas kernels: 49.5 us -> 62.4 us
  other arithmetic: 10.7 us -> 1.91 us
  local copies, waits for them, and re-layouts: 15 us -> 10 us
  starting transfers between devices: 21.7 us -> 25.7 us
    all_to_all x2 -> x1, blocking collectives: 39.8 us -> 19.2 us  [swap(): return lax.all_to_all(array, axes, split_axis=0, concat_axis=0, tiled=True)]
    pallas_call x5 -> x11, Pallas kernels: 49.5 us -> 62.4 us  [call(): pl.pallas_call(kernel, out_shape=[jax.ShapeDtypeStruct(shape, kind) for s...]
    convert_element_type x2 -> x0, other arithmetic: 8.36 us -> none  [scatter_sum(): both = (mine.astype(f32) + other.astype(f32)).astype(bf16)]
    all_to_all x4 -> x5, waiting for transfers between devices: 75 us -> 68.1 us  [swap(): return lax.all_to_all(array, axes, split_axis=0, concat_axis=0, tiled=True)]
    ppermute x2 -> x3, waiting for transfers between devices: 0.01 us -> 4.36 us  [from_other_core(): return lax.ppermute(array, 'c', [(0, 1), (1, 0)])]
    all_to_all x4 -> x5, starting transfers between devices: 21.6 us -> 24.8 us  [swap(): return lax.all_to_all(array, axes, split_axis=0, concat_axis=0, tiled=True)]
    unnamed x35 -> x13, local copies, waits for them, and re-layouts: 10.3 us -> 7.78 us
  transfers between devices with their start and end apart: 6 -> 10, of which waited for: 4 -> 6; matrix products, arithmetic and copies ran while one was open for 7% -> 2% of each run, Pallas kernels for 5% -> 14%
where the time goes in v1:
time: 208 us; the launch traced here: 207 us
  waiting for transfers between devices  73.2 us (35%)
  Pallas kernels  62.4 us (30%)
  starting transfers between devices  25.7 us (12%)
  blocking collectives  19.2 us (9%)
  between operations  14.2 us (7%)
  local copies, waits for them, and re-layouts  10 us (5%)
    all_to_all x5, waiting for transfers between devices, swap(): return lax.all_to_all(array, axes, split_axis=0, concat_axis=0, tiled=True)  68.1 us
    pallas_call x11, Pallas kernels, call(): pl.pallas_call(kernel, out_shape=[jax.ShapeDtypeStruct(shape, kind) for s...  62.4 us
    all_to_all x5, starting transfers between devices, swap(): return lax.all_to_all(array, axes, split_axis=0, concat_axis=0, tiled=True)  24.8 us
    all_to_all x1, blocking collectives, swap(): return lax.all_to_all(array, axes, split_axis=0, concat_axis=0, tiled=True)  19.2 us
    unnamed x13, local copies, waits for them, and re-layouts  7.78 us
    ppermute x3, waiting for transfers between devices, from_other_core(): return lax.ppermute(array, 'c', [(0, 1), (1, 0)])  4.36 us
  transfers between devices with their start and end apart: 10, of which 6 were waited for; matrix products, arithmetic and copies ran while one was open for 2% of the time, Pallas kernels for 14%

profile of v1, /device:TPU:0, one launch (start us, length us, event | category | flops | bytes accessed | tf_op | source)
XLA Modules:
  0.0 206.7 jit_solution(2287086555975789738)
XLA Ops:
  7.2 1.6 pad_maximum_fusion
  8.7 0.2 copy.18
  8.9 19.2 %all_to_all.30.pack = bf16[16,44,512]{2,1,0:T(8,128)(2,1)} all-to-all(bf16[16,44,512]{2,1,0:T(8,128)(2,1)S(1)} %bitcast.25), channel_id=1, replica_groups=mesh['x'=4,'h'=2,'y'=4,'l'=2,'c'=2] {'y','l','c'}, dimensions={0} | all-to-all | bytes 1441792 | tf_op jit(solution)/shard_map/all_to_all | solution.py:466
  28.1 8.3 %shard_map.143 = (bf16[32,22,512]{2,1,0:T(8,128)(2,1)}, bf16[352,512]{1,0:T(8,128)(2,1)}, bf16[352,512]{1,0:T(8,128)(2,1)}, bf16[352,1536]{1,0:T(8,128)(2,1)}, bf16[352,512]{1,0:T(8,128)(2,1)}) custom-call(bf16[16,44,512]{2,1,0:T(8,128)(2,1)} %all_to_all.30.pack, bf16[512,1536]{1,0:T(8,128)(2,1)} %inproj_far.5, bf16[512,512]{1,0:T(8,128)(2,1)} %outproj_far.5), custom_call_target="tpu_custom_call" | custom-call | flops 5000000000 | bytes 65536 | tf_op jit(solution)/shard_map/pallas_call | solution.py:451
  36.4 8.5 %all-to-all-start.1 = ((bf16[32,22,512]{2,1,0:T(8,128)(2,1)}), bf16[32,22,512]{2,1,0:T(8,128)(2,1)S(1)}, u32[]{:S(2)}, u32[]{:S(2)}) async-start(bf16[32,22,512]{2,1,0:T(8,128)(2,1)} %get-tuple-element.31), calls=%async_computation.1 | async-start | bytes 1572864 | tf_op jit(solution)/shard_map/all_to_all | solution.py:466
  44.9 0.2 reduce-scatter.3.cloned.1.call-start
  45.1 16.6 %all-to-all-done.1.pack = bf16[32,22,512]{2,1,0:T(8,128)(2,1)S(1)} async-done(((bf16[32,22,512]{2,1,0:T(8,128)(2,1)}), bf16[32,22,512]{2,1,0:T(8,128)(2,1)S(1)}, u32[]{:S(2)}, u32[]{:S(2)}) %all-to-all-start.1) | async-done | bytes 720928 | tf_op jit(solution)/shard_map/all_to_all | solution.py:466
  61.7 0.9 copy-done.4
  62.7 16.8 %shard_map.144 = (bf16[32,22,512]{2,1,0:T(8,128)(2,1)}, bf16[352,512]{1,0:T(8,128)(2,1)}, bf16[352,512]{1,0:T(8,128)(2,1)}, bf16[352,1536]{1,0:T(8,128)(2,1)}, b...) custom-call(bf16[32,22,512]{2,1,0:T(8,128)(2,1)} %copy-done.4, ...), custom_call_target="tpu_custom_call" | custom-call | flops 20000000000 | bytes 65536 | tf_op jit(solution)/shard_map/pallas_call | solution.py:451
  79.4 5.9 %shard_map.150 = (bf16[4,4,2,2,32,512]{5,4,3,2,1,0:T(8,128)(2,1)}, bf16[4,4,2,2,32,512]{5,4,3,2,1,0:T(8,128)(2,1)}) custom-call(s32[1]{0:T(128)} %bitcast.2.core, bf16[352,512]{1,0:T(8,128)(2,1)} %get-tuple-element.48.normed_far, bf16[352,2048]{1,0:T(8,128)(2,1)} %get-tuple-element.49.activated_far, bf16[352,2048]{1,0:T(8,128)(2,1)} %get-tuple-element.50.grad_inner_far, ...), custom_call_target="tpu_custom_call" | custom-call | flops 100000000 | bytes 65536 | tf_op jit(solution)/shard_map/pallas_call | solution.py:451
  85.3 0.1 collective-permute-start.2
  85.4 4.4 %collective-permute-done.2.other_far = bf16[4,4,2,2,32,512]{5,4,3,2,1,0:T(8,128)(2,1)S(1)} collective-permute-done((bf16[4,4,2,2,32,512]{5,4,3,2,1,0:T(8,128)(2,1)}, bf16[4,4,2,2,32,512]{5,4,3,2,1,0:T(8,128)(2,1)S(1)}, u32[]{:S(2)}, u32[]{:S(2)}) %collective-permute-start.2) | collective-permute-done | bytes 2097184 | tf_op jit(solution)/shard_map/ppermute | solution.py:470
  89.8 1.3 copy-done
  91.1 3.2 %shard_map.151 = bf16[4,4,2,2,32,512]{5,4,3,2,1,0:T(8,128)(2,1)} custom-call(bf16[4,4,2,2,32,512]{5,4,3,2,1,0:T(8,128)(2,1)} %get-tuple-element.52.mine_far, bf16[4,4,2,2,32,512]{5,4,3,2,1,0:T(8,128)(2,1)} %copy-done), custom_call_target="tpu_custom_call" | custom-call | flops 100000000 | bytes 65536 | tf_op jit(solution)/shard_map/pallas_call | solution.py:451
  94.2 0.0 reduce-scatter.3.cloned.1.call-update
  94.3 3.9 %all-to-all-start.2 = ((bf16[32,22,512]{2,1,0:T(8,128)(2,1)}), bf16[32,22,512]{2,1,0:T(8,128)(2,1)S(1)}, u32[]{:S(2)}, u32[]{:S(2)}) async-start(bf16[32,22,512]{2,1,0:T(8,128)(2,1)} %get-tuple-element.32), calls=%async_computation.2 | async-start | bytes 1572864 | tf_op jit(solution)/shard_map/all_to_all | solution.py:466
  98.2 4.9 %shard_map.145.weights_far = bf16[8,352,352]{2,1,0:T(8,128)(2,1)} custom-call(bf16[352,1536]{1,0:T(8,128)(2,1)} %get-tuple-element.34.packed_far), custom_call_target="tpu_custom_call" | custom-call | flops 100000000 | bytes 65536 | tf_op jit(solution)/shard_map/pallas_call | solution.py:451
  103.1 4.4 %shard_map.148 = (bf16[64,16,512]{2,1,0:T(8,128)(2,1)}, bf16[64,16,512]{2,1,0:T(8,128)(2,1)}) custom-call(s32[1]{0:T(128)} %bitcast.2.core, bf16[352,1536]{1,0:T(8,128)(2,1)} %get-tuple-element.42.grads_far, bf16[352,512]{1,0:T(8,128)(2,1)} %get-tuple-element.43.normed_far, bf16[352,512]{1,0:T(8,128)(2,1)} %get-tuple-element.44.low_far, ...), custom_call_target="tpu_custom_call" | custom-call | flops 100000000 | bytes 65536 | tf_op jit(solution)/shard_map/pallas_call | solution.py:451
  107.5 0.4 collective-permute-start.1
  107.9 7.5 %all-to-all-done.2.pack = bf16[32,22,512]{2,1,0:T(8,128)(2,1)S(1)} async-done(((bf16[32,22,512]{2,1,0:T(8,128)(2,1)}), bf16[32,22,512]{2,1,0:T(8,128)(2,1)S(1)}, u32[]{:S(2)}, u32[]{:S(2)}) %all-to-all-start.2) | async-done | bytes 720928 | tf_op jit(solution)/shard_map/all_to_all | solution.py:466
  115.4 0.9 copy-done.3
  116.3 10.7 %shard_map.146 = (bf16[16,44,512]{2,1,0:T(8,128)(2,1)}, bf16[352,1536]{1,0:T(8,128)(2,1)}, bf16[352,512]{1,0:T(8,128)(2,1)}) custom-call(bf16[32,22,512]{2,1,0:T(8,128)(2,1)} %copy-done.3, bf16[352,512]{1,0:T(8,128)(2,1)} %get-tuple-element.33.tokens_far, bf16[352,1536]{1,0:T(8,128)(2,1)} %get-tuple-element.34.packed_far, ...), custom_call_target="tpu_custom_call" | custom-call | flops 8000000000 | bytes 65536 | tf_op jit(solution)/shard_map/pallas_call | solution.py:451
  127.0 4.3 %shard_map.147 = (bf16[64,16,512]{2,1,0:T(8,128)(2,1)}, bf16[64,16,512]{2,1,0:T(8,128)(2,1)}) custom-call(s32[1]{0:T(128)} %bitcast.2.core, bf16[352,1536]{1,0:T(8,128)(2,1)} %get-tuple-element.36.grads_far, bf16[352,512]{1,0:T(8,128)(2,1)} %get-tuple-element.37.normed_far, bf16[352,512]{1,0:T(8,128)(2,1)} %get-tuple-element.38.low_far.second, ...), custom_call_target="tpu_custom_call" | custom-call | flops 100000000 | bytes 65536 | tf_op jit(solution)/shard_map/pallas_call | solution.py:451
  131.3 0.1 collective-permute-start
  131.4 3.6 %all-to-all-start.3 = ((bf16[16,44,512]{2,1,0:T(8,128)(2,1)}), bf16[16,44,512]{2,1,0:T(8,128)(2,1)S(1)}, u32[]{:S(2)}, u32[]{:S(2)}) async-start(bf16[16,44,512]{2,1,0:T(8,128)(2,1)} %get-tuple-element.35), calls=%async_computation.3 | async-start | bytes 1572864 | tf_op jit(solution)/shard_map/all_to_all | solution.py:466
  135.0 0.0 collective-permute-done.1.lat_other
  135.1 0.0 copy-start.1
  135.1 0.0 collective-permute-done.lon_other
  135.1 0.0 copy-start.2
  135.1 0.9 copy-done.1
  136.0 0.4 copy-done.2
  136.5 4.0 %shard_map.149.second = bf16[64,32,512]{2,1,0:T(8,128)(2,1)} custom-call(bf16[64,16,512]{2,1,0:T(8,128)(2,1)} %get-tuple-element.40.lon_mine, bf16[64,16,512]{2,1,0:T(8,128)(2,1)} %copy-done.2, bf16[64,16,512]{2,1,0:T(8,128)(2,1)} %get-tuple-element.46.lat_mine, bf16[64,16,512]{2,1,0:T(8,128)(2,1)} %copy-done.1), custom_call_target="tpu_custom_call" | custom-call | flops 100000000 | bytes 65536 | tf_op jit(solution)/shard_map/pallas_call | solution.py:451
  140.5 8.2 %all-to-all-done.3 = bf16[16,44,512]{2,1,0:T(8,128)(2,1)S(1)} async-done(((bf16[16,44,512]{2,1,0:T(8,128)(2,1)}), bf16[16,44,512]{2,1,0:T(8,128)(2,1)S(1)}, u32[]{:S(2)}, u32[]{:S(2)}) %all-to-all-start.3) | async-done | bytes 720928 | tf_op jit(solution)/shard_map/all_to_all | solution.py:466
  148.7 5.5 %all-to-all-start.4 = ((bf16[64,32,512]{2,1,0:T(8,128)(2,1)}), bf16[64,32,512]{2,1,0:T(8,128)(2,1)S(1)}, u32[]{:S(2)}, u32[]{:S(2)}) async-start(bf16[64,32,512]{2,1,0:T(8,128)(2,1)} %shard_map.149.second), calls=%async_computation.4 | async-start | bytes 4194304 | tf_op jit(solution)/shard_map/all_to_all | solution.py:466
  154.2 0.0 reduce-scatter.5.cloned.1.call-start
  154.2 0.0 reduce-scatter.3.cloned.1.call-done.first
  154.3 0.7 reduce-scatter.5.cloned.1.call-update
  154.9 0.2 fusion
  155.1 1.3 copy.22
  156.5 1.3 copy.23
  157.8 30.5 %all-to-all-done.4 = bf16[64,32,512]{2,1,0:T(8,128)(2,1)S(1)} async-done(((bf16[64,32,512]{2,1,0:T(8,128)(2,1)}), bf16[64,32,512]{2,1,0:T(8,128)(2,1)S(1)}, u32[]{:S(2)}, u32[]{:S(2)}) %all-to-all-start.4) | async-done | bytes 2097184 | tf_op jit(solution)/shard_map/all_to_all | solution.py:466
  188.3 0.3 convert_reduce_fusion
  188.6 0.6 slice_bitcast_fusion.1
  189.3 3.3 %all-to-all-start.5 = ((bf16[4,32,512]{2,1,0:T(8,128)(2,1)}), bf16[4,32,512]{2,1,0:T(8,128)(2,1)S(1)}, u32[]{:S(2)}, u32[]{:S(2)}) async-start(bf16[4,32,512]{2,1,0:T(8,128)(2,1)} %bitcast.26), calls=%async_computation.7 | async-start | bytes 262144 | tf_op jit(solution)/shard_map/all_to_all | solution.py:466
  192.6 0.6 slice_bitcast_fusion.3
  193.2 5.3 %all-to-all-done.5 = bf16[4,32,512]{2,1,0:T(8,128)(2,1)S(1)} async-done(((bf16[4,32,512]{2,1,0:T(8,128)(2,1)}), bf16[4,32,512]{2,1,0:T(8,128)(2,1)S(1)}, u32[]{:S(2)}, u32[]{:S(2)}) %all-to-all-start.5) | async-done | bytes 131104 | tf_op jit(solution)/shard_map/all_to_all | solution.py:466
  198.6 0.6 fusion.1
  199.2 0.6 copy.24
  (9 shorter events, 0.1 us)
Async XLA Ops:
  36.4 25.3 %all-to-all-start.1 = ((bf16[32,22,512]{2,1,0:T(8,128)(2,1)}), bf16[32,22,512]{2,1,0:T(8,128)(2,1)S(1)}, u32[]{:S(2)}, u32[]{:S(2)}) async-start(bf16[32,22,512]{2,1,0:T(8,128)(2,1)} %get-tuple-element.31), calls=%async_computation.1 | async-start | bytes 1572864 | tf_op jit(solution)/shard_map/all_to_all | solution.py:466
  44.9 109.4 %reduce-scatter.3.cloned.1.call-start = ((), (), s32[]{:S(2)}) async-start(), calls=%async_computation.8 | async-start | bytes 2621440 | tf_op jit(solution)/shard_map/reduce_scatter | solution.py:546
  61.7 0.9 copy-start.4
  85.3 4.5 %collective-permute-start.2 = (bf16[4,4,2,2,32,512]{5,4,3,2,1,0:T(8,128)(2,1)}, bf16[4,4,2,2,32,512]{5,4,3,2,1,0:T(8,128)(2,1)S(1)}, u32[]{:S(2)}, u32[]{:S(2)}) collective-permute-start(bf16[4,4,2,2,32,512]{5,4,3,2,1,0:T(8,128)(2,1)} %get-tuple-element.53), channel_id=1, source_target_pairs={{0,1},{1,0},{2,3},{3,2},{4,5},{5,4},{6,7},{7,6},{8,9},{9,8},{10,11... | collective-permute-start | bytes 6291464 | tf_op jit(solution)/shard_map/ppermute | solution.py:470
  89.8 1.3 copy-start
  94.3 21.1 %all-to-all-start.2 = ((bf16[32,22,512]{2,1,0:T(8,128)(2,1)}), bf16[32,22,512]{2,1,0:T(8,128)(2,1)S(1)}, u32[]{:S(2)}, u32[]{:S(2)}) async-start(bf16[32,22,512]{2,1,0:T(8,128)(2,1)} %get-tuple-element.32), calls=%async_computation.2 | async-start | bytes 1572864 | tf_op jit(solution)/shard_map/all_to_all | solution.py:466
  107.5 27.5 %collective-permute-start.1 = (bf16[64,16,512]{2,1,0:T(8,128)(2,1)}, bf16[64,16,512]{2,1,0:T(8,128)(2,1)S(1)}, u32[]{:S(2)}, u32[]{:S(2)}) collective-permute-start(bf16[64,16,512]{2,1,0:T(8,128)(2,1)} %get-tuple-element.47), channel_id=1, source_target_pairs={{0,1},{1,0},{2,3},{3,2},{4,5},{5,4},{6,7},{7,6},{8,9},{9,8},{10,11... | collective-permute-start | bytes 3145736 | tf_op jit(solution)/shard_map/ppermute | solution.py:470
  115.4 0.9 copy-start.3
  131.3 3.7 %collective-permute-start = (bf16[64,16,512]{2,1,0:T(8,128)(2,1)}, bf16[64,16,512]{2,1,0:T(8,128)(2,1)S(1)}, u32[]{:S(2)}, u32[]{:S(2)}) collective-permute-start(bf16[64,16,512]{2,1,0:T(8,128)(2,1)} %get-tuple-element.41), channel_id=1, source_target_pairs={{0,1},{1,0},{2,3},{3,2},{4,5},{5,4},{6,7},{7,6},{8,9},{9,8},{10,11... | collective-permute-start | bytes 3145736 | tf_op jit(solution)/shard_map/ppermute | solution.py:470
  131.4 17.3 %all-to-all-start.3 = ((bf16[16,44,512]{2,1,0:T(8,128)(2,1)}), bf16[16,44,512]{2,1,0:T(8,128)(2,1)S(1)}, u32[]{:S(2)}, u32[]{:S(2)}) async-start(bf16[16,44,512]{2,1,0:T(8,128)(2,1)} %get-tuple-element.35), calls=%async_computation.3 | async-start | bytes 1572864 | tf_op jit(solution)/shard_map/all_to_all | solution.py:466
  135.1 1.0 copy-start.1
  135.1 1.4 copy-start.2
  148.7 39.6 %all-to-all-start.4 = ((bf16[64,32,512]{2,1,0:T(8,128)(2,1)}), bf16[64,32,512]{2,1,0:T(8,128)(2,1)S(1)}, u32[]{:S(2)}, u32[]{:S(2)}) async-start(bf16[64,32,512]{2,1,0:T(8,128)(2,1)} %shard_map.149.second), calls=%async_computation.4 | async-start | bytes 4194304 | tf_op jit(solution)/shard_map/all_to_all | solution.py:466
  154.2 35.1 %reduce-scatter.5.cloned.1.call-start = ((), (), s32[]{:S(2)}) async-start(), calls=%async_computation.9 | async-start | bytes 655360 | tf_op jit(solution)/shard_map/reduce_scatter | solution.py:561
  189.3 9.3 %all-to-all-start.5 = ((bf16[4,32,512]{2,1,0:T(8,128)(2,1)}), bf16[4,32,512]{2,1,0:T(8,128)(2,1)S(1)}, u32[]{:S(2)}, u32[]{:S(2)}) async-start(bf16[4,32,512]{2,1,0:T(8,128)(2,1)} %bitcast.26), calls=%async_computation.7 | async-start | bytes 262144 | tf_op jit(solution)/shard_map/all_to_all | solution.py:466
Sparse Core Ops, SparseCore 0:
  94.4 33.3 reduce-scatter.2
  157.5 26.1 reduce-scatter.4

commit v2 on v1

--- a/solution.py
+++ b/solution.py
@@ -15,11 +15,11 @@
 LATS = 32
 NEAR = 22
 PART = 11
+PIECE = 13
 LON = ("y", "l", "c")
 TURN = ("y", "x", "h")
 CHIPS = ("x", "h", "y", "l")
-UNROLL = 1
-GRANT = 56
+UNROLL = HEADS // 2
 BLOCKS = ((0, 128), (128, 128), (256, 96))
 f32 = jnp.float32
 bf16 = jnp.bfloat16
@@ -85,8 +85,9 @@
     over_pairs(one_pair)
 
 
-def row_weights(packed_far, weights_far, packed, weights, semaphores):
+def row_weights(packed_far, after, weights_far, packed, weights, semaphores):
     mover = Mover(semaphores)
+    del after
     mover.start(packed_far, packed).wait()
 
     def one_pair(pair):
@@ -242,28 +243,27 @@
 
 
 def row_backward(
-    pack, tokens_far, packed_far, weights_far, inproj_far, outproj_far,
-    out, grads_far, low_far,
-    tokens, packed, weights, inproj, outproj, grads, low, hidden, output, upstream, semaphores,
+    core, pack, tokens_far, normed_far, packed_far, mixed_far, weights_far, inproj_far, outproj_far,
+    out, mine, other,
+    tokens, normed, packed, mixed, weights, inproj, outproj, grads, low, hidden, output, upstream, semaphores,
 ):
     mover = Mover(semaphores)
     outproj_in = mover.start(outproj_far, outproj)
     coming = [mover.start(packed_far, packed), mover.start(weights_far, weights)]
     inproj_in = mover.start(inproj_far, inproj)
     tokens_in = mover.start(tokens_far, tokens)
+    last = [mover.start(normed_far, normed), mover.start(mixed_far, mixed)]
     for block in range(LATS):
         piece = pack[block].astype(f32)
         rows = pl.ds(block * PART, PART)
         hidden[rows, :] = piece[:PART]
         output[rows, :] = piece[PART:]
     low[...] = hidden[...].astype(bf16)
-    leaving = [mover.start(low, low_far)]
     outproj_in.wait()
     upstream[...] = dot(low[...], outproj[...], 1, 1).astype(bf16)
     for copy in coming:
         copy.wait()
     attend_rows_back(packed, upstream, weights, grads)
-    leaving.append(mover.start(grads, grads_far))
     inproj_in.wait()
     grad_normed = dot(grads[...], inproj[...], 1, 1)
     tokens_in.wait()
@@ -271,8 +271,9 @@
     for block in range(16):
         rows = pl.ds(block * NEAR, NEAR)
         out[block] = jnp.concatenate([hidden[rows, :], output[rows, :]], axis=0).astype(bf16)
-    for copy in leaving:
+    for copy in last:
         copy.wait()
+    split_terms(core, grads, normed, low, mixed, mine, other)
 
 
 def to_columns(pack, first, second):
@@ -346,7 +347,7 @@
         grad_normed[...] += dot(grad, mlp_in[:, columns], 1, 1)
         return 0
 
-    lax.fori_loop(0, FF // 512, one_chunk, 0)
+    lax.fori_loop(0, FF // 512, one_chunk, 0, unroll=2)
     leaving.append(mover.start(activated, activated_far))
     leaving.append(mover.start(grad_inner, grad_inner_far))
     put_tiles(second, output[...])
@@ -364,97 +365,120 @@
         copy.wait()
 
 
-def mlp_terms(
-    core, normed_far, activated_far, grad_inner_far, cotangent_far, mine_far, other_far,
-    normed, activated, grad_inner, cotangent, mine, other, semaphores,
-):
+def block_terms(block, grads, normed, low, mixed):
+    wide = dot(grads[:, block * 384 : (block + 1) * 384], normed[...], 0, 0)
+    slim = dot(low[:, block * 128 : (block + 1) * 128], mixed[...], 0, 0)
+    return [wide.reshape(32, 12, WIDTH), slim.reshape(32, 4, WIDTH)]
+
+
+def column_terms(place, *refs):
+    far, mine, others, near, semaphores = refs[:8], refs[8], refs[9:14], refs[14:22], refs[22]
     mover = Mover(semaphores)
-    soon = [mover.start(grad_inner_far, grad_inner), mover.start(normed_far, normed)]
-    coming = [mover.start(cotangent_far, cotangent), mover.start(activated_far, activated)]
-    for copy in soon:
+    coming = [mover.start(source, target) for source, target in zip(far, near)]
+    normed_mlp, activated, grad_inner, cotangent, grads, normed, low, mixed = near
+    for copy in coming:
         copy.wait()
+    for block in range(4):
+        terms = block_terms(block, grads, normed, low, mixed)
+        inner = dot(grad_inner[:, block * 512 : (block + 1) * 512], normed_mlp[...], 0, 0)
+        outer = dot(cotangent[:, block * 128 : (block + 1) * 128], activated[...], 0, 0)
+        terms.append(inner.reshape(32, 16, WIDTH))
+        for part in range(4):
+            terms.append(outer[:, part * WIDTH : (part + 1) * WIDTH].reshape(32, 4, WIDTH))
+        both = jnp.concatenate(terms, axis=1).astype(bf16).reshape(2, 4, 2, 2, 48, WIDTH)
+        for high in range(2):
+            even, odd = both[high, :, :, 0], both[high, :, :, 1]
+            mine[block, :, high] = jnp.where(place[0] == 0, even, odd)
+            leaving = jnp.where(place[0] == 0, odd, even)
+            for row in range(4):
+                for low_z in range(2):
+                    piece, chip = divmod(16 * block + 4 * row + 2 * high + low_z, PIECE)
+                    others[piece][chip] = leaving[row, low_z]
+
+
+def split_terms(place, grads, normed, low, mixed, mine, other):
+    for block in range(4):
+        terms = jnp.concatenate(block_terms(block, grads, normed, low, mixed), axis=1)
+        terms = terms.astype(bf16).reshape(16, 2, 16, WIDTH)
+        chips = pl.ds(block * 16, 16)
+        mine[chips] = jnp.where(place[0] == 0, terms[:, 0], terms[:, 1])
+        other[chips] = jnp.where(place[0] == 0, terms[:, 1], terms[:, 0])
+
+
+def join_cores(mine, other, out):
+    for block in range(4):
+        chips = pl.ds(block * 16, 16)
+        out[chips] = (mine[chips].astype(f32) + other[chips].astype(f32)).astype(bf16)
+
+
+def add_cores(mine, *refs):
+    others, out_far, total, semaphores = refs[:5], *refs[5:]
+    mover = Mover(semaphores)
     leaving = []
     for block in range(4):
-        inner = dot(grad_inner[:, block * 512 : (block + 1) * 512], normed[...], 0, 0)
-        if block == 0:
-            for copy in coming:
-                copy.wait()
-        outer = dot(cotangent[:, block * 128 : (block + 1) * 128], activated[...], 0, 0)
-        quarters = [
-            outer[:, part * WIDTH : (part + 1) * WIDTH].reshape(32, 4, WIDTH) for part in range(4)
-        ]
-        both = jnp.concatenate([inner.reshape(32, 16, WIDTH)] + quarters, axis=1)
-        both = both.astype(bf16).reshape(2, 4, 2, 2, 32, WIDTH)
-        for high in range(2):
-            even, odd = both[high, :, :, 0], both[high, :, :, 1]
-            mine[block, high] = jnp.where(core[0] == 0, even, odd)
-            other[block, high] = jnp.where(core[0] == 0, odd, even)
-            leaving.append(mover.start(mine.at[block, high], mine_far.at[:, block, high]))
-            leaving.append(mover.start(other.at[block, high], other_far.at[:, block, high]))
+        for place in range(16):
+            row, rest = divmod(place, 4)
+            high, low_z = divmod(rest, 2)
+            piece, chip = divmod(16 * block + place, PIECE)
+            own = mine[block, row, high, low_z].astype(f32)
+            total[block, row, high, low_z] = (own + others[piece][chip].astype(f32)).astype(bf16)
+        leaving.append(mover.start(total.at[block], out_far.at[block]))
     for copy in leaving:
         copy.wait()
 
 
-def attention_terms(
-    core, grads_far, normed_far, low_far, mixed_far, mine, other, grads, normed, low, mixed, semaphores
-):
-    mover = Mover(semaphores)
-    pairs = ((grads_far, grads), (normed_far, normed), (low_far, low), (mixed_far, mixed))
-    for copy in [mover.start(far, near) for far, near in pairs]:
-        copy.wait()
-    for block in range(4):
-        wide = dot(grads[:, block * 384 : (block + 1) * 384], normed[...], 0, 0)
-        slim = dot(low[:, block * 128 : (block + 1) * 128], mixed[...], 0, 0)
-        terms = [wide.reshape(32, 12, WIDTH), slim.reshape(32, 4, WIDTH)]
-        terms = jnp.concatenate(terms, axis=1).astype(bf16).reshape(16, 2, 16, WIDTH)
-        chips = pl.ds(block * 16, 16)
-        mine[chips] = jnp.where(core[0] == 0, terms[:, 0], terms[:, 1])
-        other[chips] = jnp.where(core[0] == 0, terms[:, 1], terms[:, 0])
-
-
-def join_cores(lon_mine, lon_other, lat_mine, lat_other, out):
-    for block in range(4):
-        chips = pl.ds(block * 16, 16)
-        lon = lon_mine[chips].astype(f32) + lon_other[chips].astype(f32)
-        lat = lat_mine[chips].astype(f32) + lat_other[chips].astype(f32)
-        out[chips] = jnp.concatenate([lon, lat], axis=1).astype(bf16)
-
-
-def add_cores(mine_far, other_far, out_far, mine, other, semaphores):
-    mover = Mover(semaphores)
-    coming = [
-        (mover.start(mine_far.at[block], mine.at[block]), mover.start(other_far.at[block], other.at[block]))
-        for block in range(4)
+def sum_row(parts, lon_in, lon_out):
+    total = jnp.sum(parts[...].astype(f32), axis=0)
+    lon_in[...] = total[0:12]
+    lon_out[...] = total[12:16]
+
+
+def pick_y(place, blocks, *outs):
+    for step in range(4):
+        outs[step][...] = blocks[jnp.bitwise_xor(place[1], step)]
+
+
+def sum_pick_z(place, *refs):
+    parts, outs, total = refs[:4], refs[4:8], refs[8]
+    added = sum(part[...].astype(f32) for part in parts)
+    total[...] = added.astype(bf16).reshape(total.shape)
+    for step in range(4):
+        outs[step][...] = total[jnp.bitwise_xor(place[2], step)]
+
+
+def sum_column(*refs):
+    parts, (lat_in, lat_out, wide_in, wide_out) = refs[:4], refs[4:]
+    total = sum(part[...].astype(f32) for part in parts)
+    lat_in[...] = total[0:12]
+    lat_out[...] = total[12:16]
+    wide_in[...] = total[16:32]
+    for part in range(4):
+        wide_out[:, part * WIDTH : (part + 1) * WIDTH] = total[32 + 4 * part : 36 + 4 * part]
+
+
+SMEM, VMEM, HBM = pltpu.SMEM, pltpu.VMEM, pltpu.HBM
+
+
+def call(kernel, args, outs, scratch, semaphores, megabytes, gigaflops, aliases=None):
+    arrays = [
+        pltpu.with_memory_space_constraint(array, HBM) if place is HBM else array
+        for array, place in args
     ]
-    leaving = []
-    for block in range(4):
-        for copy in coming[block]:
-            copy.wait()
-        mine[block] = (mine[block].astype(f32) + other[block].astype(f32)).astype(bf16)
-        leaving.append(mover.start(mine.at[block], out_far.at[block]))
-    for copy in leaving:
-        copy.wait()
-
-
-def after_both(first, second, out):
-    del first, second, out
-
-
-SMEM, VMEM, HBM = pltpu.SMEM, pltpu.VMEM, pltpu.HBM
-
-
-def call(kernel, args, outs, scratch, semaphores, gigaflops, aliases=None):
-    arrays, places = zip(*args)
     scratch = [pltpu.VMEM(shape, kind) for shape, kind in scratch]
     if semaphores:
         scratch.append(pltpu.SemaphoreType.DMA((semaphores,)))
     return pl.pallas_call(
         kernel,
-        out_shape=[jax.ShapeDtypeStruct(shape, kind) for shape, kind, _ in outs],
-        in_specs=[pl.BlockSpec(memory_space=place) for place in places],
-        out_specs=[pl.BlockSpec(memory_space=place) for _, _, place in outs],
+        out_shape=[
+            jax.ShapeDtypeStruct(shape, kind) if place is pl.ANY else place(shape, kind)
+            for shape, kind, place in outs
+        ],
+        in_specs=[pl.BlockSpec(memory_space=place) for _, place in args],
+        out_specs=[
+            pl.BlockSpec(memory_space=VMEM if place is pl.ANY else place) for _, _, place in outs
+        ],
         scratch_shapes=scratch,
-        compiler_params=pltpu.CompilerParams(vmem_limit_bytes=GRANT << 20),
+        compiler_params=pltpu.CompilerParams(vmem_limit_bytes=megabytes << 20),
         cost_estimate=pl.CostEstimate(
             flops=int(gigaflops * 1e9), bytes_accessed=1 << 16, transcendentals=0
         ),
@@ -464,6 +488,15 @@
 
 def swap(array, axes):
     return lax.all_to_all(array, axes, split_axis=0, concat_axis=0, tiled=True)
+
+
+def trade(parts, axes):
+    moved = [
+        lax.ppermute(part, axes, [(place, place ^ step) for place in range(4)])
+        for step, part in enumerate(parts)
+        if step
+    ]
+    return [parts[0], *moved]
 
 
 def from_other_core(array):
@@ -481,7 +514,7 @@
 LAT_PROBS = (HEADS, LATS, ROWS)
 IN, OUT, MLP_IN, MLP_OUT = (WIDTH, 3 * WIDTH), (WIDTH, WIDTH), (WIDTH, FF), (FF, WIDTH)
 SUMS = (64, 16, WIDTH)
-BY_CHIP, HELD = (4, 4, 2, 2, 32, WIDTH), (4, 2, 4, 2, 32, WIDTH)
+BY_CHIP = (4, 4, 2, 2, 48, WIDTH)
 
 
 def low(*shapes):
@@ -496,19 +529,8 @@
     return [(array, HBM) for array in arrays]
 
 
-def weight_terms(core, grads, normed, low_upstream, mixed):
-    return call(
-        attention_terms,
-        [(core, SMEM)] + all_far(grads, normed, low_upstream, mixed),
-        [(SUMS, bf16, VMEM)] * 2,
-        low(QKV, NARROW, NARROW, NARROW),
-        4,
-        0.1,
-    )
-
-
 def per_device(tokens, cotangent, inproj_lon, outproj_lon, inproj_lat, outproj_lat, mlp_in, mlp_out):
-    core = lax.axis_index("c").astype(jnp.int32).reshape(1)
+    core = jnp.stack([lax.axis_index(axes) for axes in ("c", "y", ("h", "l"))]).astype(jnp.int32)
     pack = jnp.concatenate([tokens, cotangent], axis=2).reshape(TO_LON)
     pack, row_tokens, row_normed, row_packed, row_mixed = call(
         row_forward,
@@ -516,6 +538,7 @@
         [(TO_TURN, bf16, VMEM)] + far(NARROW, NARROW, QKV, NARROW),
         low(IN, OUT, NARROW, NARROW, QKV, NARROW) + [(NARROW, f32), (NARROW, f32), (TURNED, f32)],
         6,
+        20,
         5.0,
     )
     pack, normed, mixed, grads, upstream, *saved = call(
@@ -525,65 +548,95 @@
         low(IN, OUT, MLP_IN, MLP_OUT, NARROW, NARROW, QKV, NARROW, NARROW, WIDE, WIDE, NARROW, QKV, NARROW)
         + [(TILES, f32), (TILES, f32), (TURNED, f32)] + [(NARROW, f32)] * 4 + [(LAT_PROBS, f32)] * 2,
         12,
+        36,
         20.0,
     )
-    mlp_mine, mlp_other = call(
-        mlp_terms,
-        [(core, SMEM)] + all_far(*saved),
-        far(BY_CHIP, BY_CHIP),
-        low(NARROW, WIDE, WIDE, NARROW, HELD, HELD),
+    mine, *others = call(
+        column_terms,
+        [(core, SMEM)] + all_far(*saved, grads, normed, upstream, mixed),
+        [(BY_CHIP, bf16, VMEM)] + [((PIECE, 48, WIDTH), bf16, VMEM)] * 5,
+        low(NARROW, WIDE, WIDE, NARROW, QKV, NARROW, NARROW, NARROW),
+        8,
+        32,
+        0.1,
+    )
+    (weights,) = call(
+        row_weights,
+        [(row_packed, HBM), (mine, pl.ANY)],
+        far(LON_WEIGHTS),
+        low(QKV, LON_WEIGHTS),
+        2,
+        12,
+        0.1,
+    )
+    (column,) = call(
+        add_cores,
+        [(mine, VMEM)] + [(from_other_core(other), VMEM) for other in others],
+        far(BY_CHIP),
+        low(BY_CHIP),
+        4,
         20,
         0.1,
     )
-    (mlp,) = call(
-        add_cores,
-        all_far(mlp_mine, from_other_core(mlp_other)),
-        far(BY_CHIP),
-        low(BY_CHIP, BY_CHIP),
-        12,
-        0.1,
-    )
-    first_sum = lax.psum_scatter(mlp.reshape(FF, WIDTH), "y", scatter_dimension=0, tiled=True)
-    lat_mine, lat_other = weight_terms(core, grads, normed, upstream, mixed)
-    lat_other = from_other_core(lat_other)
-    (weights,) = call(row_weights, all_far(row_packed), far(LON_WEIGHTS), low(QKV, LON_WEIGHTS), 2, 0.1)
-    pack, grads, upstream = call(
+    column = lax.psum_scatter(column.reshape(3072, WIDTH), "x", scatter_dimension=0, tiled=True)
+    pack, lon_mine, lon_other = call(
         row_backward,
-        [(swap(pack, TURN), VMEM)] + all_far(row_tokens, row_packed, weights, inproj_lon, outproj_lon),
-        [(TO_LON, bf16, VMEM)] + far(QKV, NARROW),
-        low(NARROW, QKV, LON_WEIGHTS, IN, OUT, QKV, NARROW) + [(NARROW, f32), (NARROW, f32), (NARROW, bf16)],
+        [(core, SMEM), (swap(pack, TURN), VMEM)]
+        + all_far(row_tokens, row_normed, row_packed, row_mixed, weights, inproj_lon, outproj_lon),
+        [(TO_LON, bf16, VMEM), (SUMS, bf16, VMEM), (SUMS, bf16, VMEM)],
+        low(NARROW, NARROW, QKV, NARROW, LON_WEIGHTS, IN, OUT, QKV, NARROW)
+        + [(NARROW, f32), (NARROW, f32), (NARROW, bf16)],
         7,
-        8.0,
-    )
-    (first_sum,) = call(
-        after_both, all_far(first_sum, upstream), far(first_sum.shape), [], 0, 0.01, {0: 0}
-    )
-    second_sum = lax.psum_scatter(first_sum, "x", scatter_dimension=0, tiled=True)
-    lon_mine, lon_other = weight_terms(core, grads, row_normed, upstream, row_mixed)
+        28,
+        60.0,
+    )
     lon_other = from_other_core(lon_other)
-    pack = swap(pack, LON).reshape(4, 4, 2 * NEAR, WIDTH).astype(f32)
+    pack = swap(pack, LON)
     (both,) = call(
-        join_cores,
-        [(lon_mine, VMEM), (lon_other, VMEM), (lat_mine, VMEM), (lat_other, VMEM)],
-        [((64, 32, WIDTH), bf16, VMEM)],
+        join_cores, [(lon_mine, VMEM), (lon_other, VMEM)], [(SUMS, bf16, VMEM)], [], 0, 12, 0.1
+    )
+    unpacked = pack.reshape(4, 4, 2 * NEAR, WIDTH).astype(f32)
+    lon = call(
+        sum_row,
+        [(swap(both, CHIPS), VMEM)],
+        [((12, WIDTH), f32, pl.ANY), ((4, WIDTH), f32, pl.ANY)],
         [],
         0,
+        12,
+        60.0,
+    )
+    parts = call(
+        pick_y,
+        [(core, SMEM), (column.reshape(4, 192, WIDTH), VMEM)],
+        [((192, WIDTH), bf16, VMEM)] * 4,
+        [],
+        0,
+        8,
+        0.01,
+    )
+    parts = call(
+        sum_pick_z,
+        [(core, SMEM)] + [(part, VMEM) for part in trade(parts, "y")],
+        [((48, WIDTH), bf16, VMEM)] * 4,
+        low((4, 48, WIDTH)),
+        0,
+        8,
+        0.01,
+    )
+    column = call(
+        sum_column,
+        [(part, VMEM) for part in trade(parts, ("h", "l"))],
+        [((rows, lanes), f32, pl.ANY) for rows, lanes in ((12, WIDTH), (4, WIDTH), (16, WIDTH), (4, FF))],
+        [],
+        0,
+        4,
         0.1,
     )
-    rows = jnp.sum(swap(both, CHIPS).astype(f32), axis=0)
-    (second_sum,) = call(
-        after_both, all_far(second_sum, both), far(second_sum.shape), [], 0, 0.01, {0: 0}
-    )
-    mlp = jnp.sum(swap(second_sum.reshape(4, 32, WIDTH), ("h", "l")).astype(f32), axis=0)
     return (
-        pack[:, :, NEAR:],
-        pack[:, :, :NEAR],
-        rows[0:12].T,
-        rows[12:16].T,
-        rows[16:28].T,
-        rows[28:32].T,
-        mlp[0:16].T,
-        mlp[16:32].reshape(4, 4, WIDTH).transpose(0, 2, 1).reshape(FF, 4),
+        unpacked[:, :, NEAR:],
+        unpacked[:, :, :NEAR],
+        *(array.T for array in lon),
+        *(array.T for array in column),
     )
 
 

time: 208 us -> 172 us (0.83)
  waiting for transfers between devices: 73.2 us -> 46.5 us
  Pallas kernels: 62.4 us -> 48 us
  starting transfers between devices: 25.7 us -> 36.5 us
  local copies, waits for them, and re-layouts: 10 us -> 5.31 us
    all_to_all x5 -> x4, waiting for transfers between devices: 68.1 us -> 29.7 us  [swap(): return lax.all_to_all(array, axes, split_axis=0, concat_axis=0, tiled=True)]
    pallas_call x11, Pallas kernels: 62.4 us -> 48 us  [call(): pl.pallas_call(kernel, out_shape=[jax.ShapeDtypeStruct(shape, kind) if pl...]
    ppermute x0 -> x6, waiting for transfers between devices: none -> 14.4 us  [trade(): lax.ppermute(part, axes, [(place, place ^ step) for place in range(4)])]
    ppermute x0 -> x6, starting transfers between devices: none -> 9.59 us  [trade(): lax.ppermute(part, axes, [(place, place ^ step) for place in range(4)])]
    ppermute x3 -> x6, waiting for transfers between devices: 4.36 us -> 0.02 us  [from_other_core(): return lax.ppermute(array, 'c', [(0, 1), (1, 0)])]
    unnamed x13 -> x4, local copies, waits for them, and re-layouts: 7.78 us -> 3.78 us
    reduce_scatter x2 -> x1, waiting for transfers between devices: 0.02 us -> 2.44 us  [per_device(): lax.psum_scatter(column.reshape(3072, WIDTH), 'x', scatter_dimension=0, t...]
    all_to_all x5 -> x4, starting transfers between devices: 24.8 us -> 25.4 us  [swap(): return lax.all_to_all(array, axes, split_axis=0, concat_axis=0, tiled=True)]
  transfers between devices with their start and end apart: 10 -> 17, of which waited for: 6 -> 8; matrix products, arithmetic and copies ran while one was open for 2% -> 2% of each run, Pallas kernels for 14% -> 16%
where the time goes in v2:
time: 172 us; the launch traced here: 171 us
  Pallas kernels  48 us (28%)
  waiting for transfers between devices  46.5 us (27%)
  starting transfers between devices  36.5 us (21%)
  blocking collectives  19.1 us (11%)
  between operations  14.2 us (8%)
  local copies, waits for them, and re-layouts  5.31 us (3%)
    pallas_call x11, Pallas kernels, call(): pl.pallas_call(kernel, out_shape=[jax.ShapeDtypeStruct(shape, kind) if pl...  48 us
    all_to_all x4, waiting for transfers between devices, swap(): return lax.all_to_all(array, axes, split_axis=0, concat_axis=0, tiled=True)  29.7 us
    all_to_all x4, starting transfers between devices, swap(): return lax.all_to_all(array, axes, split_axis=0, concat_axis=0, tiled=True)  25.4 us
    all_to_all x1, blocking collectives, swap(): return lax.all_to_all(array, axes, split_axis=0, concat_axis=0, tiled=True)  19.1 us
    ppermute x6, waiting for transfers between devices, trade(): lax.ppermute(part, axes, [(place, place ^ step) for place in range(4)])  14.4 us
    ppermute x6, starting transfers between devices, trade(): lax.ppermute(part, axes, [(place, place ^ step) for place in range(4)])  9.59 us
    unnamed x4, local copies, waits for them, and re-layouts  3.78 us
  transfers between devices with their start and end apart: 17, of which 8 were waited for; matrix products, arithmetic and copies ran while one was open for 2% of the time, Pallas kernels for 16%

profile of v2, /device:TPU:0, one launch (start us, length us, event | category | flops | bytes accessed | tf_op | source)
XLA Modules:
  0.0 171.4 jit_solution(17161128668671159424)
XLA Ops:
  7.2 1.6 pad_maximum_fusion
  8.7 0.2 copy.16
  8.9 19.1 %all_to_all.25.pack = bf16[16,44,512]{2,1,0:T(8,128)(2,1)S(1)} all-to-all(bf16[16,44,512]{2,1,0:T(8,128)(2,1)S(1)} %bitcast.16), channel_id=1, replica_groups=mesh['x'=4,'h'=2,'y'=4,'l'=2,'c'=2] {'y','l','c'}, dimensions={0} | all-to-all | bytes 1441792 | tf_op jit(solution)/shard_map/all_to_all | solution.py:490
  28.0 6.6 %shard_map.143 = (bf16[32,22,512]{2,1,0:T(8,128)(2,1)}, bf16[352,512]{1,0:T(8,128)(2,1)}, bf16[352,512]{1,0:T(8,128)(2,1)}, bf16[352,1536]{1,0:T(8,128)(2,1)}, bf16[352,512]{1,0:T(8,128)(2,1)}) custom-call(bf16[16,44,512]{2,1,0:T(8,128)(2,1)S(1)} %all_to_all.25.pack, bf16[512,1536]{1,0:T(8,128)(2,1)} %inproj_far.5, bf16[512,512]{1,0:T(8,128)(2,1)} %outproj_far.5), custom_call_target="tpu_custom_call" | custom-call | flops 5000000000 | bytes 65536 | tf_op jit(solution)/shard_map/pallas_call | solution.py:470
  34.6 8.6 %all-to-all-start.1 = ((bf16[32,22,512]{2,1,0:T(8,128)(2,1)}), bf16[32,22,512]{2,1,0:T(8,128)(2,1)S(1)}, u32[]{:S(2)}, u32[]{:S(2)}) async-start(bf16[32,22,512]{2,1,0:T(8,128)(2,1)} %get-tuple-element.45), calls=%async_computation.1 | async-start | bytes 1572864 | tf_op jit(solution)/shard_map/all_to_all | solution.py:490
  43.3 16.7 %all-to-all-done.1.pack = bf16[32,22,512]{2,1,0:T(8,128)(2,1)S(1)} async-done(((bf16[32,22,512]{2,1,0:T(8,128)(2,1)}), bf16[32,22,512]{2,1,0:T(8,128)(2,1)S(1)}, u32[]{:S(2)}, u32[]{:S(2)}) %all-to-all-start.1) | async-done | bytes 720928 | tf_op jit(solution)/shard_map/all_to_all | solution.py:490
  59.9 13.8 %shard_map.144 = (bf16[32,22,512]{2,1,0:T(8,128)(2,1)}, bf16[352,512]{1,0:T(8,128)(2,1)}, bf16[352,512]{1,0:T(8,128)(2,1)}, bf16[352,1536]{1,0:T(8,128)(2,1)}, b...) custom-call(bf16[32,22,512]{2,1,0:T(8,128)(2,1)S(1)} %all-to-all-don, ...), custom_call_target="tpu_custom_call" | custom-call | flops 20000000000 | bytes 65536 | tf_op jit(solution)/shard_map/pallas_call | solution.py:470
  73.7 3.9 %all-to-all-start.2 = ((bf16[32,22,512]{2,1,0:T(8,128)(2,1)}), bf16[32,22,512]{2,1,0:T(8,128)(2,1)S(1)}, u32[]{:S(2)}, u32[]{:S(2)}) async-start(bf16[32,22,512]{2,1,0:T(8,128)(2,1)} %get-tuple-element.46), calls=%async_computation.2 | async-start | bytes 1572864 | tf_op jit(solution)/shard_map/all_to_all | solution.py:490
  77.6 0.0 reduce-scatter.2.cloned.1.call-start
  77.7 0.1 pad_add_fusion.place.core
  77.8 7.4 %shard_map.145 = (bf16[4,4,2,2,48,512]{5,4,3,2,1,0:T(8,128)(2,1)S(1)}, bf16[13,48,512]{2,1,0:T(8,128)(2,1)S(1)}, bf16[13,48,512]{2,1,0:T(8,128)(2,1)S(1)}, bf16[...) custom-call(s32[3]{0:T(128)S(1)} %pad_add_fusion.place.core, ...), custom_call_target="tpu_custom_call" | custom-call | flops 100000000 | bytes 65536 | tf_op jit(solution)/shard_map/pallas_call | solution.py:470
  85.1 0.1 collective-permute-start.1
  85.2 0.5 collective-permute-start.2
  85.7 0.3 collective-permute-start.3
  86.1 0.2 collective-permute-start.4
  86.3 0.3 collective-permute-start.5
  86.6 4.3 %shard_map.146.weights_far = bf16[8,352,352]{2,1,0:T(8,128)(2,1)} custom-call(bf16[352,1536]{1,0:T(8,128)(2,1)} %get-tuple-element.49.packed_far, bf16[4,4,2,2,48,512]{5,4,3,2,1,0:T(8,128)(2,1)S(1)} %get-tuple-element.59.after.mine), custom_call_target="tpu_custom_call" | custom-call | flops 100000000 | bytes 65536 | tf_op jit(solution)/shard_map/pallas_call | solution.py:470
  90.9 0.0 collective-permute-done.1.refs_0_
  90.9 0.0 collective-permute-done.3.refs_2_
  90.9 0.0 collective-permute-done.4.refs_3_
  91.0 1.8 %shard_map.150 = bf16[4,4,2,2,48,512]{5,4,3,2,1,0:T(8,128)(2,1)} custom-call(bf16[4,4,2,2,48,512]{5,4,3,2,1,0:T(8,128)(2,1)S(1)} %get-tuple-element.59.after.mine, bf16[13,48,512]{2,1,0:T(8,128)(2,1)S(1)} %collective-permute-done.1.refs_0_, bf16[13,48,512]{2,1,0:T(8,128)(2,1)S(1)} %collective-permute-done.2.refs_1_, ...), custom_call_target="tpu_custom_call" | custom-call | flops 100000000 | bytes 65536 | tf_op jit(solution)/shard_map/pallas_call | solution.py:470
  92.8 0.0 reduce-scatter.2.cloned.1.call-update
  92.8 0.5 all-to-all-done.2.pack
  93.3 10.1 %shard_map.147 = (bf16[16,44,512]{2,1,0:T(8,128)(2,1)}, bf16[64,16,512]{2,1,0:T(8,128)(2,1)S(1)}, bf16[64,16,512]{2,1,0:T(8,128)(2,1)S(1)}) custom-call(s32[3]{0:T(128)S(1)} %pad_add_fusion.place.core, bf16[32,22,512]{2,1,0:T(8,128)(2,1)S(1)} %all-to-all-done.2.pack, bf16[352,512]{1,0:T(8,128)(2,1)} %get-tuple-element.47.tokens_far, ...), custom_call_target="tpu_custom_call" | custom-call | flops 60000002048 | bytes 65536 | tf_op jit(solution)/shard_map/pallas_call | solution.py:470
  103.5 0.1 collective-permute-start
  103.6 4.4 %all-to-all-start.3 = ((bf16[16,44,512]{2,1,0:T(8,128)(2,1)}), bf16[16,44,512]{2,1,0:T(8,128)(2,1)}, u32[]{:S(2)}, u32[]{:S(2)}) async-start(bf16[16,44,512]{2,1,0:T(8,128)(2,1)} %get-tuple-element.60), calls=%async_computation.3 | async-start | bytes 1572864 | tf_op jit(solution)/shard_map/all_to_all | solution.py:490
  108.0 1.2 shard_map.148
  109.2 12.5 %all-to-all-done.3 = bf16[16,44,512]{2,1,0:T(8,128)(2,1)} async-done(((bf16[16,44,512]{2,1,0:T(8,128)(2,1)}), bf16[16,44,512]{2,1,0:T(8,128)(2,1)}, u32[]{:S(2)}, u32[]{:S(2)}) %all-to-all-start.3) | async-done | bytes 720928 | tf_op jit(solution)/shard_map/all_to_all | solution.py:490
  121.7 8.4 %all-to-all-start.4 = ((bf16[64,16,512]{2,1,0:T(8,128)(2,1)}), bf16[64,16,512]{2,1,0:T(8,128)(2,1)S(1)}, u32[]{:S(2)}, u32[]{:S(2)}) async-start(bf16[64,16,512]{2,1,0:T(8,128)(2,1)} %shard_map.148), calls=%async_computation.4 | async-start | bytes 2097152 | tf_op jit(solution)/shard_map/all_to_all | solution.py:490
  130.1 2.4 %reduce-scatter.2.cloned.1.call-done = bf16[768,512]{1,0:T(8,128)(2,1)} async-done(((bf16[3072,512]{1,0:T(8,128)(2,1)}), bf16[768,512]{1,0:T(8,128)(2,1)}) %reduce-scatter.2.cloned.1.call-update) | async-done | bytes 786448 | tf_op jit(solution)/shard_map/reduce_scatter | solution.py:581
  132.6 1.1 copy-done
  133.7 0.6 shard_map.151
  134.3 1.6 collective-permute-start.6
  135.9 2.7 %collective-permute-start.7 = (bf16[192,512]{1,0:T(8,128)(2,1)S(1)}, bf16[192,512]{1,0:T(8,128)(2,1)S(1)}, u32[]{:S(2)}, u32[]{:S(2)}) collective-permute-start(bf16[192,512]{1,0:T(8,128)(2,1)S(1)} %get-tuple-element.72), channel_id=1, source_target_pairs={{0,8},{4,12},{8,0},{12,4},{1,9},{5,13},{9,1},{13,5},{2,10},{6,14},... | collective-permute-start | bytes 589832 | tf_op jit(solution)/shard_map/ppermute | solution.py:495
  138.6 0.5 collective-permute-start.8
  139.1 1.4 fusion
  140.5 1.3 copy.20
  141.8 1.3 copy.19
  143.1 4.6 %collective-permute-done.6.refs_1_ = bf16[192,512]{1,0:T(8,128)(2,1)S(1)} collective-permute-done((bf16[192,512]{1,0:T(8,128)(2,1)S(1)}, bf16[192,512]{1,0:T(8,128)(2,1)S(1)}, u32[]{:S(2)}, u32[]{:S(2)}) %collective-permute-start.6) | collective-permute-done | bytes 196640 | tf_op jit(solution)/shard_map/ppermute | solution.py:495
  147.7 5.3 %collective-permute-done.7.refs_2_ = bf16[192,512]{1,0:T(8,128)(2,1)S(1)} collective-permute-done((bf16[192,512]{1,0:T(8,128)(2,1)S(1)}, bf16[192,512]{1,0:T(8,128)(2,1)S(1)}, u32[]{:S(2)}, u32[]{:S(2)}) %collective-permute-start.7) | collective-permute-done | bytes 196640 | tf_op jit(solution)/shard_map/ppermute | solution.py:495
  153.0 0.0 collective-permute-done.8.refs_3_
  153.0 0.7 shard_map.152
  153.8 1.7 collective-permute-start.9
  155.4 3.2 %collective-permute-start.10 = (bf16[48,512]{1,0:T(8,128)(2,1)S(1)}, bf16[48,512]{1,0:T(8,128)(2,1)S(1)}, u32[]{:S(2)}, u32[]{:S(2)}) collective-permute-start(bf16[48,512]{1,0:T(8,128)(2,1)S(1)} %get-tuple-element.76), channel_id=1, source_target_pairs={{0,16},{2,18},{16,0},{18,2},{1,17},{3,19},{17,1},{19,3},{4,20},{6,... | collective-permute-start | bytes 147464 | tf_op jit(solution)/shard_map/ppermute | solution.py:495
  158.6 0.8 shard_map.149
  159.4 1.8 %collective-permute-done.10.refs_2_ = bf16[48,512]{1,0:T(8,128)(2,1)S(1)} collective-permute-done((bf16[48,512]{1,0:T(8,128)(2,1)S(1)}, bf16[48,512]{1,0:T(8,128)(2,1)S(1)}, u32[]{:S(2)}, u32[]{:S(2)}) %collective-permute-start.10) | collective-permute-done | bytes 49184 | tf_op jit(solution)/shard_map/ppermute | solution.py:495
  161.2 2.7 %collective-permute-done.11.refs_3_ = bf16[48,512]{1,0:T(8,128)(2,1)S(1)} collective-permute-done((bf16[48,512]{1,0:T(8,128)(2,1)S(1)}, bf16[48,512]{1,0:T(8,128)(2,1)S(1)}, u32[]{:S(2)}, u32[]{:S(2)}) %collective-permute-start.11) | collective-permute-done | bytes 49184 | tf_op jit(solution)/shard_map/ppermute | solution.py:495
  163.9 0.6 shard_map.153
  (7 shorter events, 0.0 us)
Async XLA Ops:
  34.6 25.3 %all-to-all-start.1 = ((bf16[32,22,512]{2,1,0:T(8,128)(2,1)}), bf16[32,22,512]{2,1,0:T(8,128)(2,1)S(1)}, u32[]{:S(2)}, u32[]{:S(2)}) async-start(bf16[32,22,512]{2,1,0:T(8,128)(2,1)} %get-tuple-element.45), calls=%async_computation.1 | async-start | bytes 1572864 | tf_op jit(solution)/shard_map/all_to_all | solution.py:490
  73.7 19.6 %all-to-all-start.2 = ((bf16[32,22,512]{2,1,0:T(8,128)(2,1)}), bf16[32,22,512]{2,1,0:T(8,128)(2,1)S(1)}, u32[]{:S(2)}, u32[]{:S(2)}) async-start(bf16[32,22,512]{2,1,0:T(8,128)(2,1)} %get-tuple-element.46), calls=%async_computation.2 | async-start | bytes 1572864 | tf_op jit(solution)/shard_map/all_to_all | solution.py:490
  77.6 55.0 %reduce-scatter.2.cloned.1.call-start = ((), (), s32[]{:S(2)}) async-start(), calls=%async_computation.6 | async-start | bytes 3932160 | tf_op jit(solution)/shard_map/reduce_scatter | solution.py:581
  85.1 5.8 %collective-permute-start.1 = (bf16[13,48,512]{2,1,0:T(8,128)(2,1)S(1)}, bf16[13,48,512]{2,1,0:T(8,128)(2,1)S(1)}, u32[]{:S(2)}, u32[]{:S(2)}) collective-permute-start(bf16[13,48,512]{2,1,0:T(8,128)(2,1)S(1)} %get-tuple-element.65), channel_id=1, source_target_pairs={{0,1},{1,0},{2,3},{3,2},{4,5},{5,4},{6,7},{7,6},{8,9},{9,8},{10,11... | collective-permute-start | bytes 1916936 | tf_op jit(solution)/shard_map/ppermute | solution.py:503
  85.2 5.7 %collective-permute-start.2 = (bf16[13,48,512]{2,1,0:T(8,128)(2,1)S(1)}, bf16[13,48,512]{2,1,0:T(8,128)(2,1)S(1)}, u32[]{:S(2)}, u32[]{:S(2)}) collective-permute-start(bf16[13,48,512]{2,1,0:T(8,128)(2,1)S(1)} %get-tuple-element.66), channel_id=1, source_target_pairs={{0,1},{1,0},{2,3},{3,2},{4,5},{5,4},{6,7},{7,6},{8,9},{9,8},{10,11... | collective-permute-start | bytes 1916936 | tf_op jit(solution)/shard_map/ppermute | solution.py:503
  85.7 5.2 %collective-permute-start.3 = (bf16[13,48,512]{2,1,0:T(8,128)(2,1)S(1)}, bf16[13,48,512]{2,1,0:T(8,128)(2,1)S(1)}, u32[]{:S(2)}, u32[]{:S(2)}) collective-permute-start(bf16[13,48,512]{2,1,0:T(8,128)(2,1)S(1)} %get-tuple-element.67), channel_id=1, source_target_pairs={{0,1},{1,0},{2,3},{3,2},{4,5},{5,4},{6,7},{7,6},{8,9},{9,8},{10,11... | collective-permute-start | bytes 1916936 | tf_op jit(solution)/shard_map/ppermute | solution.py:503
  86.1 4.9 %collective-permute-start.4 = (bf16[13,48,512]{2,1,0:T(8,128)(2,1)S(1)}, bf16[13,48,512]{2,1,0:T(8,128)(2,1)S(1)}, u32[]{:S(2)}, u32[]{:S(2)}) collective-permute-start(bf16[13,48,512]{2,1,0:T(8,128)(2,1)S(1)} %get-tuple-element.68), channel_id=1, source_target_pairs={{0,1},{1,0},{2,3},{3,2},{4,5},{5,4},{6,7},{7,6},{8,9},{9,8},{10,11... | collective-permute-start | bytes 1916936 | tf_op jit(solution)/shard_map/ppermute | solution.py:503
  86.3 4.7 %collective-permute-start.5 = (bf16[13,48,512]{2,1,0:T(8,128)(2,1)S(1)}, bf16[13,48,512]{2,1,0:T(8,128)(2,1)S(1)}, u32[]{:S(2)}, u32[]{:S(2)}) collective-permute-start(bf16[13,48,512]{2,1,0:T(8,128)(2,1)S(1)} %get-tuple-element.69), channel_id=1, source_target_pairs={{0,1},{1,0},{2,3},{3,2},{4,5},{5,4},{6,7},{7,6},{8,9},{9,8},{10,11... | collective-permute-start | bytes 1916936 | tf_op jit(solution)/shard_map/ppermute | solution.py:503
  103.5 4.5 %collective-permute-start = (bf16[64,16,512]{2,1,0:T(8,128)(2,1)S(1)}, bf16[64,16,512]{2,1,0:T(8,128)(2,1)S(1)}, u32[]{:S(2)}, u32[]{:S(2)}) collective-permute-start(bf16[64,16,512]{2,1,0:T(8,128)(2,1)S(1)} %get-tuple-element.62), channel_id=1, source_target_pairs={{0,1},{1,0},{2,3},{3,2},{4,5},{5,4},{6,7},{7,6},{8,9},{9,8},{10,11... | collective-permute-start | bytes 3145736 | tf_op jit(solution)/shard_map/ppermute | solution.py:503
  103.6 18.2 %all-to-all-start.3 = ((bf16[16,44,512]{2,1,0:T(8,128)(2,1)}), bf16[16,44,512]{2,1,0:T(8,128)(2,1)}, u32[]{:S(2)}, u32[]{:S(2)}) async-start(bf16[16,44,512]{2,1,0:T(8,128)(2,1)} %get-tuple-element.60), calls=%async_computation.3 | async-start | bytes 1572864 | tf_op jit(solution)/shard_map/all_to_all | solution.py:490
  121.7 36.9 %all-to-all-start.4 = ((bf16[64,16,512]{2,1,0:T(8,128)(2,1)}), bf16[64,16,512]{2,1,0:T(8,128)(2,1)S(1)}, u32[]{:S(2)}, u32[]{:S(2)}) async-start(bf16[64,16,512]{2,1,0:T(8,128)(2,1)} %shard_map.148), calls=%async_computation.4 | async-start | bytes 2097152 | tf_op jit(solution)/shard_map/all_to_all | solution.py:490
  132.6 1.1 copy-start
  134.3 13.4 %collective-permute-start.6 = (bf16[192,512]{1,0:T(8,128)(2,1)S(1)}, bf16[192,512]{1,0:T(8,128)(2,1)S(1)}, u32[]{:S(2)}, u32[]{:S(2)}) collective-permute-start(bf16[192,512]{1,0:T(8,128)(2,1)S(1)} %get-tuple-element.71), channel_id=1, source_target_pairs={{0,4},{4,0},{8,12},{12,8},{1,5},{5,1},{9,13},{13,9},{2,6},{6,2},{1... | collective-permute-start | bytes 589832 | tf_op jit(solution)/shard_map/ppermute | solution.py:495
  135.9 17.1 %collective-permute-start.7 = (bf16[192,512]{1,0:T(8,128)(2,1)S(1)}, bf16[192,512]{1,0:T(8,128)(2,1)S(1)}, u32[]{:S(2)}, u32[]{:S(2)}) collective-permute-start(bf16[192,512]{1,0:T(8,128)(2,1)S(1)} %get-tuple-element.72), channel_id=1, source_target_pairs={{0,8},{4,12},{8,0},{12,4},{1,9},{5,13},{9,1},{13,5},{2,10},{6,14},... | collective-permute-start | bytes 589832 | tf_op jit(solution)/shard_map/ppermute | solution.py:495
  138.6 14.4 %collective-permute-start.8 = (bf16[192,512]{1,0:T(8,128)(2,1)S(1)}, bf16[192,512]{1,0:T(8,128)(2,1)S(1)}, u32[]{:S(2)}, u32[]{:S(2)}) collective-permute-start(bf16[192,512]{1,0:T(8,128)(2,1)S(1)} %get-tuple-element.73), channel_id=1, source_target_pairs={{0,12},{4,8},{8,4},{12,0},{1,13},{5,9},{9,5},{13,1},{2,14},{6,10},... | collective-permute-start | bytes 589832 | tf_op jit(solution)/shard_map/ppermute | solution.py:495
  153.8 5.6 %collective-permute-start.9 = (bf16[48,512]{1,0:T(8,128)(2,1)S(1)}, bf16[48,512]{1,0:T(8,128)(2,1)S(1)}, u32[]{:S(2)}, u32[]{:S(2)}) collective-permute-start(bf16[48,512]{1,0:T(8,128)(2,1)S(1)} %get-tuple-element.75), channel_id=1, source_target_pairs={{0,2},{2,0},{16,18},{18,16},{1,3},{3,1},{17,19},{19,17},{4,6},{6,4... | collective-permute-start | bytes 147464 | tf_op jit(solution)/shard_map/ppermute | solution.py:495
  155.4 5.7 %collective-permute-start.10 = (bf16[48,512]{1,0:T(8,128)(2,1)S(1)}, bf16[48,512]{1,0:T(8,128)(2,1)S(1)}, u32[]{:S(2)}, u32[]{:S(2)}) collective-permute-start(bf16[48,512]{1,0:T(8,128)(2,1)S(1)} %get-tuple-element.76), channel_id=1, source_target_pairs={{0,16},{2,18},{16,0},{18,2},{1,17},{3,19},{17,1},{19,3},{4,20},{6,... | collective-permute-start | bytes 147464 | tf_op jit(solution)/shard_map/ppermute | solution.py:495
  158.6 5.3 %collective-permute-start.11 = (bf16[48,512]{1,0:T(8,128)(2,1)S(1)}, bf16[48,512]{1,0:T(8,128)(2,1)S(1)}, u32[]{:S(2)}, u32[]{:S(2)}) collective-permute-start(bf16[48,512]{1,0:T(8,128)(2,1)S(1)} %get-tuple-element.77), channel_id=1, source_target_pairs={{0,18},{2,16},{16,2},{18,0},{1,19},{3,17},{17,3},{19,1},{4,22},{6,... | collective-permute-start | bytes 147464 | tf_op jit(solution)/shard_map/ppermute | solution.py:495
Sparse Core Ops, SparseCore 0:
  93.0 39.5 reduce-scatter.1

commit v3 on v2

--- a/solution.py
+++ b/solution.py
@@ -17,7 +17,7 @@
 PART = 11
 PIECE = 13
 LON = ("y", "l", "c")
-TURN = ("y", "x", "h")
+TURN = ("h", "x", "y")
 CHIPS = ("x", "h", "y", "l")
 UNROLL = HEADS // 2
 BLOCKS = ((0, 128), (128, 128), (256, 96))
@@ -276,48 +276,45 @@
     split_terms(core, grads, normed, low, mixed, mine, other)
 
 
-def to_columns(pack, first, second):
+def to_columns(pack, columns):
     for lat in range(LATS):
         piece = pack[lat].astype(f32)
         for tile in range(4):
             lanes = slice(tile * 128, (tile + 1) * 128)
-            first[tile, pl.ds(lat, PART, stride=LATS), :] = piece[:PART, lanes]
-            second[tile, pl.ds(lat, PART, stride=LATS), :] = piece[PART:, lanes]
-
-
-def joined(tiles):
-    return jnp.concatenate([tiles[tile] for tile in range(4)], axis=1)
-
-
-def put_tiles(tiles, values):
+            columns[tile, pl.ds(lat, 2 * PART, stride=LATS), :] = piece[:, lanes]
+
+
+def joined(columns, unit):
+    rows = pl.ds(unit * ROWS, ROWS)
+    return jnp.concatenate([columns[tile, rows, :] for tile in range(4)], axis=1)
+
+
+def put_columns(columns, unit, values):
     for tile in range(4):
-        tiles[tile] = values[:, tile * 128 : (tile + 1) * 128]
-
-
-def from_columns(out, first, second):
+        columns[tile, pl.ds(unit * ROWS, ROWS), :] = values[:, tile * 128 : (tile + 1) * 128]
+
+
+def from_columns(out, columns):
     for lat in range(LATS):
-        rows = pl.ds(lat, PART, stride=LATS)
-        parts = [
-            jnp.concatenate([tiles[tile, rows, :] for tile in range(4)], axis=1)
-            for tiles in (first, second)
-        ]
-        out[lat] = jnp.concatenate(parts, axis=0).astype(bf16)
+        rows = pl.ds(lat, 2 * PART, stride=LATS)
+        piece = jnp.concatenate([columns[tile, rows, :] for tile in range(4)], axis=1)
+        out[lat] = piece.astype(bf16)
 
 
 def column_both(
     pack, inproj_far, outproj_far, mlp_in_far, mlp_out_far,
     out, normed_far, mixed_far, grads_far, low_far, normed_mlp_far, activated_far, grad_inner_far, cotangent_far,
     inproj, outproj, mlp_in, mlp_out, normed, mixed, grads, low, normed_mlp, activated, grad_inner, cotangent,
-    packed, upstream, first, second, turned, hidden_one, hidden, grad_normed, output, probs, grad_scores,
+    packed, upstream, columns, turned, hidden_one, hidden, grad_normed, output, probs, grad_scores,
     semaphores,
 ):
     mover = Mover(semaphores)
     inproj_in = mover.start(inproj_far, inproj)
     outproj_in = mover.start(outproj_far, outproj)
     coming = [mover.start(mlp_in_far, mlp_in), mover.start(mlp_out_far, mlp_out)]
-    to_columns(pack, first, second)
-    hidden_one[...] = joined(first)
-    cotangent[...] = joined(second).astype(bf16)
+    to_columns(pack, columns)
+    hidden_one[...] = joined(columns, 0)
+    cotangent[...] = joined(columns, 1).astype(bf16)
     normed[...] = normalize(hidden_one[...])[0].astype(bf16)
     leaving = [mover.start(cotangent, cotangent_far), mover.start(normed, normed_far)]
     inproj_in.wait()
@@ -335,22 +332,22 @@
         copy.wait()
 
     def one_chunk(chunk, _):
-        columns = pl.ds(pl.multiple_of(chunk * 512, 512), 512)
-        inner = dot(normed_mlp[...], mlp_in[:, columns])
+        chosen = pl.ds(pl.multiple_of(chunk * 512, 512), 512)
+        inner = dot(normed_mlp[...], mlp_in[:, chosen])
         spread = 0.5 * (1.0 + lax.erf(inner * 2.0**-0.5))
         slope = spread + inner * (0.5 / jnp.pi) ** 0.5 * jnp.exp(-0.5 * inner * inner)
         active = (inner * spread).astype(bf16)
-        activated[:, columns] = active
-        output[...] += dot(active, mlp_out[columns, :])
-        grad = (dot(cotangent[...], mlp_out[columns, :], 1, 1) * slope).astype(bf16)
-        grad_inner[:, columns] = grad
-        grad_normed[...] += dot(grad, mlp_in[:, columns], 1, 1)
+        activated[:, chosen] = active
+        output[...] += dot(active, mlp_out[chosen, :])
+        grad = (dot(cotangent[...], mlp_out[chosen, :], 1, 1) * slope).astype(bf16)
+        grad_inner[:, chosen] = grad
+        grad_normed[...] += dot(grad, mlp_in[:, chosen], 1, 1)
         return 0
 
-    lax.fori_loop(0, FF // 512, one_chunk, 0, unroll=2)
+    lax.fori_loop(0, FF // 512, one_chunk, 0, unroll=4)
     leaving.append(mover.start(activated, activated_far))
     leaving.append(mover.start(grad_inner, grad_inner_far))
-    put_tiles(second, output[...])
+    put_columns(columns, 1, output[...])
     back = norm_back(*normalize(hidden[...]), grad_normed[...])
     hidden[...] = cotangent[...].astype(f32) + back
     low[...] = hidden[...].astype(bf16)
@@ -359,8 +356,8 @@
     attend_columns_back(packed, upstream, probs, grad_scores, grads)
     leaving.append(mover.start(grads, grads_far))
     back = norm_back(*normalize(hidden_one[...]), dot(grads[...], inproj[...], 1, 1))
-    put_tiles(first, hidden[...] + back)
-    from_columns(out, first, second)
+    put_columns(columns, 0, hidden[...] + back)
+    from_columns(out, columns)
     for copy in leaving:
         copy.wait()
 
@@ -371,29 +368,38 @@
     return [wide.reshape(32, 12, WIDTH), slim.reshape(32, 4, WIDTH)]
 
 
+def put_terms(place, terms, block, rows, mine, others):
+    both = jnp.concatenate(terms, axis=1).astype(bf16)
+    both = both.reshape(2, 4, 2, 2, both.shape[1], WIDTH)
+    for high in range(2):
+        even, odd = both[high, :, :, 0], both[high, :, :, 1]
+        mine[block, :, high, :, rows, :] = jnp.where(place[0] == 0, even, odd)
+        leaving = jnp.where(place[0] == 0, odd, even)
+        for row in range(4):
+            for low_z in range(2):
+                piece, chip = divmod(16 * block + 4 * row + 2 * high + low_z, PIECE)
+                others[piece][chip, rows, :] = leaving[row, low_z]
+
+
 def column_terms(place, *refs):
     far, mine, others, near, semaphores = refs[:8], refs[8], refs[9:14], refs[14:22], refs[22]
     mover = Mover(semaphores)
     coming = [mover.start(source, target) for source, target in zip(far, near)]
-    normed_mlp, activated, grad_inner, cotangent, grads, normed, low, mixed = near
-    for copy in coming:
+    grads, normed, low, mixed, normed_mlp, grad_inner, activated, cotangent = near
+    for copy in coming[:4]:
         copy.wait()
     for block in range(4):
         terms = block_terms(block, grads, normed, low, mixed)
+        put_terms(place, terms, block, pl.ds(0, 16), mine, others)
+    for copy in coming[4:]:
+        copy.wait()
+    for block in range(4):
         inner = dot(grad_inner[:, block * 512 : (block + 1) * 512], normed_mlp[...], 0, 0)
         outer = dot(cotangent[:, block * 128 : (block + 1) * 128], activated[...], 0, 0)
-        terms.append(inner.reshape(32, 16, WIDTH))
+        terms = [inner.reshape(32, 16, WIDTH)]
         for part in range(4):
             terms.append(outer[:, part * WIDTH : (part + 1) * WIDTH].reshape(32, 4, WIDTH))
-        both = jnp.concatenate(terms, axis=1).astype(bf16).reshape(2, 4, 2, 2, 48, WIDTH)
-        for high in range(2):
-            even, odd = both[high, :, :, 0], both[high, :, :, 1]
-            mine[block, :, high] = jnp.where(place[0] == 0, even, odd)
-            leaving = jnp.where(place[0] == 0, odd, even)
-            for row in range(4):
-                for low_z in range(2):
-                    piece, chip = divmod(16 * block + 4 * row + 2 * high + low_z, PIECE)
-                    others[piece][chip] = leaving[row, low_z]
+        put_terms(place, terms, block, pl.ds(16, 32), mine, others)
 
 
 def split_terms(place, grads, normed, low, mixed, mine, other):
@@ -506,7 +512,7 @@
 NARROW = (ROWS, WIDTH)
 QKV = (ROWS, 3 * WIDTH)
 WIDE = (ROWS, FF)
-TILES = (4, ROWS, 128)
+TILES = (4, 2 * ROWS, 128)
 TURNED = (WIDTH, ROWS)
 TO_TURN = (LATS, 2 * PART, WIDTH)
 TO_LON = (16, 2 * NEAR, WIDTH)
@@ -546,16 +552,16 @@
         [(swap(pack, TURN), VMEM)] + all_far(inproj_lat, outproj_lat, mlp_in, mlp_out),
         [(TO_TURN, bf16, VMEM)] + far(NARROW, NARROW, QKV, NARROW, NARROW, WIDE, WIDE, NARROW),
         low(IN, OUT, MLP_IN, MLP_OUT, NARROW, NARROW, QKV, NARROW, NARROW, WIDE, WIDE, NARROW, QKV, NARROW)
-        + [(TILES, f32), (TILES, f32), (TURNED, f32)] + [(NARROW, f32)] * 4 + [(LAT_PROBS, f32)] * 2,
+        + [(TILES, f32), (TURNED, f32)] + [(NARROW, f32)] * 4 + [(LAT_PROBS, f32)] * 2,
         12,
         36,
         20.0,
     )
     mine, *others = call(
         column_terms,
-        [(core, SMEM)] + all_far(*saved, grads, normed, upstream, mixed),
+        [(core, SMEM)] + all_far(grads, normed, upstream, mixed, *(saved[i] for i in (0, 2, 1, 3))),
         [(BY_CHIP, bf16, VMEM)] + [((PIECE, 48, WIDTH), bf16, VMEM)] * 5,
-        low(NARROW, WIDE, WIDE, NARROW, QKV, NARROW, NARROW, NARROW),
+        low(QKV, NARROW, NARROW, NARROW, NARROW, WIDE, WIDE, NARROW),
         8,
         32,
         0.1,

time: 172 us -> 170 us (0.988)
  transfers between devices with their start and end apart: 17 -> 17, of which waited for: 8 -> 8; matrix products, arithmetic and copies ran while one was open for 2% -> 2% of each run, Pallas kernels for 16% -> 15%
where the time goes in v3:
time: 170 us; the launch traced here: 169 us
  Pallas kernels  46.3 us (27%)
  waiting for transfers between devices  45.3 us (27%)
  starting transfers between devices  37.5 us (22%)
  blocking collectives  19.1 us (11%)
  between operations  14.2 us (8%)
  local copies, waits for them, and re-layouts  5.31 us (3%)
    pallas_call x11, Pallas kernels, call(): pl.pallas_call(kernel, out_shape=[jax.ShapeDtypeStruct(shape, kind) if pl...  46.3 us
    all_to_all x4, waiting for transfers between devices, swap(): return lax.all_to_all(array, axes, split_axis=0, concat_axis=0, tiled=True)  28.3 us
    all_to_all x4, starting transfers between devices, swap(): return lax.all_to_all(array, axes, split_axis=0, concat_axis=0, tiled=True)  26.2 us
    all_to_all x1, blocking collectives, swap(): return lax.all_to_all(array, axes, split_axis=0, concat_axis=0, tiled=True)  19.1 us
    ppermute x6, waiting for transfers between devices, trade(): lax.ppermute(part, axes, [(place, place ^ step) for place in range(4)])  14.4 us
    ppermute x6, starting transfers between devices, trade(): lax.ppermute(part, axes, [(place, place ^ step) for place in range(4)])  9.59 us
    unnamed x4, local copies, waits for them, and re-layouts  3.78 us
  transfers between devices with their start and end apart: 17, of which 8 were waited for; matrix products, arithmetic and copies ran while one was open for 2% of the time, Pallas kernels for 15%

profile of v3, /device:TPU:0, one launch (start us, length us, event | category | flops | bytes accessed | tf_op | source)
XLA Modules:
  0.0 169.5 jit_solution(17134067298237546056)
XLA Ops:
  7.2 1.6 pad_maximum_fusion
  8.7 0.2 copy.16
  8.9 19.1 %all_to_all.25.pack = bf16[16,44,512]{2,1,0:T(8,128)(2,1)S(1)} all-to-all(bf16[16,44,512]{2,1,0:T(8,128)(2,1)S(1)} %bitcast.16), channel_id=1, replica_groups=mesh['x'=4,'h'=2,'y'=4,'l'=2,'c'=2] {'y','l','c'}, dimensions={0} | all-to-all | bytes 1441792 | tf_op jit(solution)/shard_map/all_to_all | solution.py:496
  28.0 6.6 %shard_map.143 = (bf16[32,22,512]{2,1,0:T(8,128)(2,1)}, bf16[352,512]{1,0:T(8,128)(2,1)}, bf16[352,512]{1,0:T(8,128)(2,1)}, bf16[352,1536]{1,0:T(8,128)(2,1)}, bf16[352,512]{1,0:T(8,128)(2,1)}) custom-call(bf16[16,44,512]{2,1,0:T(8,128)(2,1)S(1)} %all_to_all.25.pack, bf16[512,1536]{1,0:T(8,128)(2,1)} %inproj_far.5, bf16[512,512]{1,0:T(8,128)(2,1)} %outproj_far.5), custom_call_target="tpu_custom_call" | custom-call | flops 5000000000 | bytes 65536 | tf_op jit(solution)/shard_map/pallas_call | solution.py:476
  34.6 8.6 %all-to-all-start.1 = ((bf16[32,22,512]{2,1,0:T(8,128)(2,1)}), bf16[32,22,512]{2,1,0:T(8,128)(2,1)S(1)}, u32[]{:S(2)}, u32[]{:S(2)}) async-start(bf16[32,22,512]{2,1,0:T(8,128)(2,1)} %get-tuple-element.45), calls=%async_computation.1 | async-start | bytes 1572864 | tf_op jit(solution)/shard_map/all_to_all | solution.py:496
  43.3 15.7 %all-to-all-done.1.pack = bf16[32,22,512]{2,1,0:T(8,128)(2,1)S(1)} async-done(((bf16[32,22,512]{2,1,0:T(8,128)(2,1)}), bf16[32,22,512]{2,1,0:T(8,128)(2,1)S(1)}, u32[]{:S(2)}, u32[]{:S(2)}) %all-to-all-start.1) | async-done | bytes 720928 | tf_op jit(solution)/shard_map/all_to_all | solution.py:496
  59.0 13.0 %shard_map.144 = (bf16[32,22,512]{2,1,0:T(8,128)(2,1)}, bf16[352,512]{1,0:T(8,128)(2,1)}, bf16[352,512]{1,0:T(8,128)(2,1)}, bf16[352,1536]{1,0:T(8,128)(2,1)}, b...) custom-call(bf16[32,22,512]{2,1,0:T(8,128)(2,1)S(1)} %all-to-all-don, ...), custom_call_target="tpu_custom_call" | custom-call | flops 20000000000 | bytes 65536 | tf_op jit(solution)/shard_map/pallas_call | solution.py:476
  72.0 4.4 %all-to-all-start.2 = ((bf16[32,22,512]{2,1,0:T(8,128)(2,1)}), bf16[32,22,512]{2,1,0:T(8,128)(2,1)S(1)}, u32[]{:S(2)}, u32[]{:S(2)}) async-start(bf16[32,22,512]{2,1,0:T(8,128)(2,1)} %get-tuple-element.46), calls=%async_computation.2 | async-start | bytes 1572864 | tf_op jit(solution)/shard_map/all_to_all | solution.py:496
  76.4 0.3 reduce-scatter.2.cloned.1.call-start
  76.7 0.1 pad_add_fusion.place.core
  76.7 6.5 %shard_map.145 = (bf16[4,4,2,2,48,512]{5,4,3,2,1,0:T(8,128)(2,1)S(1)}, bf16[13,48,512]{2,1,0:T(8,128)(2,1)S(1)}, bf16[13,48,512]{2,1,0:T(8,128)(2,1)S(1)}, bf16[...) custom-call(s32[3]{0:T(128)S(1)} %pad_add_fusion.place.core, ...), custom_call_target="tpu_custom_call" | custom-call | flops 100000000 | bytes 65536 | tf_op jit(solution)/shard_map/pallas_call | solution.py:476
  83.2 0.1 collective-permute-start.1
  83.3 0.5 collective-permute-start.2
  83.8 0.1 collective-permute-start.3
  83.9 0.4 collective-permute-start.4
  84.3 0.1 collective-permute-start.5
  84.4 4.3 %shard_map.146.weights_far = bf16[8,352,352]{2,1,0:T(8,128)(2,1)} custom-call(bf16[352,1536]{1,0:T(8,128)(2,1)} %get-tuple-element.49.packed_far, bf16[4,4,2,2,48,512]{5,4,3,2,1,0:T(8,128)(2,1)S(1)} %get-tuple-element.59.after.mine), custom_call_target="tpu_custom_call" | custom-call | flops 100000000 | bytes 65536 | tf_op jit(solution)/shard_map/pallas_call | solution.py:476
  88.8 0.0 collective-permute-done.1.refs_0_
  88.8 0.0 collective-permute-done.2.refs_1_
  88.8 0.0 collective-permute-done.4.refs_3_
  88.8 0.2 collective-permute-done.5.refs_4_
  89.0 1.8 %shard_map.150 = bf16[4,4,2,2,48,512]{5,4,3,2,1,0:T(8,128)(2,1)} custom-call(bf16[4,4,2,2,48,512]{5,4,3,2,1,0:T(8,128)(2,1)S(1)} %get-tuple-element.59.after.mine, bf16[13,48,512]{2,1,0:T(8,128)(2,1)S(1)} %collective-permute-done.1.refs_0_, bf16[13,48,512]{2,1,0:T(8,128)(2,1)S(1)} %collective-permute-done.2.refs_1_, ...), custom_call_target="tpu_custom_call" | custom-call | flops 100000000 | bytes 65536 | tf_op jit(solution)/shard_map/pallas_call | solution.py:476
  90.9 0.0 reduce-scatter.2.cloned.1.call-update
  90.9 10.1 %shard_map.147 = (bf16[16,44,512]{2,1,0:T(8,128)(2,1)}, bf16[64,16,512]{2,1,0:T(8,128)(2,1)S(1)}, bf16[64,16,512]{2,1,0:T(8,128)(2,1)S(1)}) custom-call(s32[3]{0:T(128)S(1)} %pad_add_fusion.place.core, bf16[32,22,512]{2,1,0:T(8,128)(2,1)S(1)} %all-to-all-done.2.pack, bf16[352,512]{1,0:T(8,128)(2,1)} %get-tuple-element.47.tokens_far, ...), custom_call_target="tpu_custom_call" | custom-call | flops 60000002048 | bytes 65536 | tf_op jit(solution)/shard_map/pallas_call | solution.py:476
  101.0 0.3 collective-permute-start
  101.3 4.7 %all-to-all-start.3 = ((bf16[16,44,512]{2,1,0:T(8,128)(2,1)}), bf16[16,44,512]{2,1,0:T(8,128)(2,1)}, u32[]{:S(2)}, u32[]{:S(2)}) async-start(bf16[16,44,512]{2,1,0:T(8,128)(2,1)} %get-tuple-element.60), calls=%async_computation.3 | async-start | bytes 1572864 | tf_op jit(solution)/shard_map/all_to_all | solution.py:496
  106.1 1.2 shard_map.148
  107.3 12.5 %all-to-all-done.3 = bf16[16,44,512]{2,1,0:T(8,128)(2,1)} async-done(((bf16[16,44,512]{2,1,0:T(8,128)(2,1)}), bf16[16,44,512]{2,1,0:T(8,128)(2,1)}, u32[]{:S(2)}, u32[]{:S(2)}) %all-to-all-start.3) | async-done | bytes 720928 | tf_op jit(solution)/shard_map/all_to_all | solution.py:496
  119.8 8.4 %all-to-all-start.4 = ((bf16[64,16,512]{2,1,0:T(8,128)(2,1)}), bf16[64,16,512]{2,1,0:T(8,128)(2,1)S(1)}, u32[]{:S(2)}, u32[]{:S(2)}) async-start(bf16[64,16,512]{2,1,0:T(8,128)(2,1)} %shard_map.148), calls=%async_computation.4 | async-start | bytes 2097152 | tf_op jit(solution)/shard_map/all_to_all | solution.py:496
  128.2 2.5 %reduce-scatter.2.cloned.1.call-done = bf16[768,512]{1,0:T(8,128)(2,1)} async-done(((bf16[3072,512]{1,0:T(8,128)(2,1)}), bf16[768,512]{1,0:T(8,128)(2,1)}) %reduce-scatter.2.cloned.1.call-update) | async-done | bytes 786448 | tf_op jit(solution)/shard_map/reduce_scatter | solution.py:587
  130.7 1.1 copy-done
  131.8 0.6 shard_map.151
  132.4 1.5 collective-permute-start.6
  134.0 2.7 %collective-permute-start.7 = (bf16[192,512]{1,0:T(8,128)(2,1)S(1)}, bf16[192,512]{1,0:T(8,128)(2,1)S(1)}, u32[]{:S(2)}, u32[]{:S(2)}) collective-permute-start(bf16[192,512]{1,0:T(8,128)(2,1)S(1)} %get-tuple-element.72), channel_id=1, source_target_pairs={{0,8},{4,12},{8,0},{12,4},{1,9},{5,13},{9,1},{13,5},{2,10},{6,14},... | collective-permute-start | bytes 589832 | tf_op jit(solution)/shard_map/ppermute | solution.py:501
  136.7 0.5 collective-permute-start.8
  137.2 1.4 fusion
  138.6 1.3 copy.20
  139.9 1.3 copy.19
  141.3 4.6 %collective-permute-done.6.refs_1_ = bf16[192,512]{1,0:T(8,128)(2,1)S(1)} collective-permute-done((bf16[192,512]{1,0:T(8,128)(2,1)S(1)}, bf16[192,512]{1,0:T(8,128)(2,1)S(1)}, u32[]{:S(2)}, u32[]{:S(2)}) %collective-permute-start.6) | collective-permute-done | bytes 196640 | tf_op jit(solution)/shard_map/ppermute | solution.py:501
  145.8 5.3 %collective-permute-done.7.refs_2_ = bf16[192,512]{1,0:T(8,128)(2,1)S(1)} collective-permute-done((bf16[192,512]{1,0:T(8,128)(2,1)S(1)}, bf16[192,512]{1,0:T(8,128)(2,1)S(1)}, u32[]{:S(2)}, u32[]{:S(2)}) %collective-permute-start.7) | collective-permute-done | bytes 196640 | tf_op jit(solution)/shard_map/ppermute | solution.py:501
  151.1 0.0 collective-permute-done.8.refs_3_
  151.1 0.7 shard_map.152
  151.9 1.7 collective-permute-start.9
  153.5 3.2 %collective-permute-start.10 = (bf16[48,512]{1,0:T(8,128)(2,1)S(1)}, bf16[48,512]{1,0:T(8,128)(2,1)S(1)}, u32[]{:S(2)}, u32[]{:S(2)}) collective-permute-start(bf16[48,512]{1,0:T(8,128)(2,1)S(1)} %get-tuple-element.76), channel_id=1, source_target_pairs={{0,16},{2,18},{16,0},{18,2},{1,17},{3,19},{17,1},{19,3},{4,20},{6,... | collective-permute-start | bytes 147464 | tf_op jit(solution)/shard_map/ppermute | solution.py:501
  156.7 0.8 shard_map.149
  157.5 1.8 %collective-permute-done.10.refs_2_ = bf16[48,512]{1,0:T(8,128)(2,1)S(1)} collective-permute-done((bf16[48,512]{1,0:T(8,128)(2,1)S(1)}, bf16[48,512]{1,0:T(8,128)(2,1)S(1)}, u32[]{:S(2)}, u32[]{:S(2)}) %collective-permute-start.10) | collective-permute-done | bytes 49184 | tf_op jit(solution)/shard_map/ppermute | solution.py:501
  159.3 2.7 %collective-permute-done.11.refs_3_ = bf16[48,512]{1,0:T(8,128)(2,1)S(1)} collective-permute-done((bf16[48,512]{1,0:T(8,128)(2,1)S(1)}, bf16[48,512]{1,0:T(8,128)(2,1)S(1)}, u32[]{:S(2)}, u32[]{:S(2)}) %collective-permute-start.11) | collective-permute-done | bytes 49184 | tf_op jit(solution)/shard_map/ppermute | solution.py:501
  162.0 0.6 shard_map.153
  (7 shorter events, 0.0 us)
Async XLA Ops:
  34.6 24.4 %all-to-all-start.1 = ((bf16[32,22,512]{2,1,0:T(8,128)(2,1)}), bf16[32,22,512]{2,1,0:T(8,128)(2,1)S(1)}, u32[]{:S(2)}, u32[]{:S(2)}) async-start(bf16[32,22,512]{2,1,0:T(8,128)(2,1)} %get-tuple-element.45), calls=%async_computation.1 | async-start | bytes 1572864 | tf_op jit(solution)/shard_map/all_to_all | solution.py:496
  72.0 18.9 %all-to-all-start.2 = ((bf16[32,22,512]{2,1,0:T(8,128)(2,1)}), bf16[32,22,512]{2,1,0:T(8,128)(2,1)S(1)}, u32[]{:S(2)}, u32[]{:S(2)}) async-start(bf16[32,22,512]{2,1,0:T(8,128)(2,1)} %get-tuple-element.46), calls=%async_computation.2 | async-start | bytes 1572864 | tf_op jit(solution)/shard_map/all_to_all | solution.py:496
  76.4 54.3 %reduce-scatter.2.cloned.1.call-start = ((), (), s32[]{:S(2)}) async-start(), calls=%async_computation.6 | async-start | bytes 3932160 | tf_op jit(solution)/shard_map/reduce_scatter | solution.py:587
  83.2 5.6 %collective-permute-start.1 = (bf16[13,48,512]{2,1,0:T(8,128)(2,1)S(1)}, bf16[13,48,512]{2,1,0:T(8,128)(2,1)S(1)}, u32[]{:S(2)}, u32[]{:S(2)}) collective-permute-start(bf16[13,48,512]{2,1,0:T(8,128)(2,1)S(1)} %get-tuple-element.65), channel_id=1, source_target_pairs={{0,1},{1,0},{2,3},{3,2},{4,5},{5,4},{6,7},{7,6},{8,9},{9,8},{10,11... | collective-permute-start | bytes 1916936 | tf_op jit(solution)/shard_map/ppermute | solution.py:509
  83.3 5.5 %collective-permute-start.2 = (bf16[13,48,512]{2,1,0:T(8,128)(2,1)S(1)}, bf16[13,48,512]{2,1,0:T(8,128)(2,1)S(1)}, u32[]{:S(2)}, u32[]{:S(2)}) collective-permute-start(bf16[13,48,512]{2,1,0:T(8,128)(2,1)S(1)} %get-tuple-element.66), channel_id=1, source_target_pairs={{0,1},{1,0},{2,3},{3,2},{4,5},{5,4},{6,7},{7,6},{8,9},{9,8},{10,11... | collective-permute-start | bytes 1916936 | tf_op jit(solution)/shard_map/ppermute | solution.py:509
  83.8 5.0 %collective-permute-start.3 = (bf16[13,48,512]{2,1,0:T(8,128)(2,1)S(1)}, bf16[13,48,512]{2,1,0:T(8,128)(2,1)S(1)}, u32[]{:S(2)}, u32[]{:S(2)}) collective-permute-start(bf16[13,48,512]{2,1,0:T(8,128)(2,1)S(1)} %get-tuple-element.67), channel_id=1, source_target_pairs={{0,1},{1,0},{2,3},{3,2},{4,5},{5,4},{6,7},{7,6},{8,9},{9,8},{10,11... | collective-permute-start | bytes 1916936 | tf_op jit(solution)/shard_map/ppermute | solution.py:509
  83.9 4.9 %collective-permute-start.4 = (bf16[13,48,512]{2,1,0:T(8,128)(2,1)S(1)}, bf16[13,48,512]{2,1,0:T(8,128)(2,1)S(1)}, u32[]{:S(2)}, u32[]{:S(2)}) collective-permute-start(bf16[13,48,512]{2,1,0:T(8,128)(2,1)S(1)} %get-tuple-element.68), channel_id=1, source_target_pairs={{0,1},{1,0},{2,3},{3,2},{4,5},{5,4},{6,7},{7,6},{8,9},{9,8},{10,11... | collective-permute-start | bytes 1916936 | tf_op jit(solution)/shard_map/ppermute | solution.py:509
  84.3 4.7 %collective-permute-start.5 = (bf16[13,48,512]{2,1,0:T(8,128)(2,1)S(1)}, bf16[13,48,512]{2,1,0:T(8,128)(2,1)S(1)}, u32[]{:S(2)}, u32[]{:S(2)}) collective-permute-start(bf16[13,48,512]{2,1,0:T(8,128)(2,1)S(1)} %get-tuple-element.69), channel_id=1, source_target_pairs={{0,1},{1,0},{2,3},{3,2},{4,5},{5,4},{6,7},{7,6},{8,9},{9,8},{10,11... | collective-permute-start | bytes 1916936 | tf_op jit(solution)/shard_map/ppermute | solution.py:509
  101.0 5.0 %collective-permute-start = (bf16[64,16,512]{2,1,0:T(8,128)(2,1)S(1)}, bf16[64,16,512]{2,1,0:T(8,128)(2,1)S(1)}, u32[]{:S(2)}, u32[]{:S(2)}) collective-permute-start(bf16[64,16,512]{2,1,0:T(8,128)(2,1)S(1)} %get-tuple-element.62), channel_id=1, source_target_pairs={{0,1},{1,0},{2,3},{3,2},{4,5},{5,4},{6,7},{7,6},{8,9},{9,8},{10,11... | collective-permute-start | bytes 3145736 | tf_op jit(solution)/shard_map/ppermute | solution.py:509
  101.3 18.5 %all-to-all-start.3 = ((bf16[16,44,512]{2,1,0:T(8,128)(2,1)}), bf16[16,44,512]{2,1,0:T(8,128)(2,1)}, u32[]{:S(2)}, u32[]{:S(2)}) async-start(bf16[16,44,512]{2,1,0:T(8,128)(2,1)} %get-tuple-element.60), calls=%async_computation.3 | async-start | bytes 1572864 | tf_op jit(solution)/shard_map/all_to_all | solution.py:496
  119.8 36.9 %all-to-all-start.4 = ((bf16[64,16,512]{2,1,0:T(8,128)(2,1)}), bf16[64,16,512]{2,1,0:T(8,128)(2,1)S(1)}, u32[]{:S(2)}, u32[]{:S(2)}) async-start(bf16[64,16,512]{2,1,0:T(8,128)(2,1)} %shard_map.148), calls=%async_computation.4 | async-start | bytes 2097152 | tf_op jit(solution)/shard_map/all_to_all | solution.py:496
  130.7 1.1 copy-start
  132.4 13.4 %collective-permute-start.6 = (bf16[192,512]{1,0:T(8,128)(2,1)S(1)}, bf16[192,512]{1,0:T(8,128)(2,1)S(1)}, u32[]{:S(2)}, u32[]{:S(2)}) collective-permute-start(bf16[192,512]{1,0:T(8,128)(2,1)S(1)} %get-tuple-element.71), channel_id=1, source_target_pairs={{0,4},{4,0},{8,12},{12,8},{1,5},{5,1},{9,13},{13,9},{2,6},{6,2},{1... | collective-permute-start | bytes 589832 | tf_op jit(solution)/shard_map/ppermute | solution.py:501
  134.0 17.1 %collective-permute-start.7 = (bf16[192,512]{1,0:T(8,128)(2,1)S(1)}, bf16[192,512]{1,0:T(8,128)(2,1)S(1)}, u32[]{:S(2)}, u32[]{:S(2)}) collective-permute-start(bf16[192,512]{1,0:T(8,128)(2,1)S(1)} %get-tuple-element.72), channel_id=1, source_target_pairs={{0,8},{4,12},{8,0},{12,4},{1,9},{5,13},{9,1},{13,5},{2,10},{6,14},... | collective-permute-start | bytes 589832 | tf_op jit(solution)/shard_map/ppermute | solution.py:501
  136.7 14.4 %collective-permute-start.8 = (bf16[192,512]{1,0:T(8,128)(2,1)S(1)}, bf16[192,512]{1,0:T(8,128)(2,1)S(1)}, u32[]{:S(2)}, u32[]{:S(2)}) collective-permute-start(bf16[192,512]{1,0:T(8,128)(2,1)S(1)} %get-tuple-element.73), channel_id=1, source_target_pairs={{0,12},{4,8},{8,4},{12,0},{1,13},{5,9},{9,5},{13,1},{2,14},{6,10},... | collective-permute-start | bytes 589832 | tf_op jit(solution)/shard_map/ppermute | solution.py:501
  151.9 5.6 %collective-permute-start.9 = (bf16[48,512]{1,0:T(8,128)(2,1)S(1)}, bf16[48,512]{1,0:T(8,128)(2,1)S(1)}, u32[]{:S(2)}, u32[]{:S(2)}) collective-permute-start(bf16[48,512]{1,0:T(8,128)(2,1)S(1)} %get-tuple-element.75), channel_id=1, source_target_pairs={{0,2},{2,0},{16,18},{18,16},{1,3},{3,1},{17,19},{19,17},{4,6},{6,4... | collective-permute-start | bytes 147464 | tf_op jit(solution)/shard_map/ppermute | solution.py:501
  153.5 5.7 %collective-permute-start.10 = (bf16[48,512]{1,0:T(8,128)(2,1)S(1)}, bf16[48,512]{1,0:T(8,128)(2,1)S(1)}, u32[]{:S(2)}, u32[]{:S(2)}) collective-permute-start(bf16[48,512]{1,0:T(8,128)(2,1)S(1)} %get-tuple-element.76), channel_id=1, source_target_pairs={{0,16},{2,18},{16,0},{18,2},{1,17},{3,19},{17,1},{19,3},{4,20},{6,... | collective-permute-start | bytes 147464 | tf_op jit(solution)/shard_map/ppermute | solution.py:501
  156.7 5.3 %collective-permute-start.11 = (bf16[48,512]{1,0:T(8,128)(2,1)S(1)}, bf16[48,512]{1,0:T(8,128)(2,1)S(1)}, u32[]{:S(2)}, u32[]{:S(2)}) collective-permute-start(bf16[48,512]{1,0:T(8,128)(2,1)S(1)} %get-tuple-element.77), channel_id=1, source_target_pairs={{0,18},{2,16},{16,2},{18,0},{1,19},{3,17},{17,3},{19,1},{4,22},{6,... | collective-permute-start | bytes 147464 | tf_op jit(solution)/shard_map/ppermute | solution.py:501
Sparse Core Ops, SparseCore 0:
  91.0 39.6 reduce-scatter.1

commit v4 on v3

--- a/solution.py
+++ b/solution.py
@@ -243,27 +243,28 @@
 
 
 def row_backward(
-    core, pack, tokens_far, normed_far, packed_far, mixed_far, weights_far, inproj_far, outproj_far,
-    out, mine, other,
-    tokens, normed, packed, mixed, weights, inproj, outproj, grads, low, hidden, output, upstream, semaphores,
+    pack, tokens_far, packed_far, weights_far, inproj_far, outproj_far,
+    out, grads_far, low_far,
+    tokens, packed, weights, inproj, outproj, grads, low, hidden, output, upstream, semaphores,
 ):
     mover = Mover(semaphores)
     outproj_in = mover.start(outproj_far, outproj)
     coming = [mover.start(packed_far, packed), mover.start(weights_far, weights)]
     inproj_in = mover.start(inproj_far, inproj)
     tokens_in = mover.start(tokens_far, tokens)
-    last = [mover.start(normed_far, normed), mover.start(mixed_far, mixed)]
     for block in range(LATS):
         piece = pack[block].astype(f32)
         rows = pl.ds(block * PART, PART)
         hidden[rows, :] = piece[:PART]
         output[rows, :] = piece[PART:]
     low[...] = hidden[...].astype(bf16)
+    leaving = [mover.start(low, low_far)]
     outproj_in.wait()
     upstream[...] = dot(low[...], outproj[...], 1, 1).astype(bf16)
     for copy in coming:
         copy.wait()
     attend_rows_back(packed, upstream, weights, grads)
+    leaving.append(mover.start(grads, grads_far))
     inproj_in.wait()
     grad_normed = dot(grads[...], inproj[...], 1, 1)
     tokens_in.wait()
@@ -271,9 +272,8 @@
     for block in range(16):
         rows = pl.ds(block * NEAR, NEAR)
         out[block] = jnp.concatenate([hidden[rows, :], output[rows, :]], axis=0).astype(bf16)
-    for copy in last:
-        copy.wait()
-    split_terms(core, grads, normed, low, mixed, mine, other)
+    for copy in leaving:
+        copy.wait()
 
 
 def to_columns(pack, columns):
@@ -402,19 +402,24 @@
         put_terms(place, terms, block, pl.ds(16, 32), mine, others)
 
 
-def split_terms(place, grads, normed, low, mixed, mine, other):
+def row_terms(place, *refs):
+    far, mine, others, near, semaphores = refs[:4], refs[4], refs[5:7], refs[7:11], refs[11]
+    mover = Mover(semaphores)
+    for copy in [mover.start(source, target) for source, target in zip(far, near)]:
+        copy.wait()
     for block in range(4):
-        terms = jnp.concatenate(block_terms(block, grads, normed, low, mixed), axis=1)
+        terms = jnp.concatenate(block_terms(block, *near), axis=1)
         terms = terms.astype(bf16).reshape(16, 2, 16, WIDTH)
-        chips = pl.ds(block * 16, 16)
-        mine[chips] = jnp.where(place[0] == 0, terms[:, 0], terms[:, 1])
-        other[chips] = jnp.where(place[0] == 0, terms[:, 1], terms[:, 0])
-
-
-def join_cores(mine, other, out):
+        mine[pl.ds(block * 16, 16)] = jnp.where(place[0] == 0, terms[:, 0], terms[:, 1])
+        leaving = jnp.where(place[0] == 0, terms[:, 1], terms[:, 0])
+        others[block // 2][pl.ds(block % 2 * 16, 16)] = leaving
+
+
+def join_cores(mine, first, second, out):
     for block in range(4):
         chips = pl.ds(block * 16, 16)
-        out[chips] = (mine[chips].astype(f32) + other[chips].astype(f32)).astype(bf16)
+        other = (first, second)[block // 2][pl.ds(block % 2 * 16, 16)]
+        out[chips] = (mine[chips].astype(f32) + other.astype(f32)).astype(bf16)
 
 
 def add_cores(mine, *refs):
@@ -585,21 +590,29 @@
         0.1,
     )
     column = lax.psum_scatter(column.reshape(3072, WIDTH), "x", scatter_dimension=0, tiled=True)
-    pack, lon_mine, lon_other = call(
+    pack, grads, upstream = call(
         row_backward,
-        [(core, SMEM), (swap(pack, TURN), VMEM)]
-        + all_far(row_tokens, row_normed, row_packed, row_mixed, weights, inproj_lon, outproj_lon),
-        [(TO_LON, bf16, VMEM), (SUMS, bf16, VMEM), (SUMS, bf16, VMEM)],
-        low(NARROW, NARROW, QKV, NARROW, LON_WEIGHTS, IN, OUT, QKV, NARROW)
+        [(swap(pack, TURN), VMEM)]
+        + all_far(row_tokens, row_packed, weights, inproj_lon, outproj_lon),
+        [(TO_LON, bf16, pl.ANY)] + far(QKV, NARROW),
+        low(NARROW, QKV, LON_WEIGHTS, IN, OUT, QKV, NARROW)
         + [(NARROW, f32), (NARROW, f32), (NARROW, bf16)],
         7,
         28,
         60.0,
     )
-    lon_other = from_other_core(lon_other)
+    lon_mine, *lon_others = call(
+        row_terms,
+        [(core, SMEM)] + all_far(grads, row_normed, upstream, row_mixed),
+        [(SUMS, bf16, VMEM)] + [((32, 16, WIDTH), bf16, VMEM)] * 2,
+        low(QKV, NARROW, NARROW, NARROW),
+        4,
+        20,
+        0.1,
+    )
     pack = swap(pack, LON)
     (both,) = call(
-        join_cores, [(lon_mine, VMEM), (lon_other, VMEM)], [(SUMS, bf16, VMEM)], [], 0, 12, 0.1
+        join_cores, [(lon_mine, VMEM)] + [(from_other_core(other), VMEM) for other in lon_others], [(SUMS, bf16, VMEM)], [], 0, 12, 0.1
     )
     unpacked = pack.reshape(4, 4, 2 * NEAR, WIDTH).astype(f32)
     lon = call(

time: 170 us -> 169 us (level)
  waiting for transfers between devices: 45.3 us -> 42.7 us
  Pallas kernels: 46.3 us -> 48.5 us
    all_to_all x4, waiting for transfers between devices: 28.3 us -> 21.9 us  [swap(): return lax.all_to_all(array, axes, split_axis=0, concat_axis=0, tiled=True)]
    ppermute x6 -> x7, waiting for transfers between devices: 0.23 us -> 2.42 us  [from_other_core(): return lax.ppermute(array, 'c', [(0, 1), (1, 0)])]
    pallas_call x11 -> x12, Pallas kernels: 46.3 us -> 48.5 us  [call(): pl.pallas_call(kernel, out_shape=[jax.ShapeDtypeStruct(shape, kind) if pl...]
  transfers between devices with their start and end apart: 17 -> 18, of which waited for: 8 -> 11; matrix products, arithmetic and copies ran while one was open for 2% -> 2% of each run, Pallas kernels for 15% -> 17%
where the time goes in v4:
time: 169 us; the launch traced here: 168 us
  Pallas kernels  48.5 us (29%)
  waiting for transfers between devices  42.7 us (25%)
  starting transfers between devices  37.8 us (22%)
  blocking collectives  19.1 us (11%)
  between operations  14.2 us (8%)
  local copies, waits for them, and re-layouts  4.14 us (2%)
    pallas_call x12, Pallas kernels, call(): pl.pallas_call(kernel, out_shape=[jax.ShapeDtypeStruct(shape, kind) if pl...  48.5 us
    all_to_all x4, starting transfers between devices, swap(): return lax.all_to_all(array, axes, split_axis=0, concat_axis=0, tiled=True)  26.1 us
    all_to_all x4, waiting for transfers between devices, swap(): return lax.all_to_all(array, axes, split_axis=0, concat_axis=0, tiled=True)  21.9 us
    all_to_all x1, blocking collectives, swap(): return lax.all_to_all(array, axes, split_axis=0, concat_axis=0, tiled=True)  19.1 us
    ppermute x6, waiting for transfers between devices, trade(): lax.ppermute(part, axes, [(place, place ^ step) for place in range(4)])  14.3 us
    ppermute x6, starting transfers between devices, trade(): lax.ppermute(part, axes, [(place, place ^ step) for place in range(4)])  9.67 us
    reduce_scatter x1, waiting for transfers between devices, per_device(): lax.psum_scatter(column.reshape(3072, WIDTH), 'x', scatter_dimension=0, t...  4.14 us
    unnamed x4, local copies, waits for them, and re-layouts  3.79 us
  transfers between devices with their start and end apart: 18, of which 11 were waited for; matrix products, arithmetic and copies ran while one was open for 2% of the time, Pallas kernels for 17%

profile of v4, /device:TPU:0, one launch (start us, length us, event | category | flops | bytes accessed | tf_op | source)
XLA Modules:
  0.0 168.2 jit_solution(1856269759585907213)
XLA Ops:
  7.2 1.6 pad_maximum_fusion
  8.7 0.2 copy.16
  8.9 19.1 %all_to_all.25.pack = bf16[16,44,512]{2,1,0:T(8,128)(2,1)S(1)} all-to-all(bf16[16,44,512]{2,1,0:T(8,128)(2,1)S(1)} %bitcast.17), channel_id=1, replica_groups=mesh['x'=4,'h'=2,'y'=4,'l'=2,'c'=2] {'y','l','c'}, dimensions={0} | all-to-all | bytes 1441792 | tf_op jit(solution)/shard_map/all_to_all | solution.py:501
  28.0 6.5 %shard_map.143 = (bf16[32,22,512]{2,1,0:T(8,128)(2,1)}, bf16[352,512]{1,0:T(8,128)(2,1)}, bf16[352,512]{1,0:T(8,128)(2,1)}, bf16[352,1536]{1,0:T(8,128)(2,1)}, bf16[352,512]{1,0:T(8,128)(2,1)}) custom-call(bf16[16,44,512]{2,1,0:T(8,128)(2,1)S(1)} %all_to_all.25.pack, bf16[512,1536]{1,0:T(8,128)(2,1)} %inproj_far.5, bf16[512,512]{1,0:T(8,128)(2,1)} %outproj_far.5), custom_call_target="tpu_custom_call" | custom-call | flops 5000000000 | bytes 65536 | tf_op jit(solution)/shard_map/pallas_call | solution.py:481
  34.5 8.6 %all-to-all-start.1 = ((bf16[32,22,512]{2,1,0:T(8,128)(2,1)}), bf16[32,22,512]{2,1,0:T(8,128)(2,1)S(1)}, u32[]{:S(2)}, u32[]{:S(2)}) async-start(bf16[32,22,512]{2,1,0:T(8,128)(2,1)} %get-tuple-element.48), calls=%async_computation.1 | async-start | bytes 1572864 | tf_op jit(solution)/shard_map/all_to_all | solution.py:501
  43.2 15.7 %all-to-all-done.1.pack = bf16[32,22,512]{2,1,0:T(8,128)(2,1)S(1)} async-done(((bf16[32,22,512]{2,1,0:T(8,128)(2,1)}), bf16[32,22,512]{2,1,0:T(8,128)(2,1)S(1)}, u32[]{:S(2)}, u32[]{:S(2)}) %all-to-all-start.1) | async-done | bytes 720928 | tf_op jit(solution)/shard_map/all_to_all | solution.py:501
  58.9 13.0 %shard_map.144 = (bf16[32,22,512]{2,1,0:T(8,128)(2,1)}, bf16[352,512]{1,0:T(8,128)(2,1)}, bf16[352,512]{1,0:T(8,128)(2,1)}, bf16[352,1536]{1,0:T(8,128)(2,1)}, b...) custom-call(bf16[32,22,512]{2,1,0:T(8,128)(2,1)S(1)} %all-to-all-don, ...), custom_call_target="tpu_custom_call" | custom-call | flops 20000000000 | bytes 65536 | tf_op jit(solution)/shard_map/pallas_call | solution.py:481
  71.9 4.4 %all-to-all-start.2 = ((bf16[32,22,512]{2,1,0:T(8,128)(2,1)}), bf16[32,22,512]{2,1,0:T(8,128)(2,1)S(1)}, u32[]{:S(2)}, u32[]{:S(2)}) async-start(bf16[32,22,512]{2,1,0:T(8,128)(2,1)} %get-tuple-element.49), calls=%async_computation.2 | async-start | bytes 1572864 | tf_op jit(solution)/shard_map/all_to_all | solution.py:501
  76.3 0.3 reduce-scatter.2.cloned.1.call-start
  76.6 0.1 pad_add_fusion.place
  76.7 6.5 %shard_map.145 = (bf16[4,4,2,2,48,512]{5,4,3,2,1,0:T(8,128)(2,1)S(1)}, bf16[13,48,512]{2,1,0:T(8,128)(2,1)S(1)}, bf16[13,48,512]{2,1,0:T(8,128)(2,1)S(1)}, bf16[...) custom-call(s32[3]{0:T(128)S(1)} %pad_add_fusion.place, ...), custom_call_target="tpu_custom_call" | custom-call | flops 100000000 | bytes 65536 | tf_op jit(solution)/shard_map/pallas_call | solution.py:481
  83.2 0.1 collective-permute-start.2
  83.2 0.5 collective-permute-start.3
  83.7 0.1 collective-permute-start.4
  83.8 0.4 collective-permute-start.5
  84.3 0.1 collective-permute-start.6
  84.3 4.3 %shard_map.146.weights_far = bf16[8,352,352]{2,1,0:T(8,128)(2,1)} custom-call(bf16[352,1536]{1,0:T(8,128)(2,1)} %get-tuple-element.51.packed_far, bf16[4,4,2,2,48,512]{5,4,3,2,1,0:T(8,128)(2,1)S(1)} %get-tuple-element.60.after.mine), custom_call_target="tpu_custom_call" | custom-call | flops 100000000 | bytes 65536 | tf_op jit(solution)/shard_map/pallas_call | solution.py:481
  88.7 0.2 collective-permute-done.6.refs_4_
  89.0 1.8 %shard_map.151 = bf16[4,4,2,2,48,512]{5,4,3,2,1,0:T(8,128)(2,1)} custom-call(bf16[4,4,2,2,48,512]{5,4,3,2,1,0:T(8,128)(2,1)S(1)} %get-tuple-element.60.after.mine, bf16[13,48,512]{2,1,0:T(8,128)(2,1)S(1)} %collective-permute-done.2.refs_0_, bf16[13,48,512]{2,1,0:T(8,128)(2,1)S(1)} %collective-permute-done.3.refs_1_, ...), custom_call_target="tpu_custom_call" | custom-call | flops 100000000 | bytes 65536 | tf_op jit(solution)/shard_map/pallas_call | solution.py:481
  90.9 8.8 %shard_map.147 = (bf16[16,44,512]{2,1,0:T(8,128)(2,1)}, bf16[352,1536]{1,0:T(8,128)(2,1)}, bf16[352,512]{1,0:T(8,128)(2,1)}) custom-call(bf16[32,22,512]{2,1,0:T(8,128)(2,1)S(1)} %all-to-all-done.2.pack, bf16[352,512]{1,0:T(8,128)(2,1)} %get-tuple-element.50.tokens_far, bf16[352,1536]{1,0:T(8,128)(2,1)} %get-tuple-element.51.packed_far, ...), custom_call_target="tpu_custom_call" | custom-call | flops 60000002048 | bytes 65536 | tf_op jit(solution)/shard_map/pallas_call | solution.py:481
  99.6 4.7 %all-to-all-start.3 = ((bf16[16,44,512]{2,1,0:T(8,128)(2,1)}), bf16[16,44,512]{2,1,0:T(8,128)(2,1)S(1)}, u32[]{:S(2)}, u32[]{:S(2)}) async-start(bf16[16,44,512]{2,1,0:T(8,128)(2,1)} %get-tuple-element.61), calls=%async_computation.3 | async-start | bytes 1572864 | tf_op jit(solution)/shard_map/all_to_all | solution.py:501
  104.3 3.5 %shard_map.148 = (bf16[64,16,512]{2,1,0:T(8,128)(2,1)S(1)}, bf16[32,16,512]{2,1,0:T(8,128)(2,1)S(1)}, bf16[32,16,512]{2,1,0:T(8,128)(2,1)S(1)}) custom-call(s32[3]{0:T(128)S(1)} %pad_add_fusion.place, bf16[352,1536]{1,0:T(8,128)(2,1)} %get-tuple-element.62.refs_0_, bf16[352,512]{1,0:T(8,128)(2,1)} %get-tuple-element.63.refs_1_, ...), custom_call_target="tpu_custom_call" | custom-call | flops 100000000 | bytes 65536 | tf_op jit(solution)/shard_map/pallas_call | solution.py:481
  107.9 0.5 collective-permute-start
  108.4 0.1 collective-permute-start.1
  108.5 1.4 collective-permute-done.first
  109.9 0.7 collective-permute-done.1.second
  110.7 1.2 shard_map.149
  111.9 6.1 %all-to-all-done.3 = bf16[16,44,512]{2,1,0:T(8,128)(2,1)S(1)} async-done(((bf16[16,44,512]{2,1,0:T(8,128)(2,1)}), bf16[16,44,512]{2,1,0:T(8,128)(2,1)S(1)}, u32[]{:S(2)}, u32[]{:S(2)}) %all-to-all-start.3) | async-done | bytes 720928 | tf_op jit(solution)/shard_map/all_to_all | solution.py:501
  118.0 8.5 %all-to-all-start.4 = ((bf16[64,16,512]{2,1,0:T(8,128)(2,1)}), bf16[64,16,512]{2,1,0:T(8,128)(2,1)S(1)}, u32[]{:S(2)}, u32[]{:S(2)}) async-start(bf16[64,16,512]{2,1,0:T(8,128)(2,1)} %shard_map.149), calls=%async_computation.4 | async-start | bytes 2097152 | tf_op jit(solution)/shard_map/all_to_all | solution.py:501
  126.5 4.1 %reduce-scatter.2.cloned.1.call-done = bf16[768,512]{1,0:T(8,128)(2,1)} async-done(((bf16[3072,512]{1,0:T(8,128)(2,1)}), bf16[768,512]{1,0:T(8,128)(2,1)}) %reduce-scatter.2.cloned.1.call-update) | async-done | bytes 786448 | tf_op jit(solution)/shard_map/reduce_scatter | solution.py:592
  130.6 1.1 copy-done
  131.7 0.6 shard_map.152
  132.4 1.6 collective-permute-start.7
  133.9 2.7 %collective-permute-start.8 = (bf16[192,512]{1,0:T(8,128)(2,1)S(1)}, bf16[192,512]{1,0:T(8,128)(2,1)S(1)}, u32[]{:S(2)}, u32[]{:S(2)}) collective-permute-start(bf16[192,512]{1,0:T(8,128)(2,1)S(1)} %get-tuple-element.78), channel_id=1, source_target_pairs={{0,8},{4,12},{8,0},{12,4},{1,9},{5,13},{9,1},{13,5},{2,10},{6,14},... | collective-permute-start | bytes 589832 | tf_op jit(solution)/shard_map/ppermute | solution.py:506
  136.6 0.5 collective-permute-start.9
  137.1 0.2 fusion
  137.3 1.3 copy.20
  138.7 1.3 copy.19
  140.0 3.7 %collective-permute-done.7.refs_1_ = bf16[192,512]{1,0:T(8,128)(2,1)S(1)} collective-permute-done((bf16[192,512]{1,0:T(8,128)(2,1)S(1)}, bf16[192,512]{1,0:T(8,128)(2,1)S(1)}, u32[]{:S(2)}, u32[]{:S(2)}) %collective-permute-start.7) | collective-permute-done | bytes 196640 | tf_op jit(solution)/shard_map/ppermute | solution.py:506
  143.7 5.6 %collective-permute-done.8.refs_2_ = bf16[192,512]{1,0:T(8,128)(2,1)S(1)} collective-permute-done((bf16[192,512]{1,0:T(8,128)(2,1)S(1)}, bf16[192,512]{1,0:T(8,128)(2,1)S(1)}, u32[]{:S(2)}, u32[]{:S(2)}) %collective-permute-start.8) | collective-permute-done | bytes 196640 | tf_op jit(solution)/shard_map/ppermute | solution.py:506
  149.3 0.5 collective-permute-done.9.refs_3_
  149.8 0.7 shard_map.153
  150.5 1.7 collective-permute-start.10
  152.2 3.2 %collective-permute-start.11 = (bf16[48,512]{1,0:T(8,128)(2,1)S(1)}, bf16[48,512]{1,0:T(8,128)(2,1)S(1)}, u32[]{:S(2)}, u32[]{:S(2)}) collective-permute-start(bf16[48,512]{1,0:T(8,128)(2,1)S(1)} %get-tuple-element.82), channel_id=1, source_target_pairs={{0,16},{2,18},{16,0},{18,2},{1,17},{3,19},{17,1},{19,3},{4,20},{6,... | collective-permute-start | bytes 147464 | tf_op jit(solution)/shard_map/ppermute | solution.py:506
  155.4 0.8 shard_map.150
  156.2 1.8 %collective-permute-done.11.refs_2_ = bf16[48,512]{1,0:T(8,128)(2,1)S(1)} collective-permute-done((bf16[48,512]{1,0:T(8,128)(2,1)S(1)}, bf16[48,512]{1,0:T(8,128)(2,1)S(1)}, u32[]{:S(2)}, u32[]{:S(2)}) %collective-permute-start.11) | collective-permute-done | bytes 49184 | tf_op jit(solution)/shard_map/ppermute | solution.py:506
  158.0 2.7 %collective-permute-done.12.refs_3_ = bf16[48,512]{1,0:T(8,128)(2,1)S(1)} collective-permute-done((bf16[48,512]{1,0:T(8,128)(2,1)S(1)}, bf16[48,512]{1,0:T(8,128)(2,1)S(1)}, u32[]{:S(2)}, u32[]{:S(2)}) %collective-permute-start.12) | collective-permute-done | bytes 49184 | tf_op jit(solution)/shard_map/ppermute | solution.py:506
  160.7 0.6 shard_map.154
  (10 shorter events, 0.0 us)
Async XLA Ops:
  34.5 24.4 %all-to-all-start.1 = ((bf16[32,22,512]{2,1,0:T(8,128)(2,1)}), bf16[32,22,512]{2,1,0:T(8,128)(2,1)S(1)}, u32[]{:S(2)}, u32[]{:S(2)}) async-start(bf16[32,22,512]{2,1,0:T(8,128)(2,1)} %get-tuple-element.48), calls=%async_computation.1 | async-start | bytes 1572864 | tf_op jit(solution)/shard_map/all_to_all | solution.py:501
  71.9 18.9 %all-to-all-start.2 = ((bf16[32,22,512]{2,1,0:T(8,128)(2,1)}), bf16[32,22,512]{2,1,0:T(8,128)(2,1)S(1)}, u32[]{:S(2)}, u32[]{:S(2)}) async-start(bf16[32,22,512]{2,1,0:T(8,128)(2,1)} %get-tuple-element.49), calls=%async_computation.2 | async-start | bytes 1572864 | tf_op jit(solution)/shard_map/all_to_all | solution.py:501
  76.3 54.3 %reduce-scatter.2.cloned.1.call-start = ((), (), s32[]{:S(2)}) async-start(), calls=%async_computation.6 | async-start | bytes 3932160 | tf_op jit(solution)/shard_map/reduce_scatter | solution.py:592
  83.2 5.5 %collective-permute-start.2 = (bf16[13,48,512]{2,1,0:T(8,128)(2,1)S(1)}, bf16[13,48,512]{2,1,0:T(8,128)(2,1)S(1)}, u32[]{:S(2)}, u32[]{:S(2)}) collective-permute-start(bf16[13,48,512]{2,1,0:T(8,128)(2,1)S(1)} %get-tuple-element.71), channel_id=1, source_target_pairs={{0,1},{1,0},{2,3},{3,2},{4,5},{5,4},{6,7},{7,6},{8,9},{9,8},{10,11... | collective-permute-start | bytes 1916936 | tf_op jit(solution)/shard_map/ppermute | solution.py:514
  83.2 5.5 %collective-permute-start.3 = (bf16[13,48,512]{2,1,0:T(8,128)(2,1)S(1)}, bf16[13,48,512]{2,1,0:T(8,128)(2,1)S(1)}, u32[]{:S(2)}, u32[]{:S(2)}) collective-permute-start(bf16[13,48,512]{2,1,0:T(8,128)(2,1)S(1)} %get-tuple-element.72), channel_id=1, source_target_pairs={{0,1},{1,0},{2,3},{3,2},{4,5},{5,4},{6,7},{7,6},{8,9},{9,8},{10,11... | collective-permute-start | bytes 1916936 | tf_op jit(solution)/shard_map/ppermute | solution.py:514
  83.7 5.0 %collective-permute-start.4 = (bf16[13,48,512]{2,1,0:T(8,128)(2,1)S(1)}, bf16[13,48,512]{2,1,0:T(8,128)(2,1)S(1)}, u32[]{:S(2)}, u32[]{:S(2)}) collective-permute-start(bf16[13,48,512]{2,1,0:T(8,128)(2,1)S(1)} %get-tuple-element.73), channel_id=1, source_target_pairs={{0,1},{1,0},{2,3},{3,2},{4,5},{5,4},{6,7},{7,6},{8,9},{9,8},{10,11... | collective-permute-start | bytes 1916936 | tf_op jit(solution)/shard_map/ppermute | solution.py:514
  83.8 4.9 %collective-permute-start.5 = (bf16[13,48,512]{2,1,0:T(8,128)(2,1)S(1)}, bf16[13,48,512]{2,1,0:T(8,128)(2,1)S(1)}, u32[]{:S(2)}, u32[]{:S(2)}) collective-permute-start(bf16[13,48,512]{2,1,0:T(8,128)(2,1)S(1)} %get-tuple-element.74), channel_id=1, source_target_pairs={{0,1},{1,0},{2,3},{3,2},{4,5},{5,4},{6,7},{7,6},{8,9},{9,8},{10,11... | collective-permute-start | bytes 1916936 | tf_op jit(solution)/shard_map/ppermute | solution.py:514
  84.3 4.7 %collective-permute-start.6 = (bf16[13,48,512]{2,1,0:T(8,128)(2,1)S(1)}, bf16[13,48,512]{2,1,0:T(8,128)(2,1)S(1)}, u32[]{:S(2)}, u32[]{:S(2)}) collective-permute-start(bf16[13,48,512]{2,1,0:T(8,128)(2,1)S(1)} %get-tuple-element.75), channel_id=1, source_target_pairs={{0,1},{1,0},{2,3},{3,2},{4,5},{5,4},{6,7},{7,6},{8,9},{9,8},{10,11... | collective-permute-start | bytes 1916936 | tf_op jit(solution)/shard_map/ppermute | solution.py:514
  99.6 18.4 %all-to-all-start.3 = ((bf16[16,44,512]{2,1,0:T(8,128)(2,1)}), bf16[16,44,512]{2,1,0:T(8,128)(2,1)S(1)}, u32[]{:S(2)}, u32[]{:S(2)}) async-start(bf16[16,44,512]{2,1,0:T(8,128)(2,1)} %get-tuple-element.61), calls=%async_computation.3 | async-start | bytes 1572864 | tf_op jit(solution)/shard_map/all_to_all | solution.py:501
  107.9 2.0 %collective-permute-start = (bf16[32,16,512]{2,1,0:T(8,128)(2,1)S(1)}, bf16[32,16,512]{2,1,0:T(8,128)(2,1)S(1)}, u32[]{:S(2)}, u32[]{:S(2)}) collective-permute-start(bf16[32,16,512]{2,1,0:T(8,128)(2,1)S(1)} %get-tuple-element.67), channel_id=1, source_target_pairs={{0,1},{1,0},{2,3},{3,2},{4,5},{5,4},{6,7},{7,6},{8,9},{9,8},{10,11... | collective-permute-start | bytes 1572872 | tf_op jit(solution)/shard_map/ppermute | solution.py:514
  108.4 2.3 %collective-permute-start.1 = (bf16[32,16,512]{2,1,0:T(8,128)(2,1)S(1)}, bf16[32,16,512]{2,1,0:T(8,128)(2,1)S(1)}, u32[]{:S(2)}, u32[]{:S(2)}) collective-permute-start(bf16[32,16,512]{2,1,0:T(8,128)(2,1)S(1)} %get-tuple-element.68), channel_id=1, source_target_pairs={{0,1},{1,0},{2,3},{3,2},{4,5},{5,4},{6,7},{7,6},{8,9},{9,8},{10,11... | collective-permute-start | bytes 1572872 | tf_op jit(solution)/shard_map/ppermute | solution.py:514
  118.0 37.4 %all-to-all-start.4 = ((bf16[64,16,512]{2,1,0:T(8,128)(2,1)}), bf16[64,16,512]{2,1,0:T(8,128)(2,1)S(1)}, u32[]{:S(2)}, u32[]{:S(2)}) async-start(bf16[64,16,512]{2,1,0:T(8,128)(2,1)} %shard_map.149), calls=%async_computation.4 | async-start | bytes 2097152 | tf_op jit(solution)/shard_map/all_to_all | solution.py:501
  130.6 1.1 copy-start
  132.4 11.3 %collective-permute-start.7 = (bf16[192,512]{1,0:T(8,128)(2,1)S(1)}, bf16[192,512]{1,0:T(8,128)(2,1)S(1)}, u32[]{:S(2)}, u32[]{:S(2)}) collective-permute-start(bf16[192,512]{1,0:T(8,128)(2,1)S(1)} %get-tuple-element.77), channel_id=1, source_target_pairs={{0,4},{4,0},{8,12},{12,8},{1,5},{5,1},{9,13},{13,9},{2,6},{6,2},{1... | collective-permute-start | bytes 589832 | tf_op jit(solution)/shard_map/ppermute | solution.py:506
  133.9 15.4 %collective-permute-start.8 = (bf16[192,512]{1,0:T(8,128)(2,1)S(1)}, bf16[192,512]{1,0:T(8,128)(2,1)S(1)}, u32[]{:S(2)}, u32[]{:S(2)}) collective-permute-start(bf16[192,512]{1,0:T(8,128)(2,1)S(1)} %get-tuple-element.78), channel_id=1, source_target_pairs={{0,8},{4,12},{8,0},{12,4},{1,9},{5,13},{9,1},{13,5},{2,10},{6,14},... | collective-permute-start | bytes 589832 | tf_op jit(solution)/shard_map/ppermute | solution.py:506
  136.6 13.2 %collective-permute-start.9 = (bf16[192,512]{1,0:T(8,128)(2,1)S(1)}, bf16[192,512]{1,0:T(8,128)(2,1)S(1)}, u32[]{:S(2)}, u32[]{:S(2)}) collective-permute-start(bf16[192,512]{1,0:T(8,128)(2,1)S(1)} %get-tuple-element.79), channel_id=1, source_target_pairs={{0,12},{4,8},{8,4},{12,0},{1,13},{5,9},{9,5},{13,1},{2,14},{6,10},... | collective-permute-start | bytes 589832 | tf_op jit(solution)/shard_map/ppermute | solution.py:506
  150.5 5.7 %collective-permute-start.10 = (bf16[48,512]{1,0:T(8,128)(2,1)S(1)}, bf16[48,512]{1,0:T(8,128)(2,1)S(1)}, u32[]{:S(2)}, u32[]{:S(2)}) collective-permute-start(bf16[48,512]{1,0:T(8,128)(2,1)S(1)} %get-tuple-element.81), channel_id=1, source_target_pairs={{0,2},{2,0},{16,18},{18,16},{1,3},{3,1},{17,19},{19,17},{4,6},{6,4... | collective-permute-start | bytes 147464 | tf_op jit(solution)/shard_map/ppermute | solution.py:506
  152.2 5.8 %collective-permute-start.11 = (bf16[48,512]{1,0:T(8,128)(2,1)S(1)}, bf16[48,512]{1,0:T(8,128)(2,1)S(1)}, u32[]{:S(2)}, u32[]{:S(2)}) collective-permute-start(bf16[48,512]{1,0:T(8,128)(2,1)S(1)} %get-tuple-element.82), channel_id=1, source_target_pairs={{0,16},{2,18},{16,0},{18,2},{1,17},{3,19},{17,1},{19,3},{4,20},{6,... | collective-permute-start | bytes 147464 | tf_op jit(solution)/shard_map/ppermute | solution.py:506
  155.4 5.3 %collective-permute-start.12 = (bf16[48,512]{1,0:T(8,128)(2,1)S(1)}, bf16[48,512]{1,0:T(8,128)(2,1)S(1)}, u32[]{:S(2)}, u32[]{:S(2)}) collective-permute-start(bf16[48,512]{1,0:T(8,128)(2,1)S(1)} %get-tuple-element.83), channel_id=1, source_target_pairs={{0,18},{2,16},{16,2},{18,0},{1,19},{3,17},{17,3},{19,1},{4,22},{6,... | collective-permute-start | bytes 147464 | tf_op jit(solution)/shard_map/ppermute | solution.py:506
Sparse Core Ops, SparseCore 0:
  91.0 39.6 reduce-scatter.1

commit v5 on v4

--- a/solution.py
+++ b/solution.py
@@ -444,9 +444,13 @@
     lon_out[...] = total[12:16]
 
 
-def pick_y(place, blocks, *outs):
-    for step in range(4):
-        outs[step][...] = blocks[jnp.bitwise_xor(place[1], step)]
+def pick_y(place, blocks_far, *refs):
+    outs, mover = refs[:4], Mover(refs[4])
+    copies = [
+        mover.start(blocks_far.at[jnp.bitwise_xor(place[1], step)], outs[step]) for step in range(4)
+    ]
+    for copy in copies:
+        copy.wait()
 
 
 def sum_pick_z(place, *refs):
@@ -503,9 +507,8 @@
 
 def trade(parts, axes):
     moved = [
-        lax.ppermute(part, axes, [(place, place ^ step) for place in range(4)])
-        for step, part in enumerate(parts)
-        if step
+        lax.ppermute(parts[step], axes, [(place, place ^ step) for place in range(4)])
+        for step in (2, 3, 1)
     ]
     return [parts[0], *moved]
 
@@ -626,10 +629,10 @@
     )
     parts = call(
         pick_y,
-        [(core, SMEM), (column.reshape(4, 192, WIDTH), VMEM)],
+        [(core, SMEM), (column.reshape(4, 192, WIDTH), HBM)],
         [((192, WIDTH), bf16, VMEM)] * 4,
         [],
-        0,
+        4,
         8,
         0.01,
     )

time: 169 us -> 167 us (0.988)
    unnamed x4 -> x2, local copies, waits for them, and re-layouts: 3.79 us -> 2.65 us
  transfers between devices with their start and end apart: 18 -> 18, of which waited for: 11 -> 10; matrix products, arithmetic and copies ran while one was open for 2% -> 2% of each run, Pallas kernels for 17% -> 18%
where the time goes in v5:
time: 167 us
  Pallas kernels  49.7 us (30%)
  waiting for transfers between devices  42.4 us (25%)
  starting transfers between devices  36.7 us (22%)
  blocking collectives  19.1 us (11%)
  between operations  14.2 us (9%)
  local copies, waits for them, and re-layouts  3.01 us (2%)
    pallas_call x12, Pallas kernels, call(): pl.pallas_call(kernel, out_shape=[jax.ShapeDtypeStruct(shape, kind) if pl...  49.7 us
    all_to_all x4, starting transfers between devices, swap(): return lax.all_to_all(array, axes, split_axis=0, concat_axis=0, tiled=True)  26.1 us
    all_to_all x4, waiting for transfers between devices, swap(): return lax.all_to_all(array, axes, split_axis=0, concat_axis=0, tiled=True)  21.9 us
    all_to_all x1, blocking collectives, swap(): return lax.all_to_all(array, axes, split_axis=0, concat_axis=0, tiled=True)  19.1 us
    ppermute x6, waiting for transfers between devices, trade(): lax.ppermute(parts[step], axes, [(place, place ^ step) for place in range...  13.9 us
    ppermute x6, starting transfers between devices, trade(): lax.ppermute(parts[step], axes, [(place, place ^ step) for place in range...  8.55 us
    reduce_scatter x1, waiting for transfers between devices, per_device(): lax.psum_scatter(column.reshape(3072, WIDTH), 'x', scatter_dimension=0, t...  4.15 us
  transfers between devices with their start and end apart: 18, of which 10 were waited for; matrix products, arithmetic and copies ran while one was open for 2% of the time, Pallas kernels for 18%

profile of v5, /device:TPU:0, one launch (start us, length us, event | category | flops | bytes accessed | tf_op | source)
XLA Modules:
  0.0 166.8 jit_solution(5128604100096990803)
XLA Ops:
  7.2 1.6 pad_maximum_fusion
  8.7 0.2 copy.16
  8.9 19.1 %all_to_all.25.pack = bf16[16,44,512]{2,1,0:T(8,128)(2,1)S(1)} all-to-all(bf16[16,44,512]{2,1,0:T(8,128)(2,1)S(1)} %bitcast.16), channel_id=1, replica_groups=mesh['x'=4,'h'=2,'y'=4,'l'=2,'c'=2] {'y','l','c'}, dimensions={0} | all-to-all | bytes 1441792 | tf_op jit(solution)/shard_map/all_to_all | solution.py:505
  28.0 6.5 %shard_map.143 = (bf16[32,22,512]{2,1,0:T(8,128)(2,1)}, bf16[352,512]{1,0:T(8,128)(2,1)}, bf16[352,512]{1,0:T(8,128)(2,1)}, bf16[352,1536]{1,0:T(8,128)(2,1)}, bf16[352,512]{1,0:T(8,128)(2,1)}) custom-call(bf16[16,44,512]{2,1,0:T(8,128)(2,1)S(1)} %all_to_all.25.pack, bf16[512,1536]{1,0:T(8,128)(2,1)} %inproj_far.5, bf16[512,512]{1,0:T(8,128)(2,1)} %outproj_far.5), custom_call_target="tpu_custom_call" | custom-call | flops 5000000000 | bytes 65536 | tf_op jit(solution)/shard_map/pallas_call | solution.py:485
  34.6 8.6 %all-to-all-start.1 = ((bf16[32,22,512]{2,1,0:T(8,128)(2,1)}), bf16[32,22,512]{2,1,0:T(8,128)(2,1)S(1)}, u32[]{:S(2)}, u32[]{:S(2)}) async-start(bf16[32,22,512]{2,1,0:T(8,128)(2,1)} %get-tuple-element.48), calls=%async_computation.1 | async-start | bytes 1572864 | tf_op jit(solution)/shard_map/all_to_all | solution.py:505
  43.2 15.7 %all-to-all-done.1.pack = bf16[32,22,512]{2,1,0:T(8,128)(2,1)S(1)} async-done(((bf16[32,22,512]{2,1,0:T(8,128)(2,1)}), bf16[32,22,512]{2,1,0:T(8,128)(2,1)S(1)}, u32[]{:S(2)}, u32[]{:S(2)}) %all-to-all-start.1) | async-done | bytes 720928 | tf_op jit(solution)/shard_map/all_to_all | solution.py:505
  58.9 13.0 %shard_map.144 = (bf16[32,22,512]{2,1,0:T(8,128)(2,1)}, bf16[352,512]{1,0:T(8,128)(2,1)}, bf16[352,512]{1,0:T(8,128)(2,1)}, bf16[352,1536]{1,0:T(8,128)(2,1)}, b...) custom-call(bf16[32,22,512]{2,1,0:T(8,128)(2,1)S(1)} %all-to-all-don, ...), custom_call_target="tpu_custom_call" | custom-call | flops 20000000000 | bytes 65536 | tf_op jit(solution)/shard_map/pallas_call | solution.py:485
  71.9 4.4 %all-to-all-start.2 = ((bf16[32,22,512]{2,1,0:T(8,128)(2,1)}), bf16[32,22,512]{2,1,0:T(8,128)(2,1)S(1)}, u32[]{:S(2)}, u32[]{:S(2)}) async-start(bf16[32,22,512]{2,1,0:T(8,128)(2,1)} %get-tuple-element.49), calls=%async_computation.2 | async-start | bytes 1572864 | tf_op jit(solution)/shard_map/all_to_all | solution.py:505
  76.3 0.3 reduce-scatter.2.cloned.1.call-start
  76.6 0.1 pad_add_fusion.place
  76.7 6.5 %shard_map.145 = (bf16[4,4,2,2,48,512]{5,4,3,2,1,0:T(8,128)(2,1)S(1)}, bf16[13,48,512]{2,1,0:T(8,128)(2,1)S(1)}, bf16[13,48,512]{2,1,0:T(8,128)(2,1)S(1)}, bf16[...) custom-call(s32[3]{0:T(128)S(1)} %pad_add_fusion.place, ...), custom_call_target="tpu_custom_call" | custom-call | flops 100000000 | bytes 65536 | tf_op jit(solution)/shard_map/pallas_call | solution.py:485
  83.2 0.1 collective-permute-start.2
  83.3 0.5 collective-permute-start.3
  83.7 0.1 collective-permute-start.4
  83.8 0.4 collective-permute-start.5
  84.3 0.1 collective-permute-start.6
  84.4 4.4 %shard_map.146.weights_far = bf16[8,352,352]{2,1,0:T(8,128)(2,1)} custom-call(bf16[352,1536]{1,0:T(8,128)(2,1)} %get-tuple-element.51.packed_far, bf16[4,4,2,2,48,512]{5,4,3,2,1,0:T(8,128)(2,1)S(1)} %get-tuple-element.60.after.mine), custom_call_target="tpu_custom_call" | custom-call | flops 100000000 | bytes 65536 | tf_op jit(solution)/shard_map/pallas_call | solution.py:485
  88.8 0.2 collective-permute-done.6.refs_4_
  89.0 1.9 %shard_map.151 = bf16[4,4,2,2,48,512]{5,4,3,2,1,0:T(8,128)(2,1)} custom-call(bf16[4,4,2,2,48,512]{5,4,3,2,1,0:T(8,128)(2,1)S(1)} %get-tuple-element.60.after.mine, bf16[13,48,512]{2,1,0:T(8,128)(2,1)S(1)} %collective-permute-done.2.refs_0_, bf16[13,48,512]{2,1,0:T(8,128)(2,1)S(1)} %collective-permute-done.3.refs_1_, ...), custom_call_target="tpu_custom_call" | custom-call | flops 100000000 | bytes 65536 | tf_op jit(solution)/shard_map/pallas_call | solution.py:485
  90.8 0.0 reduce-scatter.2.cloned.1.call-update
  90.9 8.8 %shard_map.147 = (bf16[16,44,512]{2,1,0:T(8,128)(2,1)}, bf16[352,1536]{1,0:T(8,128)(2,1)}, bf16[352,512]{1,0:T(8,128)(2,1)}) custom-call(bf16[32,22,512]{2,1,0:T(8,128)(2,1)S(1)} %all-to-all-done.2.pack, bf16[352,512]{1,0:T(8,128)(2,1)} %get-tuple-element.50.tokens_far, bf16[352,1536]{1,0:T(8,128)(2,1)} %get-tuple-element.51.packed_far, ...), custom_call_target="tpu_custom_call" | custom-call | flops 60000002048 | bytes 65536 | tf_op jit(solution)/shard_map/pallas_call | solution.py:485
  99.6 4.7 %all-to-all-start.3 = ((bf16[16,44,512]{2,1,0:T(8,128)(2,1)}), bf16[16,44,512]{2,1,0:T(8,128)(2,1)S(1)}, u32[]{:S(2)}, u32[]{:S(2)}) async-start(bf16[16,44,512]{2,1,0:T(8,128)(2,1)} %get-tuple-element.61), calls=%async_computation.3 | async-start | bytes 1572864 | tf_op jit(solution)/shard_map/all_to_all | solution.py:505
  104.3 3.5 %shard_map.148 = (bf16[64,16,512]{2,1,0:T(8,128)(2,1)S(1)}, bf16[32,16,512]{2,1,0:T(8,128)(2,1)S(1)}, bf16[32,16,512]{2,1,0:T(8,128)(2,1)S(1)}) custom-call(s32[3]{0:T(128)S(1)} %pad_add_fusion.place, bf16[352,1536]{1,0:T(8,128)(2,1)} %get-tuple-element.62.refs_0_, bf16[352,512]{1,0:T(8,128)(2,1)} %get-tuple-element.63.refs_1_, ...), custom_call_target="tpu_custom_call" | custom-call | flops 100000000 | bytes 65536 | tf_op jit(solution)/shard_map/pallas_call | solution.py:485
  107.9 0.5 collective-permute-start
  108.4 0.1 collective-permute-start.1
  108.5 1.4 collective-permute-done.first
  109.9 0.7 collective-permute-done.1.second
  110.7 1.2 shard_map.149
  111.9 6.1 %all-to-all-done.3 = bf16[16,44,512]{2,1,0:T(8,128)(2,1)S(1)} async-done(((bf16[16,44,512]{2,1,0:T(8,128)(2,1)}), bf16[16,44,512]{2,1,0:T(8,128)(2,1)S(1)}, u32[]{:S(2)}, u32[]{:S(2)}) %all-to-all-start.3) | async-done | bytes 720928 | tf_op jit(solution)/shard_map/all_to_all | solution.py:505
  118.0 8.5 %all-to-all-start.4 = ((bf16[64,16,512]{2,1,0:T(8,128)(2,1)}), bf16[64,16,512]{2,1,0:T(8,128)(2,1)S(1)}, u32[]{:S(2)}, u32[]{:S(2)}) async-start(bf16[64,16,512]{2,1,0:T(8,128)(2,1)} %shard_map.149), calls=%async_computation.4 | async-start | bytes 2097152 | tf_op jit(solution)/shard_map/all_to_all | solution.py:505
  126.5 4.2 %reduce-scatter.2.cloned.1.call-done = bf16[768,512]{1,0:T(8,128)(2,1)} async-done(((bf16[3072,512]{1,0:T(8,128)(2,1)}), bf16[768,512]{1,0:T(8,128)(2,1)}) %reduce-scatter.2.cloned.1.call-update) | async-done | bytes 786448 | tf_op jit(solution)/shard_map/reduce_scatter | solution.py:595
  130.6 1.8 %shard_map.152 = (bf16[192,512]{1,0:T(8,128)(2,1)S(1)}, bf16[192,512]{1,0:T(8,128)(2,1)S(1)}, bf16[192,512]{1,0:T(8,128)(2,1)S(1)}, bf16[192,512]{1,0:T(8,128)(2,1)S(1)}) custom-call(s32[3]{0:T(128)S(1)} %pad_add_fusion.place, bf16[4,192,512]{2,1,0:T(8,128)(2,1)} %bitcast.17), custom_call_target="tpu_custom_call" | custom-call | flops 10000000 | bytes 65536 | tf_op jit(solution)/shard_map/pallas_call | solution.py:485
  132.4 3.1 %collective-permute-start.7 = (bf16[192,512]{1,0:T(8,128)(2,1)S(1)}, bf16[192,512]{1,0:T(8,128)(2,1)S(1)}, u32[]{:S(2)}, u32[]{:S(2)}) collective-permute-start(bf16[192,512]{1,0:T(8,128)(2,1)S(1)} %get-tuple-element.77), channel_id=1, source_target_pairs={{0,8},{4,12},{8,0},{12,4},{1,9},{5,13},{9,1},{13,5},{2,10},{6,14},... | collective-permute-start | bytes 589832 | tf_op jit(solution)/shard_map/ppermute | solution.py:510
  135.5 1.1 collective-permute-start.8
  136.7 0.0 collective-permute-start.9
  136.7 0.2 fusion
  136.9 1.3 copy.20
  138.2 1.3 copy.19
  139.5 6.1 %collective-permute-done.7.refs_1_ = bf16[192,512]{1,0:T(8,128)(2,1)S(1)} collective-permute-done((bf16[192,512]{1,0:T(8,128)(2,1)S(1)}, bf16[192,512]{1,0:T(8,128)(2,1)S(1)}, u32[]{:S(2)}, u32[]{:S(2)}) %collective-permute-start.7) | collective-permute-done | bytes 196640 | tf_op jit(solution)/shard_map/ppermute | solution.py:510
  145.7 3.7 %collective-permute-done.8.refs_2_ = bf16[192,512]{1,0:T(8,128)(2,1)S(1)} collective-permute-done((bf16[192,512]{1,0:T(8,128)(2,1)S(1)}, bf16[192,512]{1,0:T(8,128)(2,1)S(1)}, u32[]{:S(2)}, u32[]{:S(2)}) %collective-permute-start.8) | collective-permute-done | bytes 196640 | tf_op jit(solution)/shard_map/ppermute | solution.py:510
  149.4 0.7 shard_map.153
  150.1 3.9 %collective-permute-start.10 = (bf16[48,512]{1,0:T(8,128)(2,1)S(1)}, bf16[48,512]{1,0:T(8,128)(2,1)S(1)}, u32[]{:S(2)}, u32[]{:S(2)}) collective-permute-start(bf16[48,512]{1,0:T(8,128)(2,1)S(1)} %get-tuple-element.81), channel_id=1, source_target_pairs={{0,16},{2,18},{16,0},{18,2},{1,17},{3,19},{17,1},{19,3},{4,20},{6,... | collective-permute-start | bytes 147464 | tf_op jit(solution)/shard_map/ppermute | solution.py:510
  154.0 0.2 collective-permute-start.11
  154.2 0.3 collective-permute-start.12
  154.4 0.8 shard_map.150
  155.2 0.8 collective-permute-done.10.refs_1_
  156.1 3.2 %collective-permute-done.11.refs_2_ = bf16[48,512]{1,0:T(8,128)(2,1)S(1)} collective-permute-done((bf16[48,512]{1,0:T(8,128)(2,1)S(1)}, bf16[48,512]{1,0:T(8,128)(2,1)S(1)}, u32[]{:S(2)}, u32[]{:S(2)}) %collective-permute-start.11) | collective-permute-done | bytes 49184 | tf_op jit(solution)/shard_map/ppermute | solution.py:510
  159.3 0.6 shard_map.154
  (8 shorter events, 0.0 us)
Async XLA Ops:
  34.6 24.4 %all-to-all-start.1 = ((bf16[32,22,512]{2,1,0:T(8,128)(2,1)}), bf16[32,22,512]{2,1,0:T(8,128)(2,1)S(1)}, u32[]{:S(2)}, u32[]{:S(2)}) async-start(bf16[32,22,512]{2,1,0:T(8,128)(2,1)} %get-tuple-element.48), calls=%async_computation.1 | async-start | bytes 1572864 | tf_op jit(solution)/shard_map/all_to_all | solution.py:505
  71.9 18.9 %all-to-all-start.2 = ((bf16[32,22,512]{2,1,0:T(8,128)(2,1)}), bf16[32,22,512]{2,1,0:T(8,128)(2,1)S(1)}, u32[]{:S(2)}, u32[]{:S(2)}) async-start(bf16[32,22,512]{2,1,0:T(8,128)(2,1)} %get-tuple-element.49), calls=%async_computation.2 | async-start | bytes 1572864 | tf_op jit(solution)/shard_map/all_to_all | solution.py:505
  76.3 54.3 %reduce-scatter.2.cloned.1.call-start = ((), (), s32[]{:S(2)}) async-start(), calls=%async_computation.6 | async-start | bytes 3932160 | tf_op jit(solution)/shard_map/reduce_scatter | solution.py:595
  83.2 5.6 %collective-permute-start.2 = (bf16[13,48,512]{2,1,0:T(8,128)(2,1)S(1)}, bf16[13,48,512]{2,1,0:T(8,128)(2,1)S(1)}, u32[]{:S(2)}, u32[]{:S(2)}) collective-permute-start(bf16[13,48,512]{2,1,0:T(8,128)(2,1)S(1)} %get-tuple-element.71), channel_id=1, source_target_pairs={{0,1},{1,0},{2,3},{3,2},{4,5},{5,4},{6,7},{7,6},{8,9},{9,8},{10,11... | collective-permute-start | bytes 1916936 | tf_op jit(solution)/shard_map/ppermute | solution.py:517
  83.3 5.5 %collective-permute-start.3 = (bf16[13,48,512]{2,1,0:T(8,128)(2,1)S(1)}, bf16[13,48,512]{2,1,0:T(8,128)(2,1)S(1)}, u32[]{:S(2)}, u32[]{:S(2)}) collective-permute-start(bf16[13,48,512]{2,1,0:T(8,128)(2,1)S(1)} %get-tuple-element.72), channel_id=1, source_target_pairs={{0,1},{1,0},{2,3},{3,2},{4,5},{5,4},{6,7},{7,6},{8,9},{9,8},{10,11... | collective-permute-start | bytes 1916936 | tf_op jit(solution)/shard_map/ppermute | solution.py:517
  83.7 5.0 %collective-permute-start.4 = (bf16[13,48,512]{2,1,0:T(8,128)(2,1)S(1)}, bf16[13,48,512]{2,1,0:T(8,128)(2,1)S(1)}, u32[]{:S(2)}, u32[]{:S(2)}) collective-permute-start(bf16[13,48,512]{2,1,0:T(8,128)(2,1)S(1)} %get-tuple-element.73), channel_id=1, source_target_pairs={{0,1},{1,0},{2,3},{3,2},{4,5},{5,4},{6,7},{7,6},{8,9},{9,8},{10,11... | collective-permute-start | bytes 1916936 | tf_op jit(solution)/shard_map/ppermute | solution.py:517
  83.8 4.9 %collective-permute-start.5 = (bf16[13,48,512]{2,1,0:T(8,128)(2,1)S(1)}, bf16[13,48,512]{2,1,0:T(8,128)(2,1)S(1)}, u32[]{:S(2)}, u32[]{:S(2)}) collective-permute-start(bf16[13,48,512]{2,1,0:T(8,128)(2,1)S(1)} %get-tuple-element.74), channel_id=1, source_target_pairs={{0,1},{1,0},{2,3},{3,2},{4,5},{5,4},{6,7},{7,6},{8,9},{9,8},{10,11... | collective-permute-start | bytes 1916936 | tf_op jit(solution)/shard_map/ppermute | solution.py:517
  84.3 4.7 %collective-permute-start.6 = (bf16[13,48,512]{2,1,0:T(8,128)(2,1)S(1)}, bf16[13,48,512]{2,1,0:T(8,128)(2,1)S(1)}, u32[]{:S(2)}, u32[]{:S(2)}) collective-permute-start(bf16[13,48,512]{2,1,0:T(8,128)(2,1)S(1)} %get-tuple-element.75), channel_id=1, source_target_pairs={{0,1},{1,0},{2,3},{3,2},{4,5},{5,4},{6,7},{7,6},{8,9},{9,8},{10,11... | collective-permute-start | bytes 1916936 | tf_op jit(solution)/shard_map/ppermute | solution.py:517
  99.6 18.4 %all-to-all-start.3 = ((bf16[16,44,512]{2,1,0:T(8,128)(2,1)}), bf16[16,44,512]{2,1,0:T(8,128)(2,1)S(1)}, u32[]{:S(2)}, u32[]{:S(2)}) async-start(bf16[16,44,512]{2,1,0:T(8,128)(2,1)} %get-tuple-element.61), calls=%async_computation.3 | async-start | bytes 1572864 | tf_op jit(solution)/shard_map/all_to_all | solution.py:505
  107.9 2.0 %collective-permute-start = (bf16[32,16,512]{2,1,0:T(8,128)(2,1)S(1)}, bf16[32,16,512]{2,1,0:T(8,128)(2,1)S(1)}, u32[]{:S(2)}, u32[]{:S(2)}) collective-permute-start(bf16[32,16,512]{2,1,0:T(8,128)(2,1)S(1)} %get-tuple-element.67), channel_id=1, source_target_pairs={{0,1},{1,0},{2,3},{3,2},{4,5},{5,4},{6,7},{7,6},{8,9},{9,8},{10,11... | collective-permute-start | bytes 1572872 | tf_op jit(solution)/shard_map/ppermute | solution.py:517
  108.4 2.3 %collective-permute-start.1 = (bf16[32,16,512]{2,1,0:T(8,128)(2,1)S(1)}, bf16[32,16,512]{2,1,0:T(8,128)(2,1)S(1)}, u32[]{:S(2)}, u32[]{:S(2)}) collective-permute-start(bf16[32,16,512]{2,1,0:T(8,128)(2,1)S(1)} %get-tuple-element.68), channel_id=1, source_target_pairs={{0,1},{1,0},{2,3},{3,2},{4,5},{5,4},{6,7},{7,6},{8,9},{9,8},{10,11... | collective-permute-start | bytes 1572872 | tf_op jit(solution)/shard_map/ppermute | solution.py:517
  118.0 36.4 %all-to-all-start.4 = ((bf16[64,16,512]{2,1,0:T(8,128)(2,1)}), bf16[64,16,512]{2,1,0:T(8,128)(2,1)S(1)}, u32[]{:S(2)}, u32[]{:S(2)}) async-start(bf16[64,16,512]{2,1,0:T(8,128)(2,1)} %shard_map.149), calls=%async_computation.4 | async-start | bytes 2097152 | tf_op jit(solution)/shard_map/all_to_all | solution.py:505
  132.4 13.2 %collective-permute-start.7 = (bf16[192,512]{1,0:T(8,128)(2,1)S(1)}, bf16[192,512]{1,0:T(8,128)(2,1)S(1)}, u32[]{:S(2)}, u32[]{:S(2)}) collective-permute-start(bf16[192,512]{1,0:T(8,128)(2,1)S(1)} %get-tuple-element.77), channel_id=1, source_target_pairs={{0,8},{4,12},{8,0},{12,4},{1,9},{5,13},{9,1},{13,5},{2,10},{6,14},... | collective-permute-start | bytes 589832 | tf_op jit(solution)/shard_map/ppermute | solution.py:510
  135.5 13.9 %collective-permute-start.8 = (bf16[192,512]{1,0:T(8,128)(2,1)S(1)}, bf16[192,512]{1,0:T(8,128)(2,1)S(1)}, u32[]{:S(2)}, u32[]{:S(2)}) collective-permute-start(bf16[192,512]{1,0:T(8,128)(2,1)S(1)} %get-tuple-element.78), channel_id=1, source_target_pairs={{0,12},{4,8},{8,4},{12,0},{1,13},{5,9},{9,5},{13,1},{2,14},{6,10},... | collective-permute-start | bytes 589832 | tf_op jit(solution)/shard_map/ppermute | solution.py:510
  136.7 12.7 %collective-permute-start.9 = (bf16[192,512]{1,0:T(8,128)(2,1)S(1)}, bf16[192,512]{1,0:T(8,128)(2,1)S(1)}, u32[]{:S(2)}, u32[]{:S(2)}) collective-permute-start(bf16[192,512]{1,0:T(8,128)(2,1)S(1)} %get-tuple-element.79), channel_id=1, source_target_pairs={{0,4},{4,0},{8,12},{12,8},{1,5},{5,1},{9,13},{13,9},{2,6},{6,2},{1... | collective-permute-start | bytes 589832 | tf_op jit(solution)/shard_map/ppermute | solution.py:510
  150.1 6.0 %collective-permute-start.10 = (bf16[48,512]{1,0:T(8,128)(2,1)S(1)}, bf16[48,512]{1,0:T(8,128)(2,1)S(1)}, u32[]{:S(2)}, u32[]{:S(2)}) collective-permute-start(bf16[48,512]{1,0:T(8,128)(2,1)S(1)} %get-tuple-element.81), channel_id=1, source_target_pairs={{0,16},{2,18},{16,0},{18,2},{1,17},{3,19},{17,1},{19,3},{4,20},{6,... | collective-permute-start | bytes 147464 | tf_op jit(solution)/shard_map/ppermute | solution.py:510
  154.0 5.3 %collective-permute-start.11 = (bf16[48,512]{1,0:T(8,128)(2,1)S(1)}, bf16[48,512]{1,0:T(8,128)(2,1)S(1)}, u32[]{:S(2)}, u32[]{:S(2)}) collective-permute-start(bf16[48,512]{1,0:T(8,128)(2,1)S(1)} %get-tuple-element.82), channel_id=1, source_target_pairs={{0,18},{2,16},{16,2},{18,0},{1,19},{3,17},{17,3},{19,1},{4,22},{6,... | collective-permute-start | bytes 147464 | tf_op jit(solution)/shard_map/ppermute | solution.py:510
  154.2 5.1 %collective-permute-start.12 = (bf16[48,512]{1,0:T(8,128)(2,1)S(1)}, bf16[48,512]{1,0:T(8,128)(2,1)S(1)}, u32[]{:S(2)}, u32[]{:S(2)}) collective-permute-start(bf16[48,512]{1,0:T(8,128)(2,1)S(1)} %get-tuple-element.83), channel_id=1, source_target_pairs={{0,2},{2,0},{16,18},{18,16},{1,3},{3,1},{17,19},{19,17},{4,6},{6,4... | collective-permute-start | bytes 147464 | tf_op jit(solution)/shard_map/ppermute | solution.py:510
Sparse Core Ops, SparseCore 0:
  91.0 39.6 reduce-scatter.1

commit v6 on v5

--- a/solution.py
+++ b/solution.py
@@ -223,7 +223,7 @@
         rows = pl.ds(block * NEAR, NEAR)
         hidden[rows, :] = piece[:NEAR]
         cotangent[rows, :] = piece[NEAR:]
-    values = hidden[...]
+    values = hidden[:ROWS]
     tokens[...] = values.astype(bf16)
     normed[...] = normalize(values)[0].astype(bf16)
     leaving = [mover.start(tokens, tokens_far), mover.start(normed, normed_far)]
@@ -234,7 +234,7 @@
     mixed[...] = turned[...].T.astype(bf16)
     leaving.append(mover.start(mixed, mixed_far))
     outproj_in.wait()
-    hidden[...] += dot(mixed[...], outproj[...])
+    hidden[:ROWS] += dot(mixed[...], outproj[...])
     for block in range(LATS):
         rows = pl.ds(block * PART, PART)
         out[block] = jnp.concatenate([hidden[rows, :], cotangent[rows, :]], axis=0).astype(bf16)
@@ -257,7 +257,7 @@
         rows = pl.ds(block * PART, PART)
         hidden[rows, :] = piece[:PART]
         output[rows, :] = piece[PART:]
-    low[...] = hidden[...].astype(bf16)
+    low[...] = hidden[:ROWS].astype(bf16)
     leaving = [mover.start(low, low_far)]
     outproj_in.wait()
     upstream[...] = dot(low[...], outproj[...], 1, 1).astype(bf16)
@@ -268,7 +268,7 @@
     inproj_in.wait()
     grad_normed = dot(grads[...], inproj[...], 1, 1)
     tokens_in.wait()
-    hidden[...] += norm_back(*normalize(tokens[...].astype(f32)), grad_normed)
+    hidden[:ROWS] += norm_back(*normalize(tokens[...].astype(f32)), grad_normed)
     for block in range(16):
         rows = pl.ds(block * NEAR, NEAR)
         out[block] = jnp.concatenate([hidden[rows, :], output[rows, :]], axis=0).astype(bf16)
@@ -520,7 +520,8 @@
 NARROW = (ROWS, WIDTH)
 QKV = (ROWS, 3 * WIDTH)
 WIDE = (ROWS, FF)
-TILES = (4, 2 * ROWS, 128)
+TILES = (4, 24 * LATS, 128)
+ROOMY = (ROWS + 8, WIDTH)
 TURNED = (WIDTH, ROWS)
 TO_TURN = (LATS, 2 * PART, WIDTH)
 TO_LON = (16, 2 * NEAR, WIDTH)
@@ -550,7 +551,7 @@
         row_forward,
         [(swap(pack, LON), VMEM)] + all_far(inproj_lon, outproj_lon),
         [(TO_TURN, bf16, VMEM)] + far(NARROW, NARROW, QKV, NARROW),
-        low(IN, OUT, NARROW, NARROW, QKV, NARROW) + [(NARROW, f32), (NARROW, f32), (TURNED, f32)],
+        low(IN, OUT, NARROW, NARROW, QKV, NARROW) + [(ROOMY, f32), (ROOMY, f32), (TURNED, f32)],
         6,
         20,
         5.0,
@@ -599,7 +600,7 @@
         + all_far(row_tokens, row_packed, weights, inproj_lon, outproj_lon),
         [(TO_LON, bf16, pl.ANY)] + far(QKV, NARROW),
         low(NARROW, QKV, LON_WEIGHTS, IN, OUT, QKV, NARROW)
-        + [(NARROW, f32), (NARROW, f32), (NARROW, bf16)],
+        + [(ROOMY, f32), (ROOMY, f32), (NARROW, bf16)],
         7,
         28,
         60.0,

time: 167 us -> 167 us (level)
  no operation moved by 1% of the time
where the time goes in v6:
time: 167 us
  Pallas kernels  49.7 us (30%)
  waiting for transfers between devices  42.4 us (25%)
  starting transfers between devices  36.7 us (22%)
  blocking collectives  19.1 us (11%)
  between operations  14.2 us (9%)
  local copies, waits for them, and re-layouts  3.01 us (2%)
    pallas_call x12, Pallas kernels, call(): pl.pallas_call(kernel, out_shape=[jax.ShapeDtypeStruct(shape, kind) if pl...  49.7 us
    all_to_all x4, starting transfers between devices, swap(): return lax.all_to_all(array, axes, split_axis=0, concat_axis=0, tiled=True)  26.1 us
    all_to_all x4, waiting for transfers between devices, swap(): return lax.all_to_all(array, axes, split_axis=0, concat_axis=0, tiled=True)  21.9 us
    all_to_all x1, blocking collectives, swap(): return lax.all_to_all(array, axes, split_axis=0, concat_axis=0, tiled=True)  19.1 us
    ppermute x6, waiting for transfers between devices, trade(): lax.ppermute(parts[step], axes, [(place, place ^ step) for place in range...  13.9 us
    ppermute x6, starting transfers between devices, trade(): lax.ppermute(parts[step], axes, [(place, place ^ step) for place in range...  8.55 us
    reduce_scatter x1, waiting for transfers between devices, per_device(): lax.psum_scatter(column.reshape(3072, WIDTH), 'x', scatter_dimension=0, t...  4.15 us
  transfers between devices with their start and end apart: 18, of which 10 were waited for; matrix products, arithmetic and copies ran while one was open for 2% of the time, Pallas kernels for 18%

profile of v6, /device:TPU:0, one launch (start us, length us, event | category | flops | bytes accessed | tf_op | source)
XLA Modules:
  0.0 166.8 jit_solution(11460730359347903893)
XLA Ops:
  7.2 1.6 pad_maximum_fusion
  8.7 0.2 copy.16
  8.9 19.1 %all_to_all.25.pack = bf16[16,44,512]{2,1,0:T(8,128)(2,1)S(1)} all-to-all(bf16[16,44,512]{2,1,0:T(8,128)(2,1)S(1)} %bitcast.16), channel_id=1, replica_groups=mesh['x'=4,'h'=2,'y'=4,'l'=2,'c'=2] {'y','l','c'}, dimensions={0} | all-to-all | bytes 1441792 | tf_op jit(solution)/shard_map/all_to_all | solution.py:505
  28.0 6.5 %shard_map.143 = (bf16[32,22,512]{2,1,0:T(8,128)(2,1)}, bf16[352,512]{1,0:T(8,128)(2,1)}, bf16[352,512]{1,0:T(8,128)(2,1)}, bf16[352,1536]{1,0:T(8,128)(2,1)}, bf16[352,512]{1,0:T(8,128)(2,1)}) custom-call(bf16[16,44,512]{2,1,0:T(8,128)(2,1)S(1)} %all_to_all.25.pack, bf16[512,1536]{1,0:T(8,128)(2,1)} %inproj_far.5, bf16[512,512]{1,0:T(8,128)(2,1)} %outproj_far.5), custom_call_target="tpu_custom_call" | custom-call | flops 5000000000 | bytes 65536 | tf_op jit(solution)/shard_map/pallas_call | solution.py:485
  34.6 8.6 %all-to-all-start.1 = ((bf16[32,22,512]{2,1,0:T(8,128)(2,1)}), bf16[32,22,512]{2,1,0:T(8,128)(2,1)S(1)}, u32[]{:S(2)}, u32[]{:S(2)}) async-start(bf16[32,22,512]{2,1,0:T(8,128)(2,1)} %get-tuple-element.48), calls=%async_computation.1 | async-start | bytes 1572864 | tf_op jit(solution)/shard_map/all_to_all | solution.py:505
  43.2 15.7 %all-to-all-done.1.pack = bf16[32,22,512]{2,1,0:T(8,128)(2,1)S(1)} async-done(((bf16[32,22,512]{2,1,0:T(8,128)(2,1)}), bf16[32,22,512]{2,1,0:T(8,128)(2,1)S(1)}, u32[]{:S(2)}, u32[]{:S(2)}) %all-to-all-start.1) | async-done | bytes 720928 | tf_op jit(solution)/shard_map/all_to_all | solution.py:505
  58.9 13.0 %shard_map.144 = (bf16[32,22,512]{2,1,0:T(8,128)(2,1)}, bf16[352,512]{1,0:T(8,128)(2,1)}, bf16[352,512]{1,0:T(8,128)(2,1)}, bf16[352,1536]{1,0:T(8,128)(2,1)}, b...) custom-call(bf16[32,22,512]{2,1,0:T(8,128)(2,1)S(1)} %all-to-all-don, ...), custom_call_target="tpu_custom_call" | custom-call | flops 20000000000 | bytes 65536 | tf_op jit(solution)/shard_map/pallas_call | solution.py:485
  71.9 4.4 %all-to-all-start.2 = ((bf16[32,22,512]{2,1,0:T(8,128)(2,1)}), bf16[32,22,512]{2,1,0:T(8,128)(2,1)S(1)}, u32[]{:S(2)}, u32[]{:S(2)}) async-start(bf16[32,22,512]{2,1,0:T(8,128)(2,1)} %get-tuple-element.49), calls=%async_computation.2 | async-start | bytes 1572864 | tf_op jit(solution)/shard_map/all_to_all | solution.py:505
  76.3 0.3 reduce-scatter.2.cloned.1.call-start
  76.6 0.1 pad_add_fusion.place
  76.7 6.5 %shard_map.145 = (bf16[4,4,2,2,48,512]{5,4,3,2,1,0:T(8,128)(2,1)S(1)}, bf16[13,48,512]{2,1,0:T(8,128)(2,1)S(1)}, bf16[13,48,512]{2,1,0:T(8,128)(2,1)S(1)}, bf16[...) custom-call(s32[3]{0:T(128)S(1)} %pad_add_fusion.place, ...), custom_call_target="tpu_custom_call" | custom-call | flops 100000000 | bytes 65536 | tf_op jit(solution)/shard_map/pallas_call | solution.py:485
  83.2 0.1 collective-permute-start.2
  83.3 0.5 collective-permute-start.3
  83.7 0.1 collective-permute-start.4
  83.8 0.4 collective-permute-start.5
  84.3 0.1 collective-permute-start.6
  84.4 4.4 %shard_map.146.weights_far = bf16[8,352,352]{2,1,0:T(8,128)(2,1)} custom-call(bf16[352,1536]{1,0:T(8,128)(2,1)} %get-tuple-element.51.packed_far, bf16[4,4,2,2,48,512]{5,4,3,2,1,0:T(8,128)(2,1)S(1)} %get-tuple-element.60.after.mine), custom_call_target="tpu_custom_call" | custom-call | flops 100000000 | bytes 65536 | tf_op jit(solution)/shard_map/pallas_call | solution.py:485
  88.8 0.2 collective-permute-done.6.refs_4_
  89.0 1.9 %shard_map.151 = bf16[4,4,2,2,48,512]{5,4,3,2,1,0:T(8,128)(2,1)} custom-call(bf16[4,4,2,2,48,512]{5,4,3,2,1,0:T(8,128)(2,1)S(1)} %get-tuple-element.60.after.mine, bf16[13,48,512]{2,1,0:T(8,128)(2,1)S(1)} %collective-permute-done.2.refs_0_, bf16[13,48,512]{2,1,0:T(8,128)(2,1)S(1)} %collective-permute-done.3.refs_1_, ...), custom_call_target="tpu_custom_call" | custom-call | flops 100000000 | bytes 65536 | tf_op jit(solution)/shard_map/pallas_call | solution.py:485
  90.8 0.0 reduce-scatter.2.cloned.1.call-update
  90.9 8.8 %shard_map.147 = (bf16[16,44,512]{2,1,0:T(8,128)(2,1)}, bf16[352,1536]{1,0:T(8,128)(2,1)}, bf16[352,512]{1,0:T(8,128)(2,1)}) custom-call(bf16[32,22,512]{2,1,0:T(8,128)(2,1)S(1)} %all-to-all-done.2.pack, bf16[352,512]{1,0:T(8,128)(2,1)} %get-tuple-element.50.tokens_far, bf16[352,1536]{1,0:T(8,128)(2,1)} %get-tuple-element.51.packed_far, ...), custom_call_target="tpu_custom_call" | custom-call | flops 60000002048 | bytes 65536 | tf_op jit(solution)/shard_map/pallas_call | solution.py:485
  99.6 4.7 %all-to-all-start.3 = ((bf16[16,44,512]{2,1,0:T(8,128)(2,1)}), bf16[16,44,512]{2,1,0:T(8,128)(2,1)S(1)}, u32[]{:S(2)}, u32[]{:S(2)}) async-start(bf16[16,44,512]{2,1,0:T(8,128)(2,1)} %get-tuple-element.61), calls=%async_computation.3 | async-start | bytes 1572864 | tf_op jit(solution)/shard_map/all_to_all | solution.py:505
  104.3 3.5 %shard_map.148 = (bf16[64,16,512]{2,1,0:T(8,128)(2,1)S(1)}, bf16[32,16,512]{2,1,0:T(8,128)(2,1)S(1)}, bf16[32,16,512]{2,1,0:T(8,128)(2,1)S(1)}) custom-call(s32[3]{0:T(128)S(1)} %pad_add_fusion.place, bf16[352,1536]{1,0:T(8,128)(2,1)} %get-tuple-element.62.refs_0_, bf16[352,512]{1,0:T(8,128)(2,1)} %get-tuple-element.63.refs_1_, ...), custom_call_target="tpu_custom_call" | custom-call | flops 100000000 | bytes 65536 | tf_op jit(solution)/shard_map/pallas_call | solution.py:485
  107.9 0.5 collective-permute-start
  108.4 0.1 collective-permute-start.1
  108.5 1.4 collective-permute-done.first
  109.9 0.7 collective-permute-done.1.second
  110.7 1.2 shard_map.149
  111.9 6.1 %all-to-all-done.3 = bf16[16,44,512]{2,1,0:T(8,128)(2,1)S(1)} async-done(((bf16[16,44,512]{2,1,0:T(8,128)(2,1)}), bf16[16,44,512]{2,1,0:T(8,128)(2,1)S(1)}, u32[]{:S(2)}, u32[]{:S(2)}) %all-to-all-start.3) | async-done | bytes 720928 | tf_op jit(solution)/shard_map/all_to_all | solution.py:505
  118.0 8.5 %all-to-all-start.4 = ((bf16[64,16,512]{2,1,0:T(8,128)(2,1)}), bf16[64,16,512]{2,1,0:T(8,128)(2,1)S(1)}, u32[]{:S(2)}, u32[]{:S(2)}) async-start(bf16[64,16,512]{2,1,0:T(8,128)(2,1)} %shard_map.149), calls=%async_computation.4 | async-start | bytes 2097152 | tf_op jit(solution)/shard_map/all_to_all | solution.py:505
  126.5 4.2 %reduce-scatter.2.cloned.1.call-done = bf16[768,512]{1,0:T(8,128)(2,1)} async-done(((bf16[3072,512]{1,0:T(8,128)(2,1)}), bf16[768,512]{1,0:T(8,128)(2,1)}) %reduce-scatter.2.cloned.1.call-update) | async-done | bytes 786448 | tf_op jit(solution)/shard_map/reduce_scatter | solution.py:596
  130.6 1.8 %shard_map.152 = (bf16[192,512]{1,0:T(8,128)(2,1)S(1)}, bf16[192,512]{1,0:T(8,128)(2,1)S(1)}, bf16[192,512]{1,0:T(8,128)(2,1)S(1)}, bf16[192,512]{1,0:T(8,128)(2,1)S(1)}) custom-call(s32[3]{0:T(128)S(1)} %pad_add_fusion.place, bf16[4,192,512]{2,1,0:T(8,128)(2,1)} %bitcast.17), custom_call_target="tpu_custom_call" | custom-call | flops 10000000 | bytes 65536 | tf_op jit(solution)/shard_map/pallas_call | solution.py:485
  132.4 3.1 %collective-permute-start.7 = (bf16[192,512]{1,0:T(8,128)(2,1)S(1)}, bf16[192,512]{1,0:T(8,128)(2,1)S(1)}, u32[]{:S(2)}, u32[]{:S(2)}) collective-permute-start(bf16[192,512]{1,0:T(8,128)(2,1)S(1)} %get-tuple-element.77), channel_id=1, source_target_pairs={{0,8},{4,12},{8,0},{12,4},{1,9},{5,13},{9,1},{13,5},{2,10},{6,14},... | collective-permute-start | bytes 589832 | tf_op jit(solution)/shard_map/ppermute | solution.py:510
  135.5 1.1 collective-permute-start.8
  136.7 0.0 collective-permute-start.9
  136.7 0.2 fusion
  136.9 1.3 copy.20
  138.2 1.3 copy.19
  139.5 6.1 %collective-permute-done.7.refs_1_ = bf16[192,512]{1,0:T(8,128)(2,1)S(1)} collective-permute-done((bf16[192,512]{1,0:T(8,128)(2,1)S(1)}, bf16[192,512]{1,0:T(8,128)(2,1)S(1)}, u32[]{:S(2)}, u32[]{:S(2)}) %collective-permute-start.7) | collective-permute-done | bytes 196640 | tf_op jit(solution)/shard_map/ppermute | solution.py:510
  145.7 3.7 %collective-permute-done.8.refs_2_ = bf16[192,512]{1,0:T(8,128)(2,1)S(1)} collective-permute-done((bf16[192,512]{1,0:T(8,128)(2,1)S(1)}, bf16[192,512]{1,0:T(8,128)(2,1)S(1)}, u32[]{:S(2)}, u32[]{:S(2)}) %collective-permute-start.8) | collective-permute-done | bytes 196640 | tf_op jit(solution)/shard_map/ppermute | solution.py:510
  149.4 0.7 shard_map.153
  150.1 3.9 %collective-permute-start.10 = (bf16[48,512]{1,0:T(8,128)(2,1)S(1)}, bf16[48,512]{1,0:T(8,128)(2,1)S(1)}, u32[]{:S(2)}, u32[]{:S(2)}) collective-permute-start(bf16[48,512]{1,0:T(8,128)(2,1)S(1)} %get-tuple-element.81), channel_id=1, source_target_pairs={{0,16},{2,18},{16,0},{18,2},{1,17},{3,19},{17,1},{19,3},{4,20},{6,... | collective-permute-start | bytes 147464 | tf_op jit(solution)/shard_map/ppermute | solution.py:510
  154.0 0.2 collective-permute-start.11
  154.2 0.3 collective-permute-start.12
  154.4 0.8 shard_map.150
  155.2 0.9 collective-permute-done.10.refs_1_
  156.1 3.2 %collective-permute-done.11.refs_2_ = bf16[48,512]{1,0:T(8,128)(2,1)S(1)} collective-permute-done((bf16[48,512]{1,0:T(8,128)(2,1)S(1)}, bf16[48,512]{1,0:T(8,128)(2,1)S(1)}, u32[]{:S(2)}, u32[]{:S(2)}) %collective-permute-start.11) | collective-permute-done | bytes 49184 | tf_op jit(solution)/shard_map/ppermute | solution.py:510
  159.3 0.6 shard_map.154
  (8 shorter events, 0.0 us)
Async XLA Ops:
  34.6 24.4 %all-to-all-start.1 = ((bf16[32,22,512]{2,1,0:T(8,128)(2,1)}), bf16[32,22,512]{2,1,0:T(8,128)(2,1)S(1)}, u32[]{:S(2)}, u32[]{:S(2)}) async-start(bf16[32,22,512]{2,1,0:T(8,128)(2,1)} %get-tuple-element.48), calls=%async_computation.1 | async-start | bytes 1572864 | tf_op jit(solution)/shard_map/all_to_all | solution.py:505
  71.9 18.9 %all-to-all-start.2 = ((bf16[32,22,512]{2,1,0:T(8,128)(2,1)}), bf16[32,22,512]{2,1,0:T(8,128)(2,1)S(1)}, u32[]{:S(2)}, u32[]{:S(2)}) async-start(bf16[32,22,512]{2,1,0:T(8,128)(2,1)} %get-tuple-element.49), calls=%async_computation.2 | async-start | bytes 1572864 | tf_op jit(solution)/shard_map/all_to_all | solution.py:505
  76.3 54.3 %reduce-scatter.2.cloned.1.call-start = ((), (), s32[]{:S(2)}) async-start(), calls=%async_computation.6 | async-start | bytes 3932160 | tf_op jit(solution)/shard_map/reduce_scatter | solution.py:596
  83.2 5.6 %collective-permute-start.2 = (bf16[13,48,512]{2,1,0:T(8,128)(2,1)S(1)}, bf16[13,48,512]{2,1,0:T(8,128)(2,1)S(1)}, u32[]{:S(2)}, u32[]{:S(2)}) collective-permute-start(bf16[13,48,512]{2,1,0:T(8,128)(2,1)S(1)} %get-tuple-element.71), channel_id=1, source_target_pairs={{0,1},{1,0},{2,3},{3,2},{4,5},{5,4},{6,7},{7,6},{8,9},{9,8},{10,11... | collective-permute-start | bytes 1916936 | tf_op jit(solution)/shard_map/ppermute | solution.py:517
  83.3 5.5 %collective-permute-start.3 = (bf16[13,48,512]{2,1,0:T(8,128)(2,1)S(1)}, bf16[13,48,512]{2,1,0:T(8,128)(2,1)S(1)}, u32[]{:S(2)}, u32[]{:S(2)}) collective-permute-start(bf16[13,48,512]{2,1,0:T(8,128)(2,1)S(1)} %get-tuple-element.72), channel_id=1, source_target_pairs={{0,1},{1,0},{2,3},{3,2},{4,5},{5,4},{6,7},{7,6},{8,9},{9,8},{10,11... | collective-permute-start | bytes 1916936 | tf_op jit(solution)/shard_map/ppermute | solution.py:517
  83.7 5.0 %collective-permute-start.4 = (bf16[13,48,512]{2,1,0:T(8,128)(2,1)S(1)}, bf16[13,48,512]{2,1,0:T(8,128)(2,1)S(1)}, u32[]{:S(2)}, u32[]{:S(2)}) collective-permute-start(bf16[13,48,512]{2,1,0:T(8,128)(2,1)S(1)} %get-tuple-element.73), channel_id=1, source_target_pairs={{0,1},{1,0},{2,3},{3,2},{4,5},{5,4},{6,7},{7,6},{8,9},{9,8},{10,11... | collective-permute-start | bytes 1916936 | tf_op jit(solution)/shard_map/ppermute | solution.py:517
  83.8 4.9 %collective-permute-start.5 = (bf16[13,48,512]{2,1,0:T(8,128)(2,1)S(1)}, bf16[13,48,512]{2,1,0:T(8,128)(2,1)S(1)}, u32[]{:S(2)}, u32[]{:S(2)}) collective-permute-start(bf16[13,48,512]{2,1,0:T(8,128)(2,1)S(1)} %get-tuple-element.74), channel_id=1, source_target_pairs={{0,1},{1,0},{2,3},{3,2},{4,5},{5,4},{6,7},{7,6},{8,9},{9,8},{10,11... | collective-permute-start | bytes 1916936 | tf_op jit(solution)/shard_map/ppermute | solution.py:517
  84.3 4.7 %collective-permute-start.6 = (bf16[13,48,512]{2,1,0:T(8,128)(2,1)S(1)}, bf16[13,48,512]{2,1,0:T(8,128)(2,1)S(1)}, u32[]{:S(2)}, u32[]{:S(2)}) collective-permute-start(bf16[13,48,512]{2,1,0:T(8,128)(2,1)S(1)} %get-tuple-element.75), channel_id=1, source_target_pairs={{0,1},{1,0},{2,3},{3,2},{4,5},{5,4},{6,7},{7,6},{8,9},{9,8},{10,11... | collective-permute-start | bytes 1916936 | tf_op jit(solution)/shard_map/ppermute | solution.py:517
  99.6 18.4 %all-to-all-start.3 = ((bf16[16,44,512]{2,1,0:T(8,128)(2,1)}), bf16[16,44,512]{2,1,0:T(8,128)(2,1)S(1)}, u32[]{:S(2)}, u32[]{:S(2)}) async-start(bf16[16,44,512]{2,1,0:T(8,128)(2,1)} %get-tuple-element.61), calls=%async_computation.3 | async-start | bytes 1572864 | tf_op jit(solution)/shard_map/all_to_all | solution.py:505
  107.9 2.0 %collective-permute-start = (bf16[32,16,512]{2,1,0:T(8,128)(2,1)S(1)}, bf16[32,16,512]{2,1,0:T(8,128)(2,1)S(1)}, u32[]{:S(2)}, u32[]{:S(2)}) collective-permute-start(bf16[32,16,512]{2,1,0:T(8,128)(2,1)S(1)} %get-tuple-element.67), channel_id=1, source_target_pairs={{0,1},{1,0},{2,3},{3,2},{4,5},{5,4},{6,7},{7,6},{8,9},{9,8},{10,11... | collective-permute-start | bytes 1572872 | tf_op jit(solution)/shard_map/ppermute | solution.py:517
  108.4 2.3 %collective-permute-start.1 = (bf16[32,16,512]{2,1,0:T(8,128)(2,1)S(1)}, bf16[32,16,512]{2,1,0:T(8,128)(2,1)S(1)}, u32[]{:S(2)}, u32[]{:S(2)}) collective-permute-start(bf16[32,16,512]{2,1,0:T(8,128)(2,1)S(1)} %get-tuple-element.68), channel_id=1, source_target_pairs={{0,1},{1,0},{2,3},{3,2},{4,5},{5,4},{6,7},{7,6},{8,9},{9,8},{10,11... | collective-permute-start | bytes 1572872 | tf_op jit(solution)/shard_map/ppermute | solution.py:517
  118.0 36.4 %all-to-all-start.4 = ((bf16[64,16,512]{2,1,0:T(8,128)(2,1)}), bf16[64,16,512]{2,1,0:T(8,128)(2,1)S(1)}, u32[]{:S(2)}, u32[]{:S(2)}) async-start(bf16[64,16,512]{2,1,0:T(8,128)(2,1)} %shard_map.149), calls=%async_computation.4 | async-start | bytes 2097152 | tf_op jit(solution)/shard_map/all_to_all | solution.py:505
  132.4 13.2 %collective-permute-start.7 = (bf16[192,512]{1,0:T(8,128)(2,1)S(1)}, bf16[192,512]{1,0:T(8,128)(2,1)S(1)}, u32[]{:S(2)}, u32[]{:S(2)}) collective-permute-start(bf16[192,512]{1,0:T(8,128)(2,1)S(1)} %get-tuple-element.77), channel_id=1, source_target_pairs={{0,8},{4,12},{8,0},{12,4},{1,9},{5,13},{9,1},{13,5},{2,10},{6,14},... | collective-permute-start | bytes 589832 | tf_op jit(solution)/shard_map/ppermute | solution.py:510
  135.5 13.9 %collective-permute-start.8 = (bf16[192,512]{1,0:T(8,128)(2,1)S(1)}, bf16[192,512]{1,0:T(8,128)(2,1)S(1)}, u32[]{:S(2)}, u32[]{:S(2)}) collective-permute-start(bf16[192,512]{1,0:T(8,128)(2,1)S(1)} %get-tuple-element.78), channel_id=1, source_target_pairs={{0,12},{4,8},{8,4},{12,0},{1,13},{5,9},{9,5},{13,1},{2,14},{6,10},... | collective-permute-start | bytes 589832 | tf_op jit(solution)/shard_map/ppermute | solution.py:510
  136.7 12.7 %collective-permute-start.9 = (bf16[192,512]{1,0:T(8,128)(2,1)S(1)}, bf16[192,512]{1,0:T(8,128)(2,1)S(1)}, u32[]{:S(2)}, u32[]{:S(2)}) collective-permute-start(bf16[192,512]{1,0:T(8,128)(2,1)S(1)} %get-tuple-element.79), channel_id=1, source_target_pairs={{0,4},{4,0},{8,12},{12,8},{1,5},{5,1},{9,13},{13,9},{2,6},{6,2},{1... | collective-permute-start | bytes 589832 | tf_op jit(solution)/shard_map/ppermute | solution.py:510
  150.1 6.0 %collective-permute-start.10 = (bf16[48,512]{1,0:T(8,128)(2,1)S(1)}, bf16[48,512]{1,0:T(8,128)(2,1)S(1)}, u32[]{:S(2)}, u32[]{:S(2)}) collective-permute-start(bf16[48,512]{1,0:T(8,128)(2,1)S(1)} %get-tuple-element.81), channel_id=1, source_target_pairs={{0,16},{2,18},{16,0},{18,2},{1,17},{3,19},{17,1},{19,3},{4,20},{6,... | collective-permute-start | bytes 147464 | tf_op jit(solution)/shard_map/ppermute | solution.py:510
  154.0 5.3 %collective-permute-start.11 = (bf16[48,512]{1,0:T(8,128)(2,1)S(1)}, bf16[48,512]{1,0:T(8,128)(2,1)S(1)}, u32[]{:S(2)}, u32[]{:S(2)}) collective-permute-start(bf16[48,512]{1,0:T(8,128)(2,1)S(1)} %get-tuple-element.82), channel_id=1, source_target_pairs={{0,18},{2,16},{16,2},{18,0},{1,19},{3,17},{17,3},{19,1},{4,22},{6,... | collective-permute-start | bytes 147464 | tf_op jit(solution)/shard_map/ppermute | solution.py:510
  154.2 5.1 %collective-permute-start.12 = (bf16[48,512]{1,0:T(8,128)(2,1)S(1)}, bf16[48,512]{1,0:T(8,128)(2,1)S(1)}, u32[]{:S(2)}, u32[]{:S(2)}) collective-permute-start(bf16[48,512]{1,0:T(8,128)(2,1)S(1)} %get-tuple-element.83), channel_id=1, source_target_pairs={{0,2},{2,0},{16,18},{18,16},{1,3},{3,1},{17,19},{19,17},{4,6},{6,4... | collective-permute-start | bytes 147464 | tf_op jit(solution)/shard_map/ppermute | solution.py:510
Sparse Core Ops, SparseCore 0:
  91.0 39.6 reduce-scatter.1
